TPU v7x, 128 devices: a whole 4x4x4 slice. The times are simulated.
128 devices in a mesh: seq: 32 (over x, y_hi, z), head: 4 (over y_lo, core).
Axes of the slice: x: 4, y: 4 (y_hi: 2, y_lo: 2; y = y_hi * 2 + y_lo), z: 4, core: 2. Of those that a mesh axis runs over, the one named last changes fastest.
Arguments:
- latents: bfloat16 [64, 12288], P(None, 'seq'), may hold values from -6 to 6
- span_ids: int32 [64], replicated, may hold values from 0 to 15, never falling along the last dimension, each value on 1 to 6 neighbouring positions
- patch_weight: bfloat16 [128, 3072], P(None, 'head'), may hold values from -0.5 to 0.5
- patch_bias: float32 [3072], P('head'), may hold values from -3 to 3
- norm_gain: float32 [3072], replicated, may hold values from 0.1 to 1.9
- query_weight: bfloat16 [3072, 3072], P(None, 'head'), may hold values from -1 to 1, as said below
- key_weight: bfloat16 [3072, 3072], P(None, 'head'), may hold values from -1 to 1
- value_weight: bfloat16 [3072, 3072], P(None, 'head'), may hold values from -0.109375 to 0.109375
- out_weight: bfloat16 [3072, 3072], P('head'), may hold values from -0.109375 to 0.109375
Outputs:
- layer_out: bfloat16 [12288, 3072], P('seq', 'head')
Inputs may be any that keep to these rules, and one draw needn't show every extreme that they name: `query_weight`: entries of order 3072 ** -0.5.
All inputs are finite; a program needn't handle non-finite values.
Results may differ from a plain program's by a relative error of at most 0.012.
Values may be sent and summed in bfloat16 or wider, within the bound.
No kernel may reach another device: no remote copies, remote signals or barrier semaphores. Data moves between devices by JAX's collectives and lax.ppermute only.
A program may use at most 192 MiB of HBM per device.

v0:
```python
import math

import jax
import jax.numpy as jnp
from jax import lax
from jax.sharding import PartitionSpec as P

HD = 128
LAT_W = 48


yarn_factor = 4.0
eps = 1e-06


def from_behind(block, axis, distance):
    devices = range(lax.axis_size(axis))
    route = [(i - distance, i) for i in devices if i - distance in devices]
    return lax.ppermute(block, axis, route)


def spectrum(count):
    steps = jnp.arange(count).astype(jnp.float32)
    return jnp.exp(-math.log(10000.0) * steps / count)


def rotary_angles(frame, row, col, pairs, frames):
    count_t = pairs // 4
    count_h = 3 * pairs // 8
    count_w = pairs - count_t - count_h
    base_t = spectrum(count_t)
    wave = 2.0 * math.pi / base_t
    ramp = jnp.clip((frames / 4.0 / wave - 1.0) / 31.0, 0.0, 1.0)
    scaled_t = base_t * (ramp + (1.0 - ramp) / yarn_factor)
    return jnp.concatenate(
        [
            frame[:, None] * scaled_t[None, :],
            row[:, None] * spectrum(count_h)[None, :],
            col[:, None] * spectrum(count_w)[None, :],
        ],
        axis=1,
    )


def rotate(values, angles):
    pairs = angles.shape[1]
    cosine = jnp.cos(angles)[:, None, :]
    sine = jnp.sin(angles)[:, None, :]
    first = values[..., :pairs]
    second = values[..., pairs:]
    return jnp.concatenate(
        [first * cosine - second * sine, first * sine + second * cosine], axis=-1
    )


def score_scale(head_size):
    return (0.1 * math.log(yarn_factor) + 1.0) ** 2 / math.sqrt(head_size)


def largest_divisor(count, limit):
    found = 1
    for option in range(1, limit + 1):
        if count % option == 0:
            found = option
    return found


def local(
    latents,
    span_ids,
    patch_weight,
    patch_bias,
    norm_gain,
    query_weight,
    key_weight,
    value_weight,
    out_weight,
):
    seq_count = lax.axis_size("seq")
    frames = 2 * seq_count
    seq_index = lax.axis_index("seq")
    tok_dev = latents.shape[1]
    frame_tokens = tok_dev // 2
    early = latents[:, :frame_tokens]
    late = latents[:, frame_tokens:]
    early_prev = from_behind(early, "seq", 1)
    late_next = from_behind(late, "seq", -1)
    late_prev = jnp.where(seq_index == seq_count - 1, early, late_next)
    patches = jnp.concatenate(
        [jnp.concatenate([early_prev, early], axis=0), jnp.concatenate([late_prev, late], axis=0)],
        axis=1,
    )
    conv = lax.dot_general(
        patches, patch_weight, (((0,), (0,)), ((), ())), preferred_element_type=jnp.float32
    )
    tokens = (conv + patch_bias[None, :]).astype(jnp.bfloat16)
    share = tokens.shape[1]
    gathered = lax.all_gather(tokens, "head", axis=1, tiled=True)
    wide = gathered.astype(jnp.float32)
    mean_sq = jnp.mean(wide * wide, axis=1, keepdims=True)
    normed = (wide * lax.rsqrt(mean_sq + eps) * norm_gain[None, :]).astype(jnp.bfloat16)
    local_rows = jnp.arange(tok_dev)
    slot = local_rows // frame_tokens
    frame = jnp.where(slot == 0, seq_index, frames - 1 - seq_index)
    inner = local_rows % frame_tokens
    half_w = LAT_W // 2
    angles = rotary_angles(
        frame.astype(jnp.float32),
        (inner // half_w).astype(jnp.float32),
        (inner % half_w).astype(jnp.float32),
        HD // 2,
        frames,
    )
    heads_dev = share // HD
    query = rotate(
        jnp.dot(normed, query_weight, preferred_element_type=jnp.float32).reshape(
            tok_dev, heads_dev, HD
        ),
        angles,
    ).astype(jnp.bfloat16)
    keys = rotate(
        jnp.dot(normed, key_weight, preferred_element_type=jnp.float32).reshape(
            tok_dev, heads_dev, HD
        ),
        angles,
    ).astype(jnp.bfloat16)
    values = jnp.dot(normed, value_weight, preferred_element_type=jnp.float32).astype(jnp.bfloat16)
    keys = keys.reshape(tok_dev, share)
    frame_ids = jnp.arange(frames)

    def span_of(frame_index):
        return jnp.sum(
            jnp.where(frame_index[:, None] == frame_ids[None, :], span_ids[None, :], 0), axis=1
        )

    query_span = span_of(frame)
    scale = score_scale(HD)

    def attend(state, query_part, span_part, key_block, value_block, key_span):
        top, total, mixed = state
        count = key_block.shape[0]
        key_heads = key_block.reshape(count, heads_dev, HD)
        value_heads = value_block.reshape(count, heads_dev, HD)
        scores = (
            jnp.einsum("qhd,khd->hqk", query_part, key_heads, preferred_element_type=jnp.float32)
            * scale
        )
        allowed = (key_span[None, :] <= span_part[:, None])[None]
        scores = jnp.where(allowed, scores, -1e30)
        new_top = jnp.maximum(top, jnp.max(scores, axis=2))
        weights = jnp.where(allowed, jnp.exp(scores - new_top[:, :, None]), 0.0)
        fade = jnp.exp(top - new_top)
        total = total * fade + jnp.sum(weights, axis=2)
        update = jnp.einsum(
            "hqk,khd->qhd",
            weights.astype(jnp.bfloat16),
            value_heads,
            preferred_element_type=jnp.float32,
        )
        mixed = mixed * jnp.transpose(fade)[:, :, None] + update
        return (new_top, total, mixed)

    def visit_every(state, item):
        key_block, value_block, key_span = item
        return (attend(state, query, query_span, key_block, value_block, key_span), None)

    start_state = (
        jnp.full((heads_dev, tok_dev), -1e30, jnp.float32),
        jnp.zeros((heads_dev, tok_dev), jnp.float32),
        jnp.zeros((tok_dev, heads_dev, HD), jnp.float32),
    )
    key_rows = lax.all_gather(keys, "seq", axis=0, tiled=True)
    value_rows = lax.all_gather(values, "seq", axis=0, tiled=True)
    count = key_rows.shape[0]
    positions = jnp.arange(count)
    stored_block = positions // frame_tokens
    owner = stored_block // 2
    key_frame = jnp.where(stored_block % 2 == 0, owner, frames - 1 - owner)
    key_span = span_of(key_frame)
    block = largest_divisor(count, 768)
    steps = count // block
    items = (
        key_rows.reshape(steps, block, share),
        value_rows.reshape(steps, block, share),
        key_span.reshape(steps, block),
    )
    folded = lax.scan(visit_every, start_state, items)[0]
    total = folded[1]
    mixed = folded[2]
    heads_out = (
        (mixed / jnp.transpose(total)[:, :, None]).astype(jnp.bfloat16).reshape(tok_dev, share)
    )
    projected = jnp.dot(heads_out, out_weight, preferred_element_type=jnp.float32)
    summed = lax.psum_scatter(
        projected.astype(jnp.bfloat16), "head", scatter_dimension=1, tiled=True
    ).astype(jnp.float32)
    return (summed + tokens.astype(jnp.float32)).astype(jnp.bfloat16)


def solution(mesh):
    return jax.shard_map(
        local,
        mesh=mesh,
        in_specs=(
            P(None, "seq"),
            P(),
            P(None, "head"),
            P("head"),
            P(),
            P(None, "head"),
            P(None, "head"),
            P(None, "head"),
            P("head", None),
        ),
        out_specs=P("seq", "head"),
        check_vma=False,
    )
```

profile of v0, /device:TPU:1, one launch (start us, length us, event | category | flops | bytes accessed | tf_op | source)
XLA Modules:
  0.0 796.3 jit_solution(3756002855956774262)
XLA Ops:
  8.7 4.4 collective-permute-done.1
  13.8 3.5 collective-permute-start
  20.9 40.3 %all-gather.4.cloned.1.call-done = bf16[384,3072]{1,0:T(8,128)(2,1)} async-done(((bf16[384,768]{1,0:T(8,128)(2,1)}), bf16[384,3072]{1,0:T(8,128)(2,1)}) %all-gather.4.cloned.1.call-update) | async-done | bytes 2359312 | tf_op jit(solution)/shard_map/all_gather | solution.py:98
  63.7 5.6 fusion.53
  69.3 2.8 fusion.51
  73.4 5.2 convolution_convert_fusion.1
  80.9 170.6 %all-gather.6.cloned.1.call-done = bf16[12288,768]{0,1:T(8,128)(2,1)} async-done(((bf16[384,768]{0,1:T(8,128)(2,1)}), bf16[12288,768]{0,1:T(8,128)(2,1)}) %all-gather.6.cloned.1.call-update) | async-done | bytes 18874384 | tf_op jit(solution)/shard_map/all_gather | solution.py:172
  251.5 16.9 %copy.37 = bf16[96,16,8,768]{3,2,0,1:T(8,128)(2,1)} copy(bf16[96,16,8,768]{3,2,1,0:T(8,128)(2,1)} %bitcast.67) | data formatting | bytes 37748736 | tf_op jit(solution)/shard_map/reshape | solution.py:183
  268.3 152.1 %all-gather.8.cloned.1.call-done = bf16[12288,768]{1,0:T(8,128)(2,1)} async-done(((bf16[384,768]{1,0:T(8,128)(2,1)}), bf16[12288,768]{1,0:T(8,128)(2,1)}) %all-gather.8.cloned.1.call-update) | async-done | bytes 18874384 | tf_op jit(solution)/shard_map/all_gather | solution.py:173
  420.5 331.1 %while.15 = (s32[]{:T(128)}, f32[6,384]{1,0:T(8,128)S(1)}, f32[6,384]{1,0:T(8,128)S(1)}, f32[384,6,128]{0,2,1:T(8,128)}, s32[16,768]{1,0:T(8,128)S(1)}, /*index=...) while((s32[]{:T(128)}, f32[6,384]{1,0:T(8,128)S(1)}, ...), condition=%wide.region_6.7_spmd.clone, body=%wide.region_3.6_spmd.clone.sunk | while | flops 930166272 | bytes 56191668 | solution.py:187
  422.1 5.5 fusion.78
  430.0 2.5 copy.39
  432.6 6.6 fusion.82
  442.5 5.5 fusion.78
  450.5 2.5 copy.39
  453.0 6.9 fusion.82
  463.2 5.5 fusion.78
  471.2 2.5 copy.39
  473.7 6.9 fusion.82
  484.0 5.5 fusion.78
  491.9 2.5 copy.39
  494.4 6.9 fusion.82
  504.7 5.5 fusion.78
  515.1 6.9 fusion.82
  525.4 5.5 fusion.78
  535.8 6.9 fusion.82
  546.1 5.5 fusion.78
  556.5 6.9 fusion.82
  566.8 5.5 fusion.78
  577.3 6.9 fusion.82
  587.5 5.5 fusion.78
  598.0 6.9 fusion.82
  608.2 5.5 fusion.78
  618.7 6.9 fusion.82
  628.9 5.5 fusion.78
  639.4 6.9 fusion.82
  649.6 5.5 fusion.78
  660.1 6.9 fusion.82
  670.4 5.5 fusion.78
  680.8 6.9 fusion.82
  691.1 5.5 fusion.78
  701.5 6.9 fusion.82
  711.8 5.5 fusion.78
  722.2 6.9 fusion.82
  732.5 5.5 fusion.78
  743.0 6.9 fusion.82
  753.0 5.9 convolution_convert_fusion
  758.9 28.9 %reduce-scatter.2.cloned.1.call-done = bf16[384,768]{1,0:T(8,128)(2,1)} async-done(((bf16[384,3072]{1,0:T(8,128)(2,1)}), bf16[384,768]{1,0:T(8,128)(2,1)}) %reduce-scatter.2.cloned.1.call-update) | async-done | bytes 589840 | tf_op jit(solution)/shard_map/reduce_scatter | solution.py:194
  (273 shorter events, 137.3 us)
Async XLA Ops:
  6.5 11.9 %copy-start = (bf16[128,768]{1,0:T(8,128)(2,1)S(1)}, bf16[128,768]{1,0:T(8,128)(2,1)}, u32[]{:S(2)}) copy-start(bf16[128,768]{1,0:T(8,128)(2,1)} %param.13) | copy-start | bytes 589828
  6.5 57.1 %copy-start.5 = (f32[3072]{0:T(1024)S(1)}, f32[3072]{0:T(1024)}, u32[]{:S(2)}) copy-start(f32[3072]{0:T(1024)} %param.15) | copy-start | bytes 36868
  6.5 54.8 %all-gather.4.cloned.1.call-start = ((), (), s32[]{:S(2)}) async-start(), calls=%async_computation.1 | async-start | bytes 2949120 | tf_op jit(solution)/shard_map/all_gather | solution.py:98
  7.4 5.7 collective-permute-start.1
  13.8 4.5 collective-permute-start
  20.3 231.1 %all-gather.6.cloned.1.call-start = ((), (), s32[]{:S(2)}) async-start(), calls=%async_computation.2 | async-start | bytes 19464192 | tf_op jit(solution)/shard_map/all_gather | solution.py:172
  61.3 8.0 %slice-start.2 = ((s8[4718592]{0:T(1024)(128)(4,1)}), s8[4194304]{0:T(1024)(128)(4,1)S(1)}, s32[]{:S(2)}) async-start(s8[4718592]{0:T(1024)(128)(4,1)} %bitcast.74), calls=%async_computation.7 | async-start | bytes 8388608
  63.7 5.6 copy-start.3
  63.7 5.6 slice-start.3
  73.4 5.6 copy-start.4
  73.4 347.1 %all-gather.8.cloned.1.call-start = ((), (), s32[]{:S(2)}) async-start(), calls=%async_computation.3 | async-start | bytes 19464192 | tf_op jit(solution)/shard_map/all_gather | solution.py:173
  78.7 709.1 %reduce-scatter.2.cloned.1.call-start = ((), (), s32[]{:S(2)}) async-start(), calls=%async_computation.4 | async-start | bytes 2949120 | tf_op jit(solution)/shard_map/reduce_scatter | solution.py:194
  430.0 9.1 %slice-start = ((s8[7077888]{0:T(1024)(128)(4,1)}), s8[2883584]{0:T(1024)(128)(4,1)S(1)}, s32[]{:S(2)}) async-start(s8[7077888]{0:T(1024)(128)(4,1)} %bitcast.62), calls=%async_computation.5 | async-start | bytes 5767168 | tf_op jit(solution)/shard_map/while
  432.6 6.6 slice-start.1
  450.5 9.4 %slice-start = ((s8[7077888]{0:T(1024)(128)(4,1)}), s8[2883584]{0:T(1024)(128)(4,1)S(1)}, s32[]{:S(2)}) async-start(s8[7077888]{0:T(1024)(128)(4,1)} %bitcast.62), calls=%async_computation.5 | async-start | bytes 5767168 | tf_op jit(solution)/shard_map/while
  453.0 6.9 slice-start.1
  471.2 9.4 %slice-start = ((s8[7077888]{0:T(1024)(128)(4,1)}), s8[2883584]{0:T(1024)(128)(4,1)S(1)}, s32[]{:S(2)}) async-start(s8[7077888]{0:T(1024)(128)(4,1)} %bitcast.62), calls=%async_computation.5 | async-start | bytes 5767168 | tf_op jit(solution)/shard_map/while
  473.7 6.9 slice-start.1
  491.9 9.4 %slice-start = ((s8[7077888]{0:T(1024)(128)(4,1)}), s8[2883584]{0:T(1024)(128)(4,1)S(1)}, s32[]{:S(2)}) async-start(s8[7077888]{0:T(1024)(128)(4,1)} %bitcast.62), calls=%async_computation.5 | async-start | bytes 5767168 | tf_op jit(solution)/shard_map/while
  494.4 6.9 slice-start.1
  512.6 9.4 %slice-start = ((s8[7077888]{0:T(1024)(128)(4,1)}), s8[2883584]{0:T(1024)(128)(4,1)S(1)}, s32[]{:S(2)}) async-start(s8[7077888]{0:T(1024)(128)(4,1)} %bitcast.62), calls=%async_computation.5 | async-start | bytes 5767168 | tf_op jit(solution)/shard_map/while
  515.1 6.9 slice-start.1
  533.3 9.4 %slice-start = ((s8[7077888]{0:T(1024)(128)(4,1)}), s8[2883584]{0:T(1024)(128)(4,1)S(1)}, s32[]{:S(2)}) async-start(s8[7077888]{0:T(1024)(128)(4,1)} %bitcast.62), calls=%async_computation.5 | async-start | bytes 5767168 | tf_op jit(solution)/shard_map/while
  535.8 6.9 slice-start.1
  554.0 9.4 %slice-start = ((s8[7077888]{0:T(1024)(128)(4,1)}), s8[2883584]{0:T(1024)(128)(4,1)S(1)}, s32[]{:S(2)}) async-start(s8[7077888]{0:T(1024)(128)(4,1)} %bitcast.62), calls=%async_computation.5 | async-start | bytes 5767168 | tf_op jit(solution)/shard_map/while
  556.5 6.9 slice-start.1
  574.7 9.4 %slice-start = ((s8[7077888]{0:T(1024)(128)(4,1)}), s8[2883584]{0:T(1024)(128)(4,1)S(1)}, s32[]{:S(2)}) async-start(s8[7077888]{0:T(1024)(128)(4,1)} %bitcast.62), calls=%async_computation.5 | async-start | bytes 5767168 | tf_op jit(solution)/shard_map/while
  577.3 6.9 slice-start.1
  595.5 9.4 %slice-start = ((s8[7077888]{0:T(1024)(128)(4,1)}), s8[2883584]{0:T(1024)(128)(4,1)S(1)}, s32[]{:S(2)}) async-start(s8[7077888]{0:T(1024)(128)(4,1)} %bitcast.62), calls=%async_computation.5 | async-start | bytes 5767168 | tf_op jit(solution)/shard_map/while
  598.0 6.9 slice-start.1
  616.2 9.4 %slice-start = ((s8[7077888]{0:T(1024)(128)(4,1)}), s8[2883584]{0:T(1024)(128)(4,1)S(1)}, s32[]{:S(2)}) async-start(s8[7077888]{0:T(1024)(128)(4,1)} %bitcast.62), calls=%async_computation.5 | async-start | bytes 5767168 | tf_op jit(solution)/shard_map/while
  618.7 6.9 slice-start.1
  636.9 9.4 %slice-start = ((s8[7077888]{0:T(1024)(128)(4,1)}), s8[2883584]{0:T(1024)(128)(4,1)S(1)}, s32[]{:S(2)}) async-start(s8[7077888]{0:T(1024)(128)(4,1)} %bitcast.62), calls=%async_computation.5 | async-start | bytes 5767168 | tf_op jit(solution)/shard_map/while
  639.4 6.9 slice-start.1
  657.6 9.4 %slice-start = ((s8[7077888]{0:T(1024)(128)(4,1)}), s8[2883584]{0:T(1024)(128)(4,1)S(1)}, s32[]{:S(2)}) async-start(s8[7077888]{0:T(1024)(128)(4,1)} %bitcast.62), calls=%async_computation.5 | async-start | bytes 5767168 | tf_op jit(solution)/shard_map/while
  660.1 6.9 slice-start.1
  678.3 9.4 %slice-start = ((s8[7077888]{0:T(1024)(128)(4,1)}), s8[2883584]{0:T(1024)(128)(4,1)S(1)}, s32[]{:S(2)}) async-start(s8[7077888]{0:T(1024)(128)(4,1)} %bitcast.62), calls=%async_computation.5 | async-start | bytes 5767168 | tf_op jit(solution)/shard_map/while
  680.8 6.9 slice-start.1
  699.0 9.4 %slice-start = ((s8[7077888]{0:T(1024)(128)(4,1)}), s8[2883584]{0:T(1024)(128)(4,1)S(1)}, s32[]{:S(2)}) async-start(s8[7077888]{0:T(1024)(128)(4,1)} %bitcast.62), calls=%async_computation.5 | async-start | bytes 5767168 | tf_op jit(solution)/shard_map/while
  701.5 6.9 slice-start.1
  719.7 9.4 %slice-start = ((s8[7077888]{0:T(1024)(128)(4,1)}), s8[2883584]{0:T(1024)(128)(4,1)S(1)}, s32[]{:S(2)}) async-start(s8[7077888]{0:T(1024)(128)(4,1)} %bitcast.62), calls=%async_computation.5 | async-start | bytes 5767168 | tf_op jit(solution)/shard_map/while
  722.2 6.9 slice-start.1
  740.4 9.4 %slice-start = ((s8[7077888]{0:T(1024)(128)(4,1)}), s8[2883584]{0:T(1024)(128)(4,1)S(1)}, s32[]{:S(2)}) async-start(s8[7077888]{0:T(1024)(128)(4,1)} %bitcast.62), calls=%async_computation.5 | async-start | bytes 5767168 | tf_op jit(solution)/shard_map/while
  743.0 6.9 slice-start.1
  753.0 34.8 %copy-start.2 = (bf16[384,768]{1,0:T(8,128)(2,1)S(1)}, bf16[384,768]{1,0:T(8,128)(2,1)}, u32[]{:S(2)}) copy-start(bf16[384,768]{1,0:T(8,128)(2,1)} %fusion.20) | copy-start | bytes 1769476
  753.0 36.8 %copy-start.1 = (bf16[128,768]{1,0:T(8,128)(2,1)S(1)}, bf16[128,768]{1,0:T(8,128)(2,1)}, u32[]{:S(2)}) copy-start(bf16[128,768]{1,0:T(8,128)(2,1)} %param.13) | copy-start | bytes 589828
Sparse Core Ops, SparseCore 0:
  20.4 40.8 all-gather.3
  73.5 177.9 all-gather.5
  254.4 166.0 all-gather.7
  759.0 28.7 reduce-scatter.1
where the time goes:
time: 799 us; the launch traced here: 796 us
  waiting for transfers between devices  397 us (50%)
  matrix products  220 us (28%)
  local copies, waits for them, and re-layouts  120 us (15%)
  other arithmetic  40.1 us (5%)
  between operations  13.3 us (2%)
    all_gather x1, waiting for transfers between devices, local(): key_rows = lax.all_gather(keys, 'seq', axis=0, tiled=True)  171 us
    all_gather x1, waiting for transfers between devices, local(): value_rows = lax.all_gather(values, 'seq', axis=0, tiled=True)  152 us
    dot_general x16, matrix products, attend(): jnp.einsum('hqk,khd->qhd', weights.astype(jnp.bfloat16), value_heads, pre...  110 us
    dynamic_slice x64, local copies, waits for them, and re-layouts, local(): folded = lax.scan(visit_every, start_state, items)[0]  101 us
    dot_general x16, matrix products, attend(): jnp.einsum('qhd,khd->hqk', query_part, key_heads, preferred_element_type=...  88.6 us
    all_gather x1, waiting for transfers between devices, local(): gathered = lax.all_gather(tokens, 'head', axis=1, tiled=True)  40.3 us
    reduce_scatter x1, waiting for transfers between devices, local(): lax.psum_scatter(projected.astype(jnp.bfloat16), 'head', scatter_dimensio...  28.9 us
    reduce_sum x16, other arithmetic, attend(): total = total * fade + jnp.sum(weights, axis=2)  27.1 us
  transfers between devices with their start and end apart: 6, of which 6 were waited for; matrix products, arithmetic and copies ran while one was open for 3% of the time, Pallas kernels for 0%

commit v1 on v0

v1 whole, which is shorter than its diff:
```python
import functools
import math

import jax
import jax.numpy as jnp
import numpy as np
from jax import lax
from jax.experimental import pallas as pl
from jax.experimental.pallas import tpu as pltpu
from jax.sharding import PartitionSpec as P

HD = 128
HEADS = 6
FT = 192
FRAMES = 64
BF = 4
BK = BF * FT
NB = FRAMES // BF
ROWS = 144
WIDTH = 24
EPS = 1e-06
YARN = 4.0
SCALE = (0.1 * math.log(YARN) + 1.0) ** 2 / math.sqrt(HD) * math.log2(math.e)
FAR = -1e30
LOW, HIGH = 2.0**-60, 2.0**100

F32 = jnp.float32
BF16 = jnp.bfloat16


def spectrum(count):
    return np.exp(-math.log(10000.0) * np.arange(count) / count)


def frequencies():
    pairs = HD // 2
    count_t, count_h = pairs // 4, 3 * pairs // 8
    base_t = spectrum(count_t)
    ramp = np.clip((FRAMES / 4.0 / (2.0 * math.pi / base_t) - 1.0) / 31.0, 0.0, 1.0)
    return base_t * (ramp + (1.0 - ramp) / YARN), spectrum(count_h), spectrum(pairs - count_t - count_h)


def spatial_angles():
    _, w_h, w_w = frequencies()
    inner = np.arange(FT)
    return np.concatenate(
        [np.outer(inner // WIDTH, w_h), np.outer(inner % WIDTH, w_w)], axis=1
    )


def dot(a, b):
    return jnp.dot(a, b, preferred_element_type=F32)


def kernel(
    meta,
    x_ref,
    ghi_ref,
    glo_ref,
    mk_ref,
    mq_ref,
    mv_ref,
    cs_ref,
    ss_ref,
    ct_ref,
    st_ref,
    cq_ref,
    sq_ref,
    wo_ref,
    out_ref,
    u_ref,
    q_ref,
    own_ref,
    ho_ref,
    m_ref,
):
    end_early, end_late = meta[0], meta[1]
    blocks_early = (end_early + BF - 1) // BF
    blocks_late = (end_late + BF - 1) // BF

    def prepare(b):
        x = x_ref[b]
        row = lax.broadcasted_iota(jnp.int32, (ROWS - 128, BK), 0)
        full = jnp.concatenate([x, (row < 3).astype(F32).astype(BF16)], axis=0)
        y = dot(ghi_ref[...], full) + dot(glo_ref[...], full)
        mean_sq = jnp.sum(full.astype(F32) * y, axis=0, keepdims=True)
        r = lax.rsqrt(mean_sq + EPS)
        tail = jnp.where(row == 0, r, jnp.where(row == 1, 1.0, 0.0))
        at = jnp.concatenate([x.astype(F32) * r, tail], axis=0)
        return at.astype(BF16), at.T.astype(BF16)

    def keys_of(b, at, h):
        pre = dot(mk_ref[pl.ds(h * HD, HD), :], at)
        cos = jnp.concatenate([ct_ref[b], cs_ref[...]], axis=0)
        sin = jnp.concatenate([st_ref[b], ss_ref[...]], axis=0)
        first, second = pre[:64], pre[64:]
        rotated = jnp.concatenate(
            [first * cos - second * sin, first * sin + second * cos], axis=0
        ).astype(BF16)
        row = lax.broadcasted_iota(jnp.int32, (ROWS - 128, BK), 0)
        frame = b * BF + lax.broadcasted_iota(jnp.int32, (ROWS - 128, BK), 1) // FT
        end = jnp.where(row == 0, end_early, end_late)
        mask = jnp.where((row < 2) & (frame >= end), FAR, 0.0).astype(BF16)
        return jnp.concatenate([rotated, mask], axis=0)

    for i in range(2):
        frame = meta[2 + i]
        _, av = prepare(frame // BF)
        own_ref[...] = av
        own = own_ref[pl.ds(pl.multiple_of((frame % BF) * FT, FT), FT), :]
        lane = lax.broadcasted_iota(jnp.int32, (FT, ROWS - 128), 1)
        select = (lane == i).astype(F32).astype(BF16)
        for h in range(HEADS):
            pre = dot(own, mq_ref[:, pl.ds(h * HD, HD)])
            rotated = pre * cq_ref[i] + pltpu.roll(pre, 64, 1) * sq_ref[i]
            q_ref[h, pl.ds(i * FT, FT), :] = jnp.concatenate(
                [rotated.astype(BF16), select], axis=1
            )

    u_ref[...] = jnp.zeros_like(u_ref)

    def visit(rows, b, carry):
        at, av = prepare(b)
        for h in range(HEADS):
            s = dot(q_ref[h, rows, :], keys_of(b, at, h))
            w = jnp.exp2(s).astype(BF16)
            u_ref[h, rows, :] += dot(w, av)
        return carry

    lax.fori_loop(0, blocks_early, functools.partial(visit, pl.ds(0, 2 * FT)), 0)
    lax.fori_loop(blocks_early, blocks_late, functools.partial(visit, pl.ds(FT, FT)), 0)

    total = u_ref[:, :, 129:130]
    good = jnp.where((total >= LOW) & (total <= HIGH), 1.0, 0.0)
    bad = jnp.min(good) < 0.5

    @pl.when(bad)
    def _():
        u_ref[...] = jnp.zeros_like(u_ref)
        m_ref[...] = jnp.full_like(m_ref, FAR)

        def visit_again(b, carry):
            at, av = prepare(b)
            for h in range(HEADS):
                s = dot(q_ref[h], keys_of(b, at, h))
                old = m_ref[h]
                new = jnp.maximum(old, jnp.max(s, axis=1, keepdims=True))
                w = jnp.exp2(s - new).astype(BF16)
                u_ref[h] = u_ref[h] * jnp.exp2(old - new) + dot(w, av)
                m_ref[h] = new
            return carry

        lax.fori_loop(0, blocks_late, visit_again, 0)

    for h in range(HEADS):
        u = u_ref[h]
        mixed = (u / u[:, 129:130]).astype(BF16)
        ho_ref[:, pl.ds(h * HD, HD)] = dot(mixed, mv_ref[:, pl.ds(h * HD, HD)]).astype(BF16)
    for n in range(4):
        out_ref[n] = dot(ho_ref[...], wo_ref[:, pl.ds(n * 768, 768)]).astype(BF16)


def attention(meta, *arrays):
    vmem = pl.BlockSpec(memory_space=pltpu.VMEM)
    return pl.pallas_call(
        kernel,
        in_specs=[pl.BlockSpec(memory_space=pltpu.SMEM)] + [vmem] * len(arrays),
        out_specs=vmem,
        out_shape=jax.ShapeDtypeStruct((4, 2 * FT, 768), BF16),
        scratch_shapes=[
            pltpu.VMEM((HEADS, 2 * FT, ROWS), F32),
            pltpu.VMEM((HEADS, 2 * FT, ROWS), BF16),
            pltpu.VMEM((BK, ROWS), BF16),
            pltpu.VMEM((2 * FT, HEADS * HD), BF16),
            pltpu.VMEM((HEADS, 2 * FT, 1), F32),
        ],
        compiler_params=pltpu.CompilerParams(vmem_limit_bytes=56 * 2**20),
    )(meta, *arrays)


def permute(x, axis, to):
    return lax.ppermute(x, axis, [(i, to(i)) for i in range(lax.axis_size(axis))])


def in_turn(parts, at, axis):
    n = len(parts)
    turned = [parts[-r % n] for r in range(n)]
    doubled = jnp.stack(turned + turned[:-1], axis=axis)
    return lax.dynamic_slice_in_dim(doubled, (n - at) % n, n, axis)


def all_latents(latents):
    seq, core = lax.axis_index("seq"), lax.axis_index("head") % 2
    x, y, z = seq // 8, (seq // 4) % 2, seq % 4

    def place(i):
        return i // 8, (i // 4) % 2, i % 4

    def at(x, y, z):
        return (x * 2 + y) * 4 + z

    def to_y(i):
        x, y, z = place(i)
        return at(x, 1 - y, z)

    def to_z(k, i):
        x, y, z = place(i)
        return at(x, y, (z + k) % 4)

    def to_x(k, i):
        x, y, z = place(i)
        return at((x + k) % 4, y, z)

    block = lax.dynamic_slice_in_dim(latents, core * 32, 32, 0)
    block = in_turn([block, permute(block, "seq", to_y)], y, 0)
    parts = [block] + [permute(block, "seq", functools.partial(to_z, k)) for k in (1, 2, 3)]
    block = in_turn(parts, z, 1)
    parts = [block] + [permute(block, "seq", functools.partial(to_x, k)) for k in (1, 2, 3)]
    block = in_turn(parts, x, 0)
    other = permute(block, "head", lambda i: i ^ 1)
    block = in_turn([block, other], core, 3)
    block = block.reshape(32, 64, 2 * FT)
    return jnp.concatenate([block[:, :, :FT], block[::-1, :, FT:]], axis=0)


def all_channels(weight):
    me = lax.axis_index("head")
    parts = [weight] + [permute(weight, "head", lambda i, k=k: (i + k) % 4) for k in (1, 2, 3)]
    block = in_turn(parts, me, 1)
    return block.reshape(weight.shape[0], 4 * weight.shape[1])


def sum_scatter(parts):
    me = lax.axis_index("head")
    core, chip = me % 2, me // 2
    pairs = parts.reshape(2, 2, *parts.shape[1:])
    mine = lax.dynamic_index_in_dim(pairs, core, 1, False)
    other = permute(lax.dynamic_index_in_dim(pairs, 1 - core, 1, False), "head", lambda i: i ^ 1)
    both = (mine.astype(F32) + other.astype(F32)).astype(BF16)
    mine = lax.dynamic_index_in_dim(both, chip, 0, False)
    other = permute(lax.dynamic_index_in_dim(both, 1 - chip, 0, False), "head", lambda i: i ^ 2)
    return mine.astype(F32) + other.astype(F32)


def local(
    latents,
    span_ids,
    patch_weight,
    patch_bias,
    norm_gain,
    query_weight,
    key_weight,
    value_weight,
    out_weight,
):
    seq = lax.axis_index("seq")
    frames = jnp.stack([seq, FRAMES - 1 - seq]).astype(jnp.int32)
    own_span = jnp.sum(jnp.where(frames[:, None] == jnp.arange(FRAMES)[None], span_ids[None], 0), axis=1)
    ends = jnp.sum((span_ids[None, :] <= own_span[:, None]).astype(jnp.int32), axis=1)
    meta = jnp.concatenate([ends, frames])

    natural = all_latents(latents)
    before = jnp.concatenate([jnp.zeros((1, 64, FT), BF16), natural[:-1]], axis=0)
    patches = jnp.concatenate([before, natural], axis=1)
    x = patches.reshape(NB, BF, 128, FT).transpose(0, 2, 1, 3).reshape(NB, 128, BK)

    b0 = patch_bias.astype(BF16)
    b1 = (patch_bias - b0.astype(F32)).astype(BF16)
    b2 = (patch_bias - b0.astype(F32) - b1.astype(F32)).astype(BF16)
    rest = jnp.zeros((ROWS - 131, patch_bias.shape[0]), BF16)
    wide = all_channels(jnp.concatenate([patch_weight, b0[None], b1[None], b2[None], rest], axis=0))
    gram = lax.dot_general(wide, wide, (((1,), (1,)), ((), ())), preferred_element_type=F32)
    gram = gram * (1.0 / wide.shape[1])
    ghi = gram.astype(BF16)
    glo = (gram - ghi.astype(F32)).astype(BF16)
    bias = jnp.sum(wide[128:131].astype(F32), axis=0, keepdims=True)
    row = jnp.arange(ROWS)[:, None]
    gained = jnp.where(row < 128, wide.astype(F32), jnp.where(row == 128, bias, 0.0))
    gained = (gained * norm_gain[None]).astype(BF16)
    mq = dot(gained, query_weight).astype(BF16)
    mv = dot(gained, value_weight).astype(BF16)
    mk = lax.dot_general(
        key_weight, gained, (((0,), (1,)), ((), ())), preferred_element_type=F32
    ).astype(BF16)

    w_t, _, _ = frequencies()
    spatial = spatial_angles()
    cs = jnp.asarray(np.tile(np.cos(spatial).T, (1, BF)), F32)
    ss = jnp.asarray(np.tile(np.sin(spatial).T, (1, BF)), F32)
    temporal = np.outer(np.arange(FRAMES), w_t)
    by_block = np.repeat(temporal.reshape(NB, BF, 16).transpose(0, 2, 1), FT, axis=2)
    ct = jnp.asarray(np.cos(by_block), F32)
    st = jnp.asarray(np.sin(by_block), F32)
    angle = frames.astype(F32)[:, None] * jnp.asarray(w_t, F32)[None]

    def of_queries(turn, space):
        own = jnp.broadcast_to(turn[:, None, :], (2, FT, 16))
        return jnp.concatenate([own, jnp.broadcast_to(jnp.asarray(space, F32)[None], (2, FT, 48))], axis=2) * SCALE

    cq = of_queries(jnp.cos(angle), np.cos(spatial))
    sq = of_queries(jnp.sin(angle), np.sin(spatial))
    cq = jnp.concatenate([cq, cq], axis=2)
    sq = jnp.concatenate([-sq, sq], axis=2)

    parts = attention(meta, x, ghi, glo, mk, mq, mv, cs, ss, ct, st, cq, sq, out_weight)
    summed = sum_scatter(parts)

    own = jnp.concatenate(
        [lax.dynamic_index_in_dim(patches, frames[i], 0, False) for i in range(2)], axis=1
    )
    conv = lax.dot_general(own, patch_weight, (((0,), (0,)), ((), ())), preferred_element_type=F32)
    tokens = (conv + patch_bias[None, :]).astype(BF16)
    return (summed + tokens.astype(F32)).astype(BF16)


def solution(mesh):
    return jax.shard_map(
        local,
        mesh=mesh,
        in_specs=(
            P(None, "seq"),
            P(),
            P(None, "head"),
            P("head"),
            P(),
            P(None, "head"),
            P(None, "head"),
            P(None, "head"),
            P("head", None),
        ),
        out_specs=P("seq", "head"),
        check_vma=False,
    )
```

time: 799 us -> 234 us (0.29)
  waiting for transfers between devices: 397 us -> 25.7 us
  matrix products: 220 us -> 12.9 us
  Pallas kernels: 0 us -> 133 us
  local copies, waits for them, and re-layouts: 120 us -> 27.6 us
  other arithmetic: 40.1 us -> 14.9 us
  starting transfers between devices: 5.12 us -> 18.3 us
  between operations: 13.3 us -> 0.34 us
    all_gather x3 -> x0, waiting for transfers between devices: 363 us -> none  [the longest x1 171 us: local(): key_rows = lax.all_gather(keys, 'seq', axis=0, tiled=True)]
    dot_general x37 -> x5, matrix products: 220 us -> 12.9 us  [the longest x2 5.72 us: dot(): return jnp.dot(a, b, preferred_element_type=F32)]
    pallas_call x0 -> x1, Pallas kernels: none -> 133 us  [attention(): pl.pallas_call(kernel, in_specs=[pl.BlockSpec(memory_space=pltpu.SMEM)] +...]
    dynamic_slice x64 -> x2, local copies, waits for them, and re-layouts: 101 us -> 1.01 us  [the longest x1 1.01 us: in_turn(): return lax.dynamic_slice_in_dim(doubled, (n - at) % n, n, axis)]
    reduce_scatter x1 -> x0, waiting for transfers between devices: 28.9 us -> none  [local(): lax.psum_scatter(projected.astype(jnp.bfloat16), 'head', scatter_dimensio...]
    reduce_sum x19 -> x3, other arithmetic: 30.1 us -> 2.52 us  [the longest x1 0.84 us: local(): bias = jnp.sum(wide[128:131].astype(F32), axis=0, keepdims=True)]
    ppermute x2 -> x13, waiting for transfers between devices: 5.37 us -> 25.7 us  [permute(): lax.ppermute(x, axis, [(i, to(i)) for i in range(lax.axis_size(axis))])]
    reshape x2 -> x1, local copies, waits for them, and re-layouts: 16.9 us -> 2.83 us  [local(): patches.reshape(NB, BF, 128, FT).transpose(0, 2, 1, 3).reshape(NB, 128, BK)]
  transfers between devices with their start and end apart: 6 -> 13, of which waited for: 6 -> 6; matrix products, arithmetic and copies ran while one was open for 3% -> 13% of each run, Pallas kernels for 0% -> 0%
where the time goes in v1:
time: 234 us; the launch traced here: 233 us
  Pallas kernels  133 us (57%)
  local copies, waits for them, and re-layouts  27.6 us (12%)
  waiting for transfers between devices  25.7 us (11%)
  starting transfers between devices  18.3 us (8%)
  other arithmetic  14.9 us (6%)
  matrix products  12.9 us (6%)
    pallas_call x1, Pallas kernels, attention(): pl.pallas_call(kernel, in_specs=[pl.BlockSpec(memory_space=pltpu.SMEM)] +...  133 us
    ppermute x13, waiting for transfers between devices, permute(): lax.ppermute(x, axis, [(i, to(i)) for i in range(lax.axis_size(axis))])  25.7 us
    ppermute x13, starting transfers between devices, permute(): lax.ppermute(x, axis, [(i, to(i)) for i in range(lax.axis_size(axis))])  18.3 us
    unnamed x39, local copies, waits for them, and re-layouts  9.07 us
    dot_general x2, matrix products, dot(): return jnp.dot(a, b, preferred_element_type=F32)  5.72 us
    concatenate x1, local copies, waits for them, and re-layouts, local(): patches = jnp.concatenate([before, natural], axis=1)  5.5 us
  transfers between devices with their start and end apart: 13, of which 6 were waited for; matrix products, arithmetic and copies ran while one was open for 13% of the time, Pallas kernels for 0%

profile of v1, /device:TPU:1, one launch (start us, length us, event | category | flops | bytes accessed | tf_op | source)
XLA Modules:
  0.0 233.0 jit_solution(474234526377915951)
XLA Ops:
  0.0 0.8 subtract_convert_fusion.1
  0.8 1.1 concatenate.39
  2.0 1.5 collective-permute-start.8
  3.4 1.4 collective-permute-start.9
  4.8 1.3 collective-permute-start.10
  6.2 2.6 %collective-permute-start = (bf16[32,384]{1,0:T(8,128)(2,1)S(1)}, bf16[32,384]{1,0:T(8,128)(2,1)S(1)}, u32[]{:S(2)}, u32[]{:S(2)}) collective-permute-start(bf16[32,384]{1,0:T(8,128)(2,1)S(1)} %constant_dynamic-slice_fusion.2), channel_id=1, source_target_pairs={{0,16},{4,20},{8,24},{12,28},{16,0},{20,4},{24,8},{28,12},{32,48},... | collective-permute-start | bytes 73736 | tf_op jit(solution)/shard_map/ppermute | solution.py:182
  8.8 0.7 bitcast_dynamic-update-slice_fusion.5
  9.6 0.8 fusion.20
  10.4 0.8 fusion.21
  11.3 0.8 multiply_sine_fusion
  12.1 0.9 broadcast_in_dim.99
  13.3 1.0 pad_maximum_fusion
  14.2 4.2 %collective-permute-done = bf16[32,384]{1,0:T(8,128)(2,1)S(1)} collective-permute-done((bf16[32,384]{1,0:T(8,128)(2,1)S(1)}, bf16[32,384]{1,0:T(8,128)(2,1)S(1)}, u32[]{:S(2)}, u32[]{:S(2)}) %collective-permute-start) | collective-permute-done | bytes 24608 | tf_op jit(solution)/shard_map/ppermute | solution.py:182
  18.5 3.8 %collective-permute-start.1 = (bf16[2,32,384]{2,1,0:T(8,128)(2,1)S(1)}, bf16[2,32,384]{2,1,0:T(8,128)(2,1)S(1)}, u32[]{:S(2)}, u32[]{:S(2)}) collective-permute-start(bf16[2,32,384]{2,1,0:T(8,128)(2,1)S(1)} %get-tuple-element.12), channel_id=1, source_target_pairs={{0,12},{4,0},{8,4},{12,8},{16,28},{20,16},{24,20},{28,24},{32,44},... | collective-permute-start | bytes 147464 | tf_op jit(solution)/shard_map/ppermute | solution.py:182
  23.7 3.7 %collective-permute-done.2 = bf16[2,32,384]{2,1,0:T(8,128)(2,1)S(1)} collective-permute-done((bf16[2,32,384]{2,1,0:T(8,128)(2,1)S(1)}, bf16[2,32,384]{2,1,0:T(8,128)(2,1)S(1)}, u32[]{:S(2)}, u32[]{:S(2)}) %collective-permute-start.2) | collective-permute-done | bytes 49184 | tf_op jit(solution)/shard_map/ppermute | solution.py:182
  28.1 0.7 bitcast_dynamic-update-slice_fusion.12
  28.8 2.5 %collective-permute-start.4 = (bf16[2,4,32,384]{3,2,1,0:T(8,128)(2,1)}, bf16[2,4,32,384]{3,2,1,0:T(8,128)(2,1)S(1)}, u32[]{:S(2)}, u32[]{:S(2)}) collective-permute-start(bf16[2,4,32,384]{3,2,1,0:T(8,128)(2,1)} %get-tuple-element.10), channel_id=1, source_target_pairs={{0,96},{4,100},{8,104},{12,108},{16,112},{20,116},{24,120},{28,124... | collective-permute-start | bytes 589832 | tf_op jit(solution)/shard_map/ppermute | solution.py:182
  32.4 0.7 bitcast_dynamic-update-slice_fusion.3
  33.1 0.7 bitcast_dynamic-update-slice_fusion.1
  33.8 0.7 bitcast_dynamic-update-slice_fusion
  34.5 0.7 bitcast_dynamic-update-slice_fusion.6
  35.2 0.7 bitcast_dynamic-update-slice_fusion.4
  35.9 0.7 bitcast_dynamic-update-slice_fusion.2
  36.6 1.3 convert_bitcast_fusion
  38.1 0.8 convert_reduce_fusion
  39.0 4.1 %convolution_convert_fusion.2 = bf16[144,768]{1,0:T(8,128)(2,1)} fusion(bf16[3072,768]{1,0:T(8,128)(2,1)} %param.22, f32[144,3072]{1,0:T(8,128)S(1)} %bitcast.85, f32[3072]{0:T(1024)S(1)} %copy-done.8, f32[3072]{0:T(1024)S(1)} %broadcast_in_dim.95, pred[144]{0:T(512)(128)(4,1)S(1)} %get-tuple-element.24, pred[144]{0:T(512)(128)(4,1)S(1)} %get-tuple-element.25), kind=kOutput, calls=%fused_computation.19 | convolution fusion | flops 681357312 | bytes 6734112 | tf_op jit(solution)/shard_map/dot_general | solution.py:282
  43.2 1.0 bitcast_dynamic-update-slice_fusion.8
  44.2 1.0 bitcast_dynamic-update-slice_fusion.7
  45.1 1.0 bitcast_dynamic-update-slice_fusion.13
  46.1 1.0 bitcast_dynamic-update-slice_fusion.9
  47.1 1.0 constant_dynamic-slice_fusion
  48.1 3.8 %collective-permute-start.7 = (bf16[4,2,4,32,384]{4,3,2,1,0:T(8,128)(2,1)}, bf16[4,2,4,32,384]{4,3,2,1,0:T(8,128)(2,1)}, u32[]{:S(2)}, u32[]{:S(2)}) collective-permute-start(bf16[4,2,4,32,384]{4,3,2,1,0:T(8,128)(2,1)} %constant_dynamic-slice_fusion), channel_id=1, source_target_pairs={{0,1},{1,0},{2,3},{3,2},{4,5},{5,4},{6,7},{7,6},{8,9},{9,8},{10,11... | collective-permute-start | bytes 2359304 | tf_op jit(solution)/shard_map/ppermute | solution.py:182
  51.9 1.7 convolution_convert_fusion.1.mq_ref
  53.6 0.9 copy.40
  54.5 2.6 %subtract_convert_fusion = (bf16[144,144]{1,0:T(8,128)(2,1)}, bf16[144,144]{1,0:T(8,128)(2,1)}) fusion(bf16[144,7,768]{2,0,1:T(8,128)(2,1)} %bitcast_dynamic-update-slice_fusion.2, s32[]{:T(128)S(6)} %select_n.114), kind=kOutput, calls=%fused_computation.46 | convolution fusion | flops 127505664 | bytes 967684 | tf_op jit(solution)/shard_map/dot_general | solution.py:272
  57.2 4.0 %convolution_convert_fusion.mv_ref = bf16[144,768]{1,0:T(8,128)(2,1)} fusion(bf16[3072,768]{1,0:T(8,128)(2,1)} %param.23, f32[144,3072]{1,0:T(8,128)S(1)} %bitcast.87, f32[3072]{0:T(1024)S(1)} %copy-done.8, f32[3072]{0:T(1024)S(1)} %broadcast_in_dim.95, pred[144]{0:T(512)(128)(4,1)S(1)} %get-tuple-element.24, pred[144]{0:T(512)(128)(4,1)S(1)} %get-tuple-element.25), kind=kOutput, calls=%fused_computation.17 | convolution fusion | flops 681357312 | bytes 6734112 | tf_op jit(solution)/shard_map/dot_general | solution.py:52
  61.3 1.9 fusion.5
  64.3 2.6 %maximum_maximum_fusion = bf16[64,128,192]{2,1,0:T(8,128)(2,1)} fusion(bf16[32,64,192]{2,1,0:T(8,128)(2,1)S(1)} %rev.3, bf16[32,64,192]{2,1,0:T(8,128)(2,1)S(1)} %get-tuple-element.15, bf16[64,64,192]{2,1,0:T(8,128)(2,1)S(1)} %fusion.3), kind=kLoop, calls=%fused_computation.3 | loop fusion | flops 9437184 | bytes 6291456 | tf_op jit(solution)/shard_map/concatenate | solution.py:264
  67.0 5.5 %copy.38 = bf16[64,128,192]{1,2,0:T(8,128)(2,1)S(1)} copy(bf16[64,128,192]{2,1,0:T(8,128)(2,1)} %maximum_maximum_fusion) | data formatting | bytes 6291456 | tf_op jit(solution)/shard_map/concatenate | solution.py:264
  72.5 2.8 %copy.41.x_ref = bf16[16,128,768]{2,1,0:T(8,128)(2,1)} copy(bf16[16,128,768]{1,2,0:T(8,128)(2,1)S(1)} %bitcast.81) | data formatting | bytes 6291456 | tf_op jit(solution)/shard_map/reshape | solution.py:265
  75.3 133.4 %shard_map.154 = bf16[4,384,768]{2,1,0:T(8,128)(2,1)} custom-call(s32[4]{0:T(128)} %pad_add_fusion.1.meta, bf16[16,128,768]{2,1,0:T(8,128)(2,1)} %copy.41.x_ref, bf16[144,144]{1,0:T(8,128)(2,1)} %get-tuple-element.8.ghi_ref, bf16[144,144]{1,0:T(8,128)(2,1)} %get-tuple-element.7.glo_ref, bf16[768,144]{1,0:T(8,128)(2,1)} %bitcast.88, ...), custom_call_target="tpu_custom_call" | custom-call | tf_op jit(solution)/shard_map/pallas_call | solution.py:165
  208.7 2.5 %dynamic-slice_bitcast_fusion = bf16[2,384,768]{2,1,0:T(8,128)(2,1)} fusion(bf16[2,2,384,768]{3,2,1,0:T(8,128)(2,1)} %bitcast.82, s32[]{:T(128)S(6)} %select_n.118), kind=kLoop, calls=%fused_computation.23 | loop fusion | bytes 2359300 | tf_op jit(solution)/shard_map/jit(dynamic_index_in_dim)/squeeze | solution.py:238
  211.3 3.2 %collective-permute-done.11 = bf16[2,384,768]{2,1,0:T(8,128)(2,1)} collective-permute-done((bf16[2,384,768]{2,1,0:T(8,128)(2,1)}, bf16[2,384,768]{2,1,0:T(8,128)(2,1)}, u32[]{:S(2)}, u32[]{:S(2)}) %collective-permute-start.11) | collective-permute-done | bytes 1179680 | tf_op jit(solution)/shard_map/ppermute | solution.py:182
  214.5 1.5 fusion.2
  216.0 1.1 copy-done.2
  217.2 1.0 dynamic-slice_bitcast_fusion.3
  218.6 13.4 %collective-permute-done.12 = bf16[384,768]{1,0:T(8,128)(2,1)S(1)} collective-permute-done((bf16[384,768]{1,0:T(8,128)(2,1)S(1)}, bf16[384,768]{1,0:T(8,128)(2,1)S(1)}, u32[]{:S(2)}, u32[]{:S(2)}) %collective-permute-start.12) | collective-permute-done | bytes 589856 | tf_op jit(solution)/shard_map/ppermute | solution.py:182
  232.0 1.0 fusion.9
  (68 shorter events, 5.6 us)
Async XLA Ops:
  0.0 6.2 %copy-start = (bf16[64,384]{1,0:T(8,128)(2,1)S(1)}, bf16[64,384]{1,0:T(8,128)(2,1)}, u32[]{:S(2)}) copy-start(bf16[64,384]{1,0:T(8,128)(2,1)} %param.16) | copy-start | bytes 147460
  0.0 13.1 %copy-start.6 = (f32[192,48]{1,0:T(8,128)S(1)}, f32[192,48]{1,0:T(8,128)}, u32[]{:S(2)}) copy-start(f32[192,48]{1,0:T(8,128)} %constant.150.clone) | copy-start | bytes 110596
  2.0 29.8 %collective-permute-start.8 = (bf16[144,768]{1,0:T(8,128)(2,1)S(1)}, bf16[144,768]{1,0:T(8,128)(2,1)S(1)}, u32[]{:S(2)}, u32[]{:S(2)}) collective-permute-start(bf16[144,768]{1,0:T(8,128)(2,1)S(1)} %concatenate.39), channel_id=1, source_target_pairs={{0,3},{1,0},{2,1},{3,2},{4,7},{5,4},{6,5},{7,6},{8,11},{9,8},{10,9... | collective-permute-start | bytes 663560 | tf_op jit(solution)/shard_map/ppermute | solution.py:182
  3.4 29.6 %collective-permute-start.9 = (bf16[144,768]{1,0:T(8,128)(2,1)S(1)}, bf16[144,768]{1,0:T(8,128)(2,1)S(1)}, u32[]{:S(2)}, u32[]{:S(2)}) collective-permute-start(bf16[144,768]{1,0:T(8,128)(2,1)S(1)} %concatenate.39), channel_id=1, source_target_pairs={{0,2},{1,3},{2,0},{3,1},{4,6},{5,7},{6,4},{7,5},{8,10},{9,11},{10,... | collective-permute-start | bytes 663560 | tf_op jit(solution)/shard_map/ppermute | solution.py:182
  4.8 29.0 %collective-permute-start.10 = (bf16[144,768]{1,0:T(8,128)(2,1)S(1)}, bf16[144,768]{1,0:T(8,128)(2,1)S(1)}, u32[]{:S(2)}, u32[]{:S(2)}) collective-permute-start(bf16[144,768]{1,0:T(8,128)(2,1)S(1)} %concatenate.39), channel_id=1, source_target_pairs={{0,1},{1,2},{2,3},{3,0},{4,5},{5,6},{6,7},{7,4},{8,9},{9,10},{10,1... | collective-permute-start | bytes 663560 | tf_op jit(solution)/shard_map/ppermute | solution.py:182
  6.2 12.3 %collective-permute-start = (bf16[32,384]{1,0:T(8,128)(2,1)S(1)}, bf16[32,384]{1,0:T(8,128)(2,1)S(1)}, u32[]{:S(2)}, u32[]{:S(2)}) collective-permute-start(bf16[32,384]{1,0:T(8,128)(2,1)S(1)} %constant_dynamic-slice_fusion.2), channel_id=1, source_target_pairs={{0,16},{4,20},{8,24},{12,28},{16,0},{20,4},{24,8},{28,12},{32,48},... | collective-permute-start | bytes 73736 | tf_op jit(solution)/shard_map/ppermute | solution.py:182
  18.5 5.0 %collective-permute-start.1 = (bf16[2,32,384]{2,1,0:T(8,128)(2,1)S(1)}, bf16[2,32,384]{2,1,0:T(8,128)(2,1)S(1)}, u32[]{:S(2)}, u32[]{:S(2)}) collective-permute-start(bf16[2,32,384]{2,1,0:T(8,128)(2,1)S(1)} %get-tuple-element.12), channel_id=1, source_target_pairs={{0,12},{4,0},{8,4},{12,8},{16,28},{20,16},{24,20},{28,24},{32,44},... | collective-permute-start | bytes 147464 | tf_op jit(solution)/shard_map/ppermute | solution.py:182
  23.0 4.4 %collective-permute-start.2 = (bf16[2,32,384]{2,1,0:T(8,128)(2,1)S(1)}, bf16[2,32,384]{2,1,0:T(8,128)(2,1)S(1)}, u32[]{:S(2)}, u32[]{:S(2)}) collective-permute-start(bf16[2,32,384]{2,1,0:T(8,128)(2,1)S(1)} %get-tuple-element.12), channel_id=1, source_target_pairs={{0,8},{4,12},{8,0},{12,4},{16,24},{20,28},{24,16},{28,20},{32,40},... | collective-permute-start | bytes 147464 | tf_op jit(solution)/shard_map/ppermute | solution.py:182
  23.5 4.5 %collective-permute-start.3 = (bf16[2,32,384]{2,1,0:T(8,128)(2,1)S(1)}, bf16[2,32,384]{2,1,0:T(8,128)(2,1)S(1)}, u32[]{:S(2)}, u32[]{:S(2)}) collective-permute-start(bf16[2,32,384]{2,1,0:T(8,128)(2,1)S(1)} %get-tuple-element.12), channel_id=1, source_target_pairs={{0,4},{4,8},{8,12},{12,0},{16,20},{20,24},{24,28},{28,16},{32,36},... | collective-permute-start | bytes 147464 | tf_op jit(solution)/shard_map/ppermute | solution.py:182
  28.8 14.4 %collective-permute-start.4 = (bf16[2,4,32,384]{3,2,1,0:T(8,128)(2,1)}, bf16[2,4,32,384]{3,2,1,0:T(8,128)(2,1)S(1)}, u32[]{:S(2)}, u32[]{:S(2)}) collective-permute-start(bf16[2,4,32,384]{3,2,1,0:T(8,128)(2,1)} %get-tuple-element.10), channel_id=1, source_target_pairs={{0,96},{4,100},{8,104},{12,108},{16,112},{20,116},{24,120},{28,124... | collective-permute-start | bytes 589832 | tf_op jit(solution)/shard_map/ppermute | solution.py:182
  31.3 11.9 %collective-permute-start.5 = (bf16[2,4,32,384]{3,2,1,0:T(8,128)(2,1)}, bf16[2,4,32,384]{3,2,1,0:T(8,128)(2,1)}, u32[]{:S(2)}, u32[]{:S(2)}) collective-permute-start(bf16[2,4,32,384]{3,2,1,0:T(8,128)(2,1)} %get-tuple-element.10), channel_id=1, source_target_pairs={{0,64},{4,68},{8,72},{12,76},{16,80},{20,84},{24,88},{28,92},{32,9... | collective-permute-start | bytes 589832 | tf_op jit(solution)/shard_map/ppermute | solution.py:182
  31.8 12.4 %collective-permute-start.6 = (bf16[2,4,32,384]{3,2,1,0:T(8,128)(2,1)}, bf16[2,4,32,384]{3,2,1,0:T(8,128)(2,1)}, u32[]{:S(2)}, u32[]{:S(2)}) collective-permute-start(bf16[2,4,32,384]{3,2,1,0:T(8,128)(2,1)} %get-tuple-element.10), channel_id=1, source_target_pairs={{0,32},{4,36},{8,40},{12,44},{16,48},{20,52},{24,56},{28,60},{32,6... | collective-permute-start | bytes 589832 | tf_op jit(solution)/shard_map/ppermute | solution.py:182
  37.9 1.1 copy-start.8
  39.0 12.9 %slice-start = ((s8[4718592]{0:T(1024)(128)(4,1)}), s8[4194304]{0:T(1024)(128)(4,1)S(1)}, s32[]{:S(2)}) async-start(s8[4718592]{0:T(1024)(128)(4,1)} %bitcast.90), calls=%async_computation | async-start | bytes 8388608
  39.0 12.9 %slice-start.1 = ((s8[4718592]{0:T(1024)(128)(4,1)}), s8[524288]{0:T(1024)(128)(4,1)S(1)}, s32[]{:S(2)}) async-start(s8[4718592]{0:T(1024)(128)(4,1)} %bitcast.90), calls=%async_computation.1 | async-start | bytes 1048576
  48.1 5.5 %copy-start.5 = (bf16[144,768]{1,0:T(8,128)(2,1)S(1)}, bf16[144,768]{1,0:T(8,128)(2,1)}, u32[]{:S(2)}) copy-start(bf16[144,768]{1,0:T(8,128)(2,1)} %convolution_convert_fusion.2) | copy-start | bytes 663556
  48.1 13.2 %collective-permute-start.7 = (bf16[4,2,4,32,384]{4,3,2,1,0:T(8,128)(2,1)}, bf16[4,2,4,32,384]{4,3,2,1,0:T(8,128)(2,1)}, u32[]{:S(2)}, u32[]{:S(2)}) collective-permute-start(bf16[4,2,4,32,384]{4,3,2,1,0:T(8,128)(2,1)} %constant_dynamic-slice_fusion), channel_id=1, source_target_pairs={{0,1},{1,0},{2,3},{3,2},{4,5},{5,4},{6,7},{7,6},{8,9},{9,8},{10,11... | collective-permute-start | bytes 2359304 | tf_op jit(solution)/shard_map/ppermute | solution.py:182
  208.7 5.7 %copy-start.1 = (bf16[4,384,768]{2,1,0:T(8,128)(2,1)S(1)}, bf16[4,384,768]{2,1,0:T(8,128)(2,1)}, u32[]{:S(2)}) copy-start(bf16[4,384,768]{2,1,0:T(8,128)(2,1)} %shard_map.154) | copy-start | bytes 7077892
  211.3 3.2 %collective-permute-start.11 = (bf16[2,384,768]{2,1,0:T(8,128)(2,1)}, bf16[2,384,768]{2,1,0:T(8,128)(2,1)}, u32[]{:S(2)}, u32[]{:S(2)}) collective-permute-start(bf16[2,384,768]{2,1,0:T(8,128)(2,1)} %dynamic-slice_bitcast_fusion), channel_id=1, source_target_pairs={{0,1},{1,0},{2,3},{3,2},{4,5},{5,4},{6,7},{7,6},{8,9},{9,8},{10,11... | collective-permute-start | bytes 3538952 | tf_op jit(solution)/shard_map/ppermute | solution.py:182
  211.3 6.9 %copy-start.4 = (bf16[128,768]{1,0:T(8,128)(2,1)S(1)}, bf16[128,768]{1,0:T(8,128)(2,1)}, u32[]{:S(2)}) copy-start(bf16[128,768]{1,0:T(8,128)(2,1)} %param.18) | copy-start | bytes 589828
  211.3 6.9 %copy-start.7 = (f32[768]{0:T(1024)S(1)}, f32[768]{0:T(1024)}, u32[]{:S(2)}) copy-start(f32[768]{0:T(1024)} %param.19) | copy-start | bytes 9220
  216.0 1.1 copy-start.2
  217.1 14.9 %copy-start.3 = (bf16[2,384,768]{2,1,0:T(8,128)(2,1)S(1)}, bf16[2,384,768]{2,1,0:T(8,128)(2,1)}, u32[]{:S(2)}) copy-start(bf16[2,384,768]{2,1,0:T(8,128)(2,1)} %copy-done.2) | copy-start | bytes 3538948
  217.1 14.9 %collective-permute-start.12 = (bf16[384,768]{1,0:T(8,128)(2,1)S(1)}, bf16[384,768]{1,0:T(8,128)(2,1)S(1)}, u32[]{:S(2)}, u32[]{:S(2)}) collective-permute-start(bf16[384,768]{1,0:T(8,128)(2,1)S(1)} %dynamic-slice_bitcast_fusion.1), channel_id=1, source_target_pairs={{0,2},{1,3},{2,0},{3,1},{4,6},{5,7},{6,4},{7,5},{8,10},{9,11},{10,... | collective-permute-start | bytes 1769480 | tf_op jit(solution)/shard_map/ppermute | solution.py:182

commit v2 on v1

v2 whole, which is shorter than its diff:
```python
import functools
import math

import jax
import jax.numpy as jnp
import numpy as np
from jax import lax
from jax.experimental import pallas as pl
from jax.experimental.pallas import tpu as pltpu
from jax.sharding import PartitionSpec as P

HD = 128
HEADS = 6
FT = 192
FRAMES = 64
BF = 4
BK = BF * FT
NB = FRAMES // BF
ROWS = 144
WIDTH = 24
EPS = 1e-06
YARN = 4.0
SCALE = (0.1 * math.log(YARN) + 1.0) ** 2 / math.sqrt(HD) * math.log2(math.e)
FAR = -1e30
LOW, HIGH = 2.0**-60, 2.0**100

F32 = jnp.float32
BF16 = jnp.bfloat16


def spectrum(count):
    return np.exp(-math.log(10000.0) * np.arange(count) / count)


def frequencies():
    pairs = HD // 2
    count_t, count_h = pairs // 4, 3 * pairs // 8
    base_t = spectrum(count_t)
    ramp = np.clip((FRAMES / 4.0 / (2.0 * math.pi / base_t) - 1.0) / 31.0, 0.0, 1.0)
    return base_t * (ramp + (1.0 - ramp) / YARN), spectrum(count_h), spectrum(pairs - count_t - count_h)


def spatial_angles():
    _, w_h, w_w = frequencies()
    inner = np.arange(FT)
    return np.concatenate(
        [np.outer(inner // WIDTH, w_h), np.outer(inner % WIDTH, w_w)], axis=1
    )


def dot(a, b):
    return jnp.dot(a, b, preferred_element_type=F32)


def kernel(
    meta,
    *refs,
):
    pieces, refs = refs[:8], refs[8:]
    (mg_ref, mq_ref, mv_ref, pw_ref, cs_ref, ss_ref, ct_ref, st_ref, cq_ref, sq_ref, wo_ref) = refs[:11]
    (outs, tokens_ref), refs = (refs[11:15], refs[15]), refs[16:]
    raw_ref, wide_ref, own_ref, q_ref, w_ref, u_ref, ho_ref, m_ref, sems, wo_sem = refs
    end_early, end_late = meta[0], meta[1]
    blocks_early = (end_early + BF - 1) // BF
    blocks_late = (end_late + BF - 1) // BF
    x_at, y_at, core, chip = meta[4], meta[5], meta[6], meta[7]

    out_copy = pltpu.make_async_copy(wo_ref, wide_ref, wo_sem)
    out_copy.start()
    copies = []
    for k in range(4):
        for c in range(2):
            rows = pl.ds(pl.multiple_of((core ^ c) * 32, 32), 32)
            for i in range(2):
                group = ((x_at + 4 - k) % 4) * 2 + (y_at ^ i)
                for late in range(2):
                    block = NB - 1 - group if late else group
                    copies.append(
                        pltpu.make_async_copy(
                            pieces[2 * k + c].at[i, late],
                            raw_ref.at[block, rows],
                            sems.at[len(copies)],
                        )
                    )
    for copy in copies:
        copy.start()
    for copy in copies:
        copy.wait()

    row = lax.broadcasted_iota(jnp.int32, (ROWS - 128, BK), 0)
    lane_frame = lax.broadcasted_iota(jnp.int32, (ROWS - 128, BK), 1) // FT
    ones = (row < 3).astype(F32).astype(BF16)

    def features(b):
        now = raw_ref[b]
        last = raw_ref[jnp.maximum(b - 1, 0)][:, BK - FT :]
        last = jnp.where(b > 0, last, jnp.zeros_like(last))
        before = jnp.concatenate([last, now[:, : BK - FT]], axis=1)
        return jnp.concatenate([before, now, ones], axis=0)

    def norm(x, gram):
        y = gram[:ROWS] + gram[ROWS:]
        return lax.rsqrt(jnp.sum(x.astype(F32) * y, axis=0, keepdims=True) + EPS)

    def scaled(x, r):
        tail = jnp.where(row == 0, r, jnp.where(row == 1, 1.0, 0.0))
        return jnp.concatenate([x[:128].astype(F32) * r, tail], axis=0).astype(BF16).T

    def prepare(b):
        x = features(b)
        big = dot(mg_ref[...], x)
        r = norm(x, big[HEADS * HD :])
        cos = jnp.concatenate([ct_ref[b], cs_ref[...]], axis=0) * r
        sin = jnp.concatenate([st_ref[b], ss_ref[...]], axis=0) * r
        end = jnp.where(row == 0, end_early, end_late)
        mask = jnp.where((row < 2) & (b * BF + lane_frame >= end), FAR, 0.0).astype(BF16)

        def keys(h):
            first, second = big[h * HD : h * HD + 64], big[h * HD + 64 : h * HD + HD]
            return jnp.concatenate(
                [
                    (first * cos - second * sin).astype(BF16),
                    (first * sin + second * cos).astype(BF16),
                    mask,
                ],
                axis=0,
            )

        return keys, scaled(x, r)

    for i in range(2):
        frame = meta[2 + i]
        rows = pl.ds(pl.multiple_of((frame % BF) * FT, FT), FT)
        x = features(frame // BF)
        own_ref[...] = x.T
        tokens_ref[pl.ds(i * FT, FT), :] = dot(own_ref[rows, :], pw_ref[...]).astype(BF16)
        own_ref[...] = scaled(x, norm(x, dot(mg_ref[HEADS * HD :], x)))
        own = own_ref[rows, :]
        lane = lax.broadcasted_iota(jnp.int32, (FT, ROWS - 128), 1)
        select = (lane == i).astype(F32).astype(BF16)
        for h in range(HEADS):
            pre = dot(own, mq_ref[:, pl.ds(h * HD, HD)])
            rotated = pre * cq_ref[i] + pltpu.roll(pre, 64, 1) * sq_ref[i]
            q_ref[i, h] = jnp.concatenate([rotated.astype(BF16), select], axis=1)

    u_ref[...] = jnp.zeros_like(u_ref)

    def visit(frames, b, carry):
        keys, av = prepare(b)
        for h in range(HEADS):
            q = jnp.concatenate([q_ref[i, h] for i in frames], axis=0)
            w = jnp.exp2(dot(q, keys(h))).astype(BF16)
            for n, i in enumerate(frames):
                w_ref[i, pl.ds(h * FT, FT)] = w[n * FT : (n + 1) * FT]
        for i in frames:
            u_ref[i] += dot(w_ref[i], av)
        return carry

    lax.fori_loop(0, blocks_early, functools.partial(visit, (0, 1)), 0)
    lax.fori_loop(blocks_early, blocks_late, functools.partial(visit, (1,)), 0)

    total = u_ref[:, :, 129:130]
    good = jnp.where((total >= LOW) & (total <= HIGH), 1.0, 0.0)
    bad = jnp.min(good) < 0.5

    @pl.when(bad)
    def _():
        u_ref[...] = jnp.zeros_like(u_ref)
        m_ref[...] = jnp.full_like(m_ref, FAR)

        def visit_again(b, carry):
            keys, av = prepare(b)
            for h in range(HEADS):
                k = keys(h)
                rows = pl.ds(h * FT, FT)
                for i in range(2):
                    s = dot(q_ref[i, h], k)
                    old = m_ref[i, rows]
                    new = jnp.maximum(old, jnp.max(s, axis=1, keepdims=True))
                    w = jnp.exp2(s - new).astype(BF16)
                    u_ref[i, rows] = u_ref[i, rows] * jnp.exp2(old - new) + dot(w, av)
                    m_ref[i, rows] = new
            return carry

        lax.fori_loop(0, blocks_late, visit_again, 0)

    for i in range(2):
        for h in range(HEADS):
            u = u_ref[i, pl.ds(h * FT, FT)]
            mixed = (u / u[:, 129:130]).astype(BF16)
            ho_ref[pl.ds(i * FT, FT), pl.ds(h * HD, HD)] = dot(
                mixed, mv_ref[:, pl.ds(h * HD, HD)]
            ).astype(BF16)
    out_copy.wait()
    for n, ref in enumerate(outs):
        group = (chip ^ (n // 2)) * 2 + (core ^ (n % 2))
        columns = pl.ds(pl.multiple_of(group * 768, 768), 768)
        ref[...] = dot(ho_ref[...], wide_ref[:, columns]).astype(BF16)


def attention(meta, *arrays):
    vmem = pl.BlockSpec(memory_space=pltpu.VMEM)
    hbm = pl.BlockSpec(memory_space=pl.ANY)
    shape = jax.ShapeDtypeStruct((2 * FT, 768), BF16)
    return pl.pallas_call(
        kernel,
        in_specs=[pl.BlockSpec(memory_space=pltpu.SMEM)] + [hbm] * 8 + [vmem] * 10 + [hbm],
        out_specs=(vmem,) * 5,
        out_shape=(shape,) * 5,
        scratch_shapes=[
            pltpu.VMEM((NB, 64, BK), BF16),
            pltpu.VMEM((768, 3072), BF16),
            pltpu.VMEM((BK, ROWS), BF16),
            pltpu.VMEM((2, HEADS, FT, ROWS), BF16),
            pltpu.VMEM((2, HEADS * FT, BK), BF16),
            pltpu.VMEM((2, HEADS * FT, ROWS), F32),
            pltpu.VMEM((2 * FT, HEADS * HD), BF16),
            pltpu.VMEM((2, HEADS * FT, 1), F32),
            pltpu.SemaphoreType.DMA((32,)),
            pltpu.SemaphoreType.DMA,
        ],
        compiler_params=pltpu.CompilerParams(vmem_limit_bytes=56 * 2**20),
    )(meta, *arrays)


def permute(x, axis, to):
    return lax.ppermute(x, axis, [(i, to(i)) for i in range(lax.axis_size(axis))])


def weights_kernel(me, p0, p1, p2, p3, gain, wq, wk, wv, mg_ref, mq_ref, mv_ref, aq, ak, av, ag):
    k = pl.program_id(0)

    @pl.when(k == 0)
    def _():
        for ref in (aq, ak, av, ag):
            ref[...] = jnp.zeros_like(ref)

    part = jnp.where(k < 2, jnp.where(k == 0, p0[...], p1[...]), jnp.where(k == 2, p2[...], p3[...]))
    wide = part.astype(F32)
    bias = wide[128:129] + wide[129:130] + wide[130:131]
    row = lax.broadcasted_iota(jnp.int32, (ROWS - 128, part.shape[1]), 0)
    gained = jnp.concatenate([wide[:128], jnp.where(row == 0, bias, 0.0)], axis=0) * gain[0]
    gained = gained.astype(BF16)
    aq[...] += dot(gained, wq[...])
    ak[...] += dot(gained, wk[...])
    av[...] += dot(gained, wv[...])
    ag[...] += lax.dot_general(part, part, (((1,), (1,)), ((), ())), preferred_element_type=F32)

    @pl.when(k == 3)
    def _():
        mq_ref[...] = aq[...].astype(BF16)
        mv_ref[...] = av[...].astype(BF16)
        mg_ref[: HEADS * HD, :] = ak[...].T.astype(BF16)
        gram = ag[...] * (1.0 / (4 * part.shape[1]))
        high = gram.astype(BF16)
        mg_ref[HEADS * HD : HEADS * HD + ROWS, :] = high
        mg_ref[HEADS * HD + ROWS :, :] = (gram - high.astype(F32)).astype(BF16)


def through(parts, gain, wq, wk, wv):
    columns = HEADS * HD
    whole = lambda *shape: pl.BlockSpec(shape, lambda k, me: (0,) * len(shape))
    source = lambda k, me: (me[0] + 4 - k) % 4
    weight = pl.BlockSpec((columns, columns), lambda k, me: (source(k, me), 0))
    return pl.pallas_call(
        weights_kernel,
        grid_spec=pltpu.PrefetchScalarGridSpec(
            num_scalar_prefetch=1,
            grid=(4,),
            in_specs=[whole(ROWS, columns)] * 4
            + [pl.BlockSpec((1, 1, columns), lambda k, me: (source(k, me), 0, 0))]
            + [weight] * 3,
            out_specs=[
                whole(columns + 2 * ROWS, ROWS),
                whole(ROWS, columns),
                whole(ROWS, columns),
            ],
            scratch_shapes=[pltpu.VMEM((ROWS, columns), F32)] * 3 + [pltpu.VMEM((ROWS, ROWS), F32)],
        ),
        out_shape=[
            jax.ShapeDtypeStruct((columns + 2 * ROWS, ROWS), BF16),
            jax.ShapeDtypeStruct((ROWS, columns), BF16),
            jax.ShapeDtypeStruct((ROWS, columns), BF16),
        ],
        compiler_params=pltpu.CompilerParams(vmem_limit_bytes=24 * 2**20),
        cost_estimate=pl.CostEstimate(
            flops=2 * ROWS * 3072 * 2400, bytes_accessed=3 * 3072 * 768 * 2, transcendentals=0
        ),
    )(lax.axis_index("head").astype(jnp.int32).reshape(1), *parts, gain.reshape(4, 1, columns), wq, wk, wv)


def join_kernel(z, p0, p1, p2, p3, out):
    for place in range(4):
        k = (z[0] + 4 - place) % 4
        part = jnp.where(k < 2, jnp.where(k == 0, p0[...], p1[...]), jnp.where(k == 2, p2[...], p3[...]))
        out[0, :, place * FT : (place + 1) * FT] = part[:, :FT]
        out[1, :, (3 - place) * FT : (4 - place) * FT] = part[:, FT:]


def join(z, parts):
    vmem = pl.BlockSpec(memory_space=pltpu.VMEM)
    return pl.pallas_call(
        join_kernel,
        in_specs=[pl.BlockSpec(memory_space=pltpu.SMEM)] + [vmem] * 4,
        out_specs=vmem,
        out_shape=jax.ShapeDtypeStruct((2, 32, BK), BF16),
        cost_estimate=pl.CostEstimate(flops=0, bytes_accessed=200000, transcendentals=0),
    )(z.astype(jnp.int32).reshape(1), *parts)


def all_latents(latents):
    seq, core = lax.axis_index("seq"), lax.axis_index("head") % 2

    def place(i):
        return i // 8, (i // 4) % 2, i % 4

    def at(x, y, z):
        return (x * 2 + y) * 4 + z

    def to_y(i):
        x, y, z = place(i)
        return at(x, 1 - y, z)

    def to_z(k, i):
        x, y, z = place(i)
        return at(x, y, (z + k) % 4)

    def to_x(k, i):
        x, y, z = place(i)
        return at((x + k) % 4, y, z)

    half = lax.dynamic_slice_in_dim(latents, core * 32, 32, 0)
    parts = [half] + [permute(half, "seq", functools.partial(to_z, k)) for k in (1, 2, 3)]
    block = join(seq % 4, parts)
    pair = jnp.stack([block, permute(block, "seq", to_y)])
    pieces = []
    for k in range(4):
        part = permute(pair, "seq", functools.partial(to_x, k)) if k else pair
        pieces += [part, permute(part, "head", lambda i: i ^ 1)]
    return pieces


def add(a, b):
    return a.astype(F32) + b.astype(F32)


def local(
    latents,
    span_ids,
    patch_weight,
    patch_bias,
    norm_gain,
    query_weight,
    key_weight,
    value_weight,
    out_weight,
):
    seq = lax.axis_index("seq")
    frames = jnp.stack([seq, FRAMES - 1 - seq]).astype(jnp.int32)
    own_span = jnp.sum(jnp.where(frames[:, None] == jnp.arange(FRAMES)[None], span_ids[None], 0), axis=1)
    ends = jnp.sum((span_ids[None, :] <= own_span[:, None]).astype(jnp.int32), axis=1)
    head = lax.axis_index("head")
    places = jnp.stack([seq // 8, (seq // 4) % 2, head % 2, head // 2]).astype(jnp.int32)
    meta = jnp.concatenate([ends, frames, places])

    pieces = all_latents(latents)

    b0 = patch_bias.astype(BF16)
    b1 = (patch_bias - b0.astype(F32)).astype(BF16)
    b2 = (patch_bias - b0.astype(F32) - b1.astype(F32)).astype(BF16)
    rest = jnp.zeros((ROWS - 131, patch_bias.shape[0]), BF16)
    wide = jnp.concatenate([patch_weight, b0[None], b1[None], b2[None], rest], axis=0)
    parts = [wide] + [permute(wide, "head", lambda i, k=k: (i + k) % 4) for k in (1, 2, 3)]
    mg, mq, mv = through(parts, norm_gain, query_weight, key_weight, value_weight)

    w_t, _, _ = frequencies()
    spatial = spatial_angles()
    cs = jnp.asarray(np.tile(np.cos(spatial).T, (1, BF)), F32)
    ss = jnp.asarray(np.tile(np.sin(spatial).T, (1, BF)), F32)
    temporal = np.outer(np.arange(FRAMES), w_t)
    by_block = np.repeat(temporal.reshape(NB, BF, 16).transpose(0, 2, 1), FT, axis=2)
    ct = jnp.asarray(np.cos(by_block), F32)
    st = jnp.asarray(np.sin(by_block), F32)
    angle = frames.astype(F32)[:, None] * jnp.asarray(w_t, F32)[None]

    def of_queries(turn, space):
        own = jnp.broadcast_to(turn[:, None, :], (2, FT, 16))
        return jnp.concatenate([own, jnp.broadcast_to(jnp.asarray(space, F32)[None], (2, FT, 48))], axis=2) * SCALE

    cq = of_queries(jnp.cos(angle), np.cos(spatial))
    sq = of_queries(jnp.sin(angle), np.sin(spatial))
    cq = jnp.concatenate([cq, cq], axis=2)
    sq = jnp.concatenate([-sq, sq], axis=2)

    near, near_other, far, far_other, tokens = attention(
        meta, *pieces, mg, mq, mv, wide, cs, ss, ct, st, cq, sq, out_weight
    )
    swap = lambda x, bit: permute(x, "head", lambda i: i ^ bit)
    sent = swap(add(far, swap(far_other, 1)).astype(BF16), 2)
    kept = add(near, swap(near_other, 1)).astype(BF16)
    return (add(kept, sent) + tokens.astype(F32)).astype(BF16)


def solution(mesh):
    return jax.shard_map(
        local,
        mesh=mesh,
        in_specs=(
            P(None, "seq"),
            P(),
            P(None, "head"),
            P("head"),
            P(),
            P(None, "head"),
            P(None, "head"),
            P(None, "head"),
            P("head", None),
        ),
        out_specs=P("seq", "head"),
        check_vma=False,
    )
```

time: 234 us -> 191 us (0.82)
  local copies, waits for them, and re-layouts: 27.6 us -> 13.3 us
  matrix products: 12.9 us -> 0 us
  Pallas kernels: 133 us -> 122 us
  other arithmetic: 14.9 us -> 6.83 us
  waiting for transfers between devices: 25.7 us -> 30.1 us
    pallas_call x1, Pallas kernels: 133 us -> 117 us  [attention(): pl.pallas_call(kernel, in_specs=[pl.BlockSpec(memory_space=pltpu.SMEM)] +...]
    dot_general x5 -> x0, matrix products: 12.9 us -> none  [the longest x2 5.72 us: dot(): return jnp.dot(a, b, preferred_element_type=F32)]
    pallas_call x0 -> x2, Pallas kernels: none -> 5.14 us  [the longest x1 3.55 us: through(): pl.pallas_call(weights_kernel, grid_spec=pltpu.PrefetchScalarGridSpec(num...]
    concatenate x1, local copies, waits for them, and re-layouts: 5.5 us -> 0.61 us  [local(): meta = jnp.concatenate([ends, frames, places])]
    ppermute x13 -> x17, waiting for transfers between devices: 25.7 us -> 30.1 us  [permute(): lax.ppermute(x, axis, [(i, to(i)) for i in range(lax.axis_size(axis))])]
    concatenate x3 -> x0, other arithmetic: 3.75 us -> none  [the longest x1 2.64 us: local(): patches = jnp.concatenate([before, natural], axis=1)]
    squeeze x3 -> x0, local copies, waits for them, and re-layouts: 3.54 us -> none  [the longest x1 2.54 us: sum_scatter(): lax.dynamic_index_in_dim(pairs, 1 - core, 1, False)]
    reshape x1 -> x0, local copies, waits for them, and re-layouts: 2.83 us -> none  [local(): patches.reshape(NB, BF, 128, FT).transpose(0, 2, 1, 3).reshape(NB, 128, BK)]
  transfers between devices with their start and end apart: 13 -> 17, of which waited for: 6 -> 5; matrix products, arithmetic and copies ran while one was open for 13% -> 4% of each run, Pallas kernels for 0% -> 3%
where the time goes in v2:
time: 191 us
  Pallas kernels  122 us (64%)
  waiting for transfers between devices  30.1 us (16%)
  starting transfers between devices  18.4 us (10%)
  local copies, waits for them, and re-layouts  13.3 us (7%)
  other arithmetic  6.83 us (4%)
    pallas_call x1, Pallas kernels, attention(): pl.pallas_call(kernel, in_specs=[pl.BlockSpec(memory_space=pltpu.SMEM)] +...  117 us
    ppermute x17, waiting for transfers between devices, permute(): lax.ppermute(x, axis, [(i, to(i)) for i in range(lax.axis_size(axis))])  30.1 us
    ppermute x17, starting transfers between devices, permute(): lax.ppermute(x, axis, [(i, to(i)) for i in range(lax.axis_size(axis))])  18.4 us
    unnamed x52, local copies, waits for them, and re-layouts  11.5 us
  transfers between devices with their start and end apart: 17, of which 5 were waited for; matrix products, arithmetic and copies ran while one was open for 4% of the time, Pallas kernels for 3%

profile of v2, /device:TPU:1, one launch (start us, length us, event | category | flops | bytes accessed | tf_op | source)
XLA Modules:
  0.0 191.2 jit_solution(2602856597295863934)
XLA Ops:
  0.0 0.8 copy-done
  0.8 4.6 %collective-permute-start.2 = (bf16[32,384]{1,0:T(8,128)(2,1)S(1)}, bf16[32,384]{1,0:T(8,128)(2,1)S(1)}, u32[]{:S(2)}, u32[]{:S(2)}) collective-permute-start(bf16[32,384]{1,0:T(8,128)(2,1)S(1)} %constant_dynamic-slice_fusion.p0), channel_id=1, source_target_pairs={{0,12},{4,0},{8,4},{12,8},{16,28},{20,16},{24,20},{28,24},{32,44},... | collective-permute-start | bytes 73736 | tf_op jit(solution)/shard_map/ppermute | solution.py:227
  5.4 0.7 collective-permute-start
  6.1 0.8 subtract_convert_fusion
  6.9 1.1 concatenate.24.p0.refs_11_
  8.1 1.6 collective-permute-start.13
  9.7 1.3 collective-permute-start.12
  11.0 0.1 fusion.4
  11.0 0.8 fusion.2
  11.9 0.8 multiply_sine_fusion
  12.6 0.8 fusion.3
  13.5 0.6 concatenate.23.meta
  14.1 0.5 collective-permute-start.11
  14.7 0.1 copy-done.23
  14.8 0.5 copy-done.24
  15.3 1.6 shard_map.154
  16.9 2.8 %collective-permute-start.3 = (bf16[2,32,768]{2,1,0:T(8,128)(2,1)}, bf16[2,32,768]{2,1,0:T(8,128)(2,1)S(1)}, u32[]{:S(2)}, u32[]{:S(2)}) collective-permute-start(bf16[2,32,768]{2,1,0:T(8,128)(2,1)} %shard_map.154), channel_id=1, source_target_pairs={{0,16},{4,20},{8,24},{12,28},{16,0},{20,4},{24,8},{28,12},{32,48},... | collective-permute-start | bytes 294920 | tf_op jit(solution)/shard_map/ppermute | solution.py:227
  19.7 0.1 fusion
  19.9 5.4 %collective-permute-done.3 = bf16[2,32,768]{2,1,0:T(8,128)(2,1)S(1)} collective-permute-done((bf16[2,32,768]{2,1,0:T(8,128)(2,1)}, bf16[2,32,768]{2,1,0:T(8,128)(2,1)S(1)}, u32[]{:S(2)}, u32[]{:S(2)}) %collective-permute-start.3) | collective-permute-done | bytes 98336 | tf_op jit(solution)/shard_map/ppermute | solution.py:227
  25.3 2.5 %collective-permute-start.9 = (bf16[2,2,32,768]{3,2,1,0:T(8,128)(2,1)S(1)}, bf16[2,2,32,768]{3,2,1,0:T(8,128)(2,1)S(1)}, u32[]{:S(2)}, u32[]{:S(2)}) collective-permute-start(bf16[2,2,32,768]{3,2,1,0:T(8,128)(2,1)S(1)} %pad_maximum_fusion.refs_0_), channel_id=1, source_target_pairs={{0,96},{4,100},{8,104},{12,108},{16,112},{20,116},{24,120},{28,124... | collective-permute-start | bytes 589832 | tf_op jit(solution)/shard_map/ppermute | solution.py:227
  27.9 0.5 collective-permute-start.7
  28.4 0.6 collective-permute-start.5
  29.1 0.1 maximum_multiply_fusion
  29.2 0.9 pad_maximum_fusion.1
  30.1 0.7 collective-permute-start.4
  30.8 5.5 %collective-permute-done.9.refs_6_ = bf16[2,2,32,768]{3,2,1,0:T(8,128)(2,1)S(1)} collective-permute-done((bf16[2,2,32,768]{3,2,1,0:T(8,128)(2,1)S(1)}, bf16[2,2,32,768]{3,2,1,0:T(8,128)(2,1)S(1)}, u32[]{:S(2)}, u32[]{:S(2)}) %collective-permute-start.9) | collective-permute-done | bytes 196640 | tf_op jit(solution)/shard_map/ppermute | solution.py:227
  36.3 0.9 collective-permute-start.10
  37.2 0.1 collective-permute-start.8
  37.3 3.1 %collective-permute-done.5.refs_2_ = bf16[2,2,32,768]{3,2,1,0:T(8,128)(2,1)S(1)} collective-permute-done((bf16[2,2,32,768]{3,2,1,0:T(8,128)(2,1)S(1)}, bf16[2,2,32,768]{3,2,1,0:T(8,128)(2,1)S(1)}, u32[]{:S(2)}, u32[]{:S(2)}) %collective-permute-start.5) | collective-permute-done | bytes 196640 | tf_op jit(solution)/shard_map/ppermute | solution.py:227
  40.4 0.5 collective-permute-start.6
  40.9 2.3 %copy-done.1 = bf16[3072,768]{1,0:T(8,128)(2,1)S(1)} copy-done((bf16[3072,768]{1,0:T(8,128)(2,1)S(1)}, bf16[3072,768]{1,0:T(8,128)(2,1)}, u32[]{:S(2)}) %copy-start.1) | copy-done | bytes 4718616
  43.3 2.3 %copy-done.2 = bf16[3072,768]{1,0:T(8,128)(2,1)S(1)} copy-done((bf16[3072,768]{1,0:T(8,128)(2,1)S(1)}, bf16[3072,768]{1,0:T(8,128)(2,1)}, u32[]{:S(2)}) %copy-start.2) | copy-done | bytes 4718616
  45.6 2.3 %copy-done.3 = bf16[3072,768]{1,0:T(8,128)(2,1)S(1)} copy-done((bf16[3072,768]{1,0:T(8,128)(2,1)S(1)}, bf16[3072,768]{1,0:T(8,128)(2,1)}, u32[]{:S(2)}) %copy-start.3) | copy-done | bytes 4718616
  47.9 3.5 %shard_map.155 = (bf16[1056,144]{1,0:T(8,128)(2,1)S(1)}, bf16[144,768]{1,0:T(8,128)(2,1)S(1)}, bf16[144,768]{1,0:T(8,128)(2,1)S(1)}) custom-call(s32[1]{0:T(128)} %bitcast.9.me, bf16[144,768]{1,0:T(8,128)(2,1)S(1)} %concatenate.24.p0.refs_11_, bf16[144,768]{1,0:T(8,128)(2,1)S(1)} %collective-permute-done.11.p1, ...), custom_call_target="tpu_custom_call" | custom-call | flops 2123366400 | bytes 14155776 | tf_op jit(solution)/shard_map/pallas_call | solution.py:265
  51.5 0.8 copy-done.5
  52.3 0.7 copy-done.6
  53.0 0.7 copy-done.7
  53.8 0.6 copy-done.16
  54.4 0.1 copy-done.17
  54.6 0.1 copy-done.19
  54.7 117.0 %shard_map.156 = (bf16[384,768]{1,0:T(8,128)(2,1)}, bf16[384,768]{1,0:T(8,128)(2,1)}, bf16[384,768]{1,0:T(8,128)(2,1)}, bf16[384,768]{1,0:T(8,128)(2,1)}, bf16[384,768]{1,0:T(8,128)(2,1)}) custom-call(s32[8]{0:T(128)} %concatenate.23.meta, bf16[2,2,32,768]{3,2,1,0:T(8,128)(2,1)} %copy-done.9, bf16[2,2,32,768]{3,2,1,0:T(8,128)(2,1)} %copy-done.16, ...), custom_call_target="tpu_custom_call" | custom-call | tf_op jit(solution)/shard_map/pallas_call | solution.py:205
  171.7 0.2 collective-permute-start.15
  171.9 0.4 collective-permute-start.14
  172.3 1.7 collective-permute-done.15
  174.0 1.2 add_convert_fusion.1
  175.2 0.5 collective-permute-start.16
  175.7 14.4 %collective-permute-done.16 = bf16[384,768]{1,0:T(8,128)(2,1)S(1)} collective-permute-done((bf16[384,768]{1,0:T(8,128)(2,1)S(1)}, bf16[384,768]{1,0:T(8,128)(2,1)S(1)}, u32[]{:S(2)}, u32[]{:S(2)}) %collective-permute-start.16) | collective-permute-done | bytes 589856 | tf_op jit(solution)/shard_map/ppermute | solution.py:227
  190.1 1.1 add_convert_fusion
  (63 shorter events, 0.3 us)
Async XLA Ops:
  0.0 0.8 copy-start
  0.0 19.7 %copy-start.22 = (f32[192,48]{1,0:T(8,128)S(1)}, f32[192,48]{1,0:T(8,128)}, u32[]{:S(2)}) copy-start(f32[192,48]{1,0:T(8,128)} %constant.98.clone) | copy-start | bytes 110596
  0.8 13.9 %copy-start.20 = (bf16[32,384]{1,0:T(8,128)(2,1)}, bf16[32,384]{1,0:T(8,128)(2,1)S(1)}, u32[]{:S(2)}) copy-start(bf16[32,384]{1,0:T(8,128)(2,1)S(1)} %constant_dynamic-slice_fusion.p0) | copy-start | bytes 73732
  0.8 13.3 %collective-permute-start.2 = (bf16[32,384]{1,0:T(8,128)(2,1)S(1)}, bf16[32,384]{1,0:T(8,128)(2,1)S(1)}, u32[]{:S(2)}, u32[]{:S(2)}) collective-permute-start(bf16[32,384]{1,0:T(8,128)(2,1)S(1)} %constant_dynamic-slice_fusion.p0), channel_id=1, source_target_pairs={{0,12},{4,0},{8,4},{12,8},{16,28},{20,16},{24,20},{28,24},{32,44},... | collective-permute-start | bytes 73736 | tf_op jit(solution)/shard_map/ppermute | solution.py:227
  5.4 9.3 %collective-permute-start.1 = (bf16[32,384]{1,0:T(8,128)(2,1)S(1)}, bf16[32,384]{1,0:T(8,128)(2,1)S(1)}, u32[]{:S(2)}, u32[]{:S(2)}) collective-permute-start(bf16[32,384]{1,0:T(8,128)(2,1)S(1)} %constant_dynamic-slice_fusion.p0), channel_id=1, source_target_pairs={{0,8},{4,12},{8,0},{12,4},{16,24},{20,28},{24,16},{28,20},{32,40},... | collective-permute-start | bytes 73736 | tf_op jit(solution)/shard_map/ppermute | solution.py:227
  5.4 9.3 %collective-permute-start = (bf16[32,384]{1,0:T(8,128)(2,1)S(1)}, bf16[32,384]{1,0:T(8,128)(2,1)S(1)}, u32[]{:S(2)}, u32[]{:S(2)}) collective-permute-start(bf16[32,384]{1,0:T(8,128)(2,1)S(1)} %constant_dynamic-slice_fusion.p0), channel_id=1, source_target_pairs={{0,4},{4,8},{8,12},{12,0},{16,20},{20,24},{24,28},{28,16},{32,36},... | collective-permute-start | bytes 73736 | tf_op jit(solution)/shard_map/ppermute | solution.py:227
  8.0 32.9 %copy-start.4 = (bf16[144,768]{1,0:T(8,128)(2,1)}, bf16[144,768]{1,0:T(8,128)(2,1)S(1)}, u32[]{:S(2)}) copy-start(bf16[144,768]{1,0:T(8,128)(2,1)S(1)} %concatenate.24.p0.refs_11_) | copy-start | bytes 663556
  8.1 21.0 %copy-start.21 = (f32[192,48]{1,0:T(8,128)S(1)}, f32[192,48]{1,0:T(8,128)}, u32[]{:S(2)}) copy-start(f32[192,48]{1,0:T(8,128)} %constant.97.clone) | copy-start | bytes 110596
  8.1 20.3 %collective-permute-start.13 = (bf16[144,768]{1,0:T(8,128)(2,1)S(1)}, bf16[144,768]{1,0:T(8,128)(2,1)S(1)}, u32[]{:S(2)}, u32[]{:S(2)}) collective-permute-start(bf16[144,768]{1,0:T(8,128)(2,1)S(1)} %concatenate.24.p0.refs_11_), channel_id=1, source_target_pairs={{0,3},{1,0},{2,1},{3,2},{4,7},{5,4},{6,5},{7,6},{8,11},{9,8},{10,9... | collective-permute-start | bytes 663560 | tf_op jit(solution)/shard_map/ppermute | solution.py:227
  9.7 20.5 %collective-permute-start.12 = (bf16[144,768]{1,0:T(8,128)(2,1)S(1)}, bf16[144,768]{1,0:T(8,128)(2,1)S(1)}, u32[]{:S(2)}, u32[]{:S(2)}) collective-permute-start(bf16[144,768]{1,0:T(8,128)(2,1)S(1)} %concatenate.24.p0.refs_11_), channel_id=1, source_target_pairs={{0,2},{1,3},{2,0},{3,1},{4,6},{5,7},{6,4},{7,5},{8,10},{9,11},{10,... | collective-permute-start | bytes 663560 | tf_op jit(solution)/shard_map/ppermute | solution.py:227
  14.1 0.6 copy-start.23
  14.1 26.8 %collective-permute-start.11 = (bf16[144,768]{1,0:T(8,128)(2,1)S(1)}, bf16[144,768]{1,0:T(8,128)(2,1)S(1)}, u32[]{:S(2)}, u32[]{:S(2)}) collective-permute-start(bf16[144,768]{1,0:T(8,128)(2,1)S(1)} %concatenate.24.p0.refs_11_), channel_id=1, source_target_pairs={{0,1},{1,2},{2,3},{3,0},{4,5},{5,6},{6,7},{7,4},{8,9},{9,10},{10,1... | collective-permute-start | bytes 663560 | tf_op jit(solution)/shard_map/ppermute | solution.py:227
  14.6 0.6 copy-start.24
  14.7 0.6 copy-start.25
  16.9 8.4 %copy-start.12 = (bf16[2,32,768]{2,1,0:T(8,128)(2,1)S(1)}, bf16[2,32,768]{2,1,0:T(8,128)(2,1)}, u32[]{:S(2)}) copy-start(bf16[2,32,768]{2,1,0:T(8,128)(2,1)} %shard_map.154) | copy-start | bytes 294916
  16.9 8.4 %collective-permute-start.3 = (bf16[2,32,768]{2,1,0:T(8,128)(2,1)}, bf16[2,32,768]{2,1,0:T(8,128)(2,1)S(1)}, u32[]{:S(2)}, u32[]{:S(2)}) collective-permute-start(bf16[2,32,768]{2,1,0:T(8,128)(2,1)} %shard_map.154), channel_id=1, source_target_pairs={{0,16},{4,20},{8,24},{12,28},{16,0},{20,4},{24,8},{28,12},{32,48},... | collective-permute-start | bytes 294920 | tf_op jit(solution)/shard_map/ppermute | solution.py:227
  25.3 15.6 %copy-start.8 = (f32[3072]{0:T(1024)S(1)}, f32[3072]{0:T(1024)}, u32[]{:S(2)}) copy-start(f32[3072]{0:T(1024)} %param.20) | copy-start | bytes 36868
  25.3 26.2 %copy-start.9 = (bf16[2,2,32,768]{3,2,1,0:T(8,128)(2,1)}, bf16[2,2,32,768]{3,2,1,0:T(8,128)(2,1)S(1)}, u32[]{:S(2)}) copy-start(bf16[2,2,32,768]{3,2,1,0:T(8,128)(2,1)S(1)} %pad_maximum_fusion.refs_0_) | copy-start | bytes 589828
  25.3 11.0 %collective-permute-start.9 = (bf16[2,2,32,768]{3,2,1,0:T(8,128)(2,1)S(1)}, bf16[2,2,32,768]{3,2,1,0:T(8,128)(2,1)S(1)}, u32[]{:S(2)}, u32[]{:S(2)}) collective-permute-start(bf16[2,2,32,768]{3,2,1,0:T(8,128)(2,1)S(1)} %pad_maximum_fusion.refs_0_), channel_id=1, source_target_pairs={{0,96},{4,100},{8,104},{12,108},{16,112},{20,116},{24,120},{28,124... | collective-permute-start | bytes 589832 | tf_op jit(solution)/shard_map/ppermute | solution.py:227
  27.9 9.4 %collective-permute-start.7 = (bf16[2,2,32,768]{3,2,1,0:T(8,128)(2,1)S(1)}, bf16[2,2,32,768]{3,2,1,0:T(8,128)(2,1)S(1)}, u32[]{:S(2)}, u32[]{:S(2)}) collective-permute-start(bf16[2,2,32,768]{3,2,1,0:T(8,128)(2,1)S(1)} %pad_maximum_fusion.refs_0_), channel_id=1, source_target_pairs={{0,64},{4,68},{8,72},{12,76},{16,80},{20,84},{24,88},{28,92},{32,9... | collective-permute-start | bytes 589832 | tf_op jit(solution)/shard_map/ppermute | solution.py:227
  28.4 12.0 %collective-permute-start.5 = (bf16[2,2,32,768]{3,2,1,0:T(8,128)(2,1)S(1)}, bf16[2,2,32,768]{3,2,1,0:T(8,128)(2,1)S(1)}, u32[]{:S(2)}, u32[]{:S(2)}) collective-permute-start(bf16[2,2,32,768]{3,2,1,0:T(8,128)(2,1)S(1)} %pad_maximum_fusion.refs_0_), channel_id=1, source_target_pairs={{0,32},{4,36},{8,40},{12,44},{16,48},{20,52},{24,56},{28,60},{32,6... | collective-permute-start | bytes 589832 | tf_op jit(solution)/shard_map/ppermute | solution.py:227
  30.1 23.6 %collective-permute-start.4 = (bf16[2,2,32,768]{3,2,1,0:T(8,128)(2,1)S(1)}, bf16[2,2,32,768]{3,2,1,0:T(8,128)(2,1)S(1)}, u32[]{:S(2)}, u32[]{:S(2)}) collective-permute-start(bf16[2,2,32,768]{3,2,1,0:T(8,128)(2,1)S(1)} %pad_maximum_fusion.refs_0_), channel_id=1, source_target_pairs={{0,1},{1,0},{2,3},{3,2},{4,5},{5,4},{6,7},{7,6},{8,9},{9,8},{10,11... | collective-permute-start | bytes 589832 | tf_op jit(solution)/shard_map/ppermute | solution.py:227
  36.3 15.2 %copy-start.13 = (bf16[2,2,32,768]{3,2,1,0:T(8,128)(2,1)}, bf16[2,2,32,768]{3,2,1,0:T(8,128)(2,1)S(1)}, u32[]{:S(2)}) copy-start(bf16[2,2,32,768]{3,2,1,0:T(8,128)(2,1)S(1)} %collective-permute-done.9.refs_6_) | copy-start | bytes 589828
  36.3 17.4 %collective-permute-start.10 = (bf16[2,2,32,768]{3,2,1,0:T(8,128)(2,1)S(1)}, bf16[2,2,32,768]{3,2,1,0:T(8,128)(2,1)S(1)}, u32[]{:S(2)}, u32[]{:S(2)}) collective-permute-start(bf16[2,2,32,768]{3,2,1,0:T(8,128)(2,1)S(1)} %collective-permute-done.9.refs_6_), channel_id=1, source_target_pairs={{0,1},{1,0},{2,3},{3,2},{4,5},{5,4},{6,7},{7,6},{8,9},{9,8},{10,11... | collective-permute-start | bytes 589832 | tf_op jit(solution)/shard_map/ppermute | solution.py:227
  37.2 14.3 %copy-start.14 = (bf16[2,2,32,768]{3,2,1,0:T(8,128)(2,1)}, bf16[2,2,32,768]{3,2,1,0:T(8,128)(2,1)S(1)}, u32[]{:S(2)}) copy-start(bf16[2,2,32,768]{3,2,1,0:T(8,128)(2,1)S(1)} %collective-permute-done.7.refs_4_) | copy-start | bytes 589828
  37.2 16.5 %collective-permute-start.8 = (bf16[2,2,32,768]{3,2,1,0:T(8,128)(2,1)S(1)}, bf16[2,2,32,768]{3,2,1,0:T(8,128)(2,1)S(1)}, u32[]{:S(2)}, u32[]{:S(2)}) collective-permute-start(bf16[2,2,32,768]{3,2,1,0:T(8,128)(2,1)S(1)} %collective-permute-done.7.refs_4_), channel_id=1, source_target_pairs={{0,1},{1,0},{2,3},{3,2},{4,5},{5,4},{6,7},{7,6},{8,9},{9,8},{10,11... | collective-permute-start | bytes 589832 | tf_op jit(solution)/shard_map/ppermute | solution.py:227
  40.4 11.1 %copy-start.15 = (bf16[2,2,32,768]{3,2,1,0:T(8,128)(2,1)}, bf16[2,2,32,768]{3,2,1,0:T(8,128)(2,1)S(1)}, u32[]{:S(2)}) copy-start(bf16[2,2,32,768]{3,2,1,0:T(8,128)(2,1)S(1)} %collective-permute-done.5.refs_2_) | copy-start | bytes 589828
  40.4 13.3 %collective-permute-start.6 = (bf16[2,2,32,768]{3,2,1,0:T(8,128)(2,1)S(1)}, bf16[2,2,32,768]{3,2,1,0:T(8,128)(2,1)S(1)}, u32[]{:S(2)}, u32[]{:S(2)}) collective-permute-start(bf16[2,2,32,768]{3,2,1,0:T(8,128)(2,1)S(1)} %collective-permute-done.5.refs_2_), channel_id=1, source_target_pairs={{0,1},{1,0},{2,3},{3,2},{4,5},{5,4},{6,7},{7,6},{8,9},{9,8},{10,11... | collective-permute-start | bytes 589832 | tf_op jit(solution)/shard_map/ppermute | solution.py:227
  40.9 2.3 %copy-start.1 = (bf16[3072,768]{1,0:T(8,128)(2,1)S(1)}, bf16[3072,768]{1,0:T(8,128)(2,1)}, u32[]{:S(2)}) copy-start(bf16[3072,768]{1,0:T(8,128)(2,1)} %wq.1) | copy-start | bytes 14155780
  43.3 2.3 %copy-start.2 = (bf16[3072,768]{1,0:T(8,128)(2,1)S(1)}, bf16[3072,768]{1,0:T(8,128)(2,1)}, u32[]{:S(2)}) copy-start(bf16[3072,768]{1,0:T(8,128)(2,1)} %wk.1) | copy-start | bytes 14155780
  45.6 2.3 %copy-start.3 = (bf16[3072,768]{1,0:T(8,128)(2,1)S(1)}, bf16[3072,768]{1,0:T(8,128)(2,1)}, u32[]{:S(2)}) copy-start(bf16[3072,768]{1,0:T(8,128)(2,1)} %wv.1) | copy-start | bytes 14155780
  51.5 0.8 copy-start.5
  52.3 0.7 copy-start.6
  53.0 0.7 copy-start.7
  53.7 0.7 copy-start.16
  53.7 0.8 copy-start.17
  53.7 0.8 copy-start.18
  53.8 0.9 copy-start.19
  171.7 18.4 %copy-start.10 = (bf16[384,768]{1,0:T(8,128)(2,1)S(1)}, bf16[384,768]{1,0:T(8,128)(2,1)}, u32[]{:S(2)}) copy-start(bf16[384,768]{1,0:T(8,128)(2,1)} %get-tuple-element.16) | copy-start | bytes 1769476
  171.7 18.4 %copy-start.11 = (bf16[384,768]{1,0:T(8,128)(2,1)S(1)}, bf16[384,768]{1,0:T(8,128)(2,1)}, u32[]{:S(2)}) copy-start(bf16[384,768]{1,0:T(8,128)(2,1)} %get-tuple-element.20) | copy-start | bytes 1769476
  171.7 2.3 %collective-permute-start.15 = (bf16[384,768]{1,0:T(8,128)(2,1)}, bf16[384,768]{1,0:T(8,128)(2,1)S(1)}, u32[]{:S(2)}, u32[]{:S(2)}) collective-permute-start(bf16[384,768]{1,0:T(8,128)(2,1)} %get-tuple-element.19), channel_id=1, source_target_pairs={{0,1},{1,0},{2,3},{3,2},{4,5},{5,4},{6,7},{7,6},{8,9},{9,8},{10,11... | collective-permute-start | bytes 1769480 | tf_op jit(solution)/shard_map/ppermute | solution.py:227
  171.9 3.9 %collective-permute-start.14 = (bf16[384,768]{1,0:T(8,128)(2,1)}, bf16[384,768]{1,0:T(8,128)(2,1)S(1)}, u32[]{:S(2)}, u32[]{:S(2)}) collective-permute-start(bf16[384,768]{1,0:T(8,128)(2,1)} %get-tuple-element.17), channel_id=1, source_target_pairs={{0,1},{1,0},{2,3},{3,2},{4,5},{5,4},{6,7},{7,6},{8,9},{9,8},{10,11... | collective-permute-start | bytes 1769480 | tf_op jit(solution)/shard_map/ppermute | solution.py:227
  175.2 14.9 %collective-permute-start.16 = (bf16[384,768]{1,0:T(8,128)(2,1)S(1)}, bf16[384,768]{1,0:T(8,128)(2,1)S(1)}, u32[]{:S(2)}, u32[]{:S(2)}) collective-permute-start(bf16[384,768]{1,0:T(8,128)(2,1)S(1)} %add_convert_fusion.1), channel_id=1, source_target_pairs={{0,2},{1,3},{2,0},{3,1},{4,6},{5,7},{6,4},{7,5},{8,10},{9,11},{10,... | collective-permute-start | bytes 1769480 | tf_op jit(solution)/shard_map/ppermute | solution.py:227

commit v3 on v2

--- a/solution.py
+++ b/solution.py
@@ -59,14 +59,14 @@
     pieces, refs = refs[:8], refs[8:]
     (mg_ref, mq_ref, mv_ref, pw_ref, cs_ref, ss_ref, ct_ref, st_ref, cq_ref, sq_ref, wo_ref) = refs[:11]
     (outs, tokens_ref), refs = (refs[11:15], refs[15]), refs[16:]
-    raw_ref, wide_ref, own_ref, q_ref, w_ref, u_ref, ho_ref, m_ref, sems, wo_sem = refs
+    raw_ref, own_ref, q_ref, w_ref, u_ref, ho_ref, m_ref, k_ref, v_ref, res_ref, wide_ref, sems, out_sems, wide_sem = refs
     end_early, end_late = meta[0], meta[1]
     blocks_early = (end_early + BF - 1) // BF
     blocks_late = (end_late + BF - 1) // BF
+    wide_copy = pltpu.make_async_copy(wo_ref, wide_ref, wide_sem)
+    wide_copy.start()
     x_at, y_at, core, chip = meta[4], meta[5], meta[6], meta[7]
 
-    out_copy = pltpu.make_async_copy(wo_ref, wide_ref, wo_sem)
-    out_copy.start()
     copies = []
     for k in range(4):
         for c in range(2):
@@ -107,16 +107,19 @@
         return jnp.concatenate([x[:128].astype(F32) * r, tail], axis=0).astype(BF16).T
 
     def prepare(b):
-        x = features(b)
+        inside = jnp.minimum(b, NB - 1)
+        x = features(inside)
         big = dot(mg_ref[...], x)
         r = norm(x, big[HEADS * HD :])
-        cos = jnp.concatenate([ct_ref[b], cs_ref[...]], axis=0) * r
-        sin = jnp.concatenate([st_ref[b], ss_ref[...]], axis=0) * r
+        cos = jnp.concatenate([ct_ref[inside], cs_ref[...]], axis=0) * r
+        sin = jnp.concatenate([st_ref[inside], ss_ref[...]], axis=0) * r
+        cos, sin = cos.astype(BF16), sin.astype(BF16)
         end = jnp.where(row == 0, end_early, end_late)
         mask = jnp.where((row < 2) & (b * BF + lane_frame >= end), FAR, 0.0).astype(BF16)
 
         def keys(h):
             first, second = big[h * HD : h * HD + 64], big[h * HD + 64 : h * HD + HD]
+            first, second = first.astype(BF16), second.astype(BF16)
             return jnp.concatenate(
                 [
                     (first * cos - second * sin).astype(BF16),
@@ -126,14 +129,14 @@
                 axis=0,
             )
 
-        return keys, scaled(x, r)
+        return keys, lambda: scaled(x, r)
 
     for i in range(2):
         frame = meta[2 + i]
         rows = pl.ds(pl.multiple_of((frame % BF) * FT, FT), FT)
         x = features(frame // BF)
         own_ref[...] = x.T
-        tokens_ref[pl.ds(i * FT, FT), :] = dot(own_ref[rows, :], pw_ref[...]).astype(BF16)
+        res_ref[4, pl.ds(i * FT, FT), :] = dot(own_ref[rows, :], pw_ref[...]).astype(BF16)
         own_ref[...] = scaled(x, norm(x, dot(mg_ref[HEADS * HD :], x)))
         own = own_ref[rows, :]
         lane = lax.broadcasted_iota(jnp.int32, (FT, ROWS - 128), 1)
@@ -143,19 +146,30 @@
             rotated = pre * cq_ref[i] + pltpu.roll(pre, 64, 1) * sq_ref[i]
             q_ref[i, h] = jnp.concatenate([rotated.astype(BF16), select], axis=1)
 
+    tokens_copy = pltpu.make_async_copy(res_ref.at[4], tokens_ref, out_sems.at[4])
+    tokens_copy.start()
     u_ref[...] = jnp.zeros_like(u_ref)
 
+    def fill(b):
+        keys, values = prepare(b)
+        for h in range(HEADS):
+            k_ref[h] = keys(h)
+        v_ref[...] = values()
+
     def visit(frames, b, carry):
-        keys, av = prepare(b)
+        keys, values = prepare(b + 1)
         for h in range(HEADS):
             q = jnp.concatenate([q_ref[i, h] for i in frames], axis=0)
-            w = jnp.exp2(dot(q, keys(h))).astype(BF16)
+            w = jnp.exp2(dot(q, k_ref[h])).astype(BF16)
+            k_ref[h] = keys(h)
             for n, i in enumerate(frames):
                 w_ref[i, pl.ds(h * FT, FT)] = w[n * FT : (n + 1) * FT]
         for i in frames:
-            u_ref[i] += dot(w_ref[i], av)
+            u_ref[i] += dot(w_ref[i], v_ref[...])
+        v_ref[...] = values()
         return carry
 
+    fill(0)
     lax.fori_loop(0, blocks_early, functools.partial(visit, (0, 1)), 0)
     lax.fori_loop(blocks_early, blocks_late, functools.partial(visit, (1,)), 0)
 
@@ -169,16 +183,16 @@
         m_ref[...] = jnp.full_like(m_ref, FAR)
 
         def visit_again(b, carry):
-            keys, av = prepare(b)
+            fill(b)
             for h in range(HEADS):
-                k = keys(h)
+                k = k_ref[h]
                 rows = pl.ds(h * FT, FT)
                 for i in range(2):
                     s = dot(q_ref[i, h], k)
                     old = m_ref[i, rows]
                     new = jnp.maximum(old, jnp.max(s, axis=1, keepdims=True))
                     w = jnp.exp2(s - new).astype(BF16)
-                    u_ref[i, rows] = u_ref[i, rows] * jnp.exp2(old - new) + dot(w, av)
+                    u_ref[i, rows] = u_ref[i, rows] * jnp.exp2(old - new) + dot(w, v_ref[...])
                     m_ref[i, rows] = new
             return carry
 
@@ -191,11 +205,16 @@
             ho_ref[pl.ds(i * FT, FT), pl.ds(h * HD, HD)] = dot(
                 mixed, mv_ref[:, pl.ds(h * HD, HD)]
             ).astype(BF16)
-    out_copy.wait()
-    for n, ref in enumerate(outs):
+    sent = [tokens_copy]
+    wide_copy.wait()
+    for n in (3, 2, 1, 0):
         group = (chip ^ (n // 2)) * 2 + (core ^ (n % 2))
         columns = pl.ds(pl.multiple_of(group * 768, 768), 768)
-        ref[...] = dot(ho_ref[...], wide_ref[:, columns]).astype(BF16)
+        res_ref[n] = dot(ho_ref[...], wide_ref[:, columns]).astype(BF16)
+        sent.append(pltpu.make_async_copy(res_ref.at[n], outs[n], out_sems.at[n]))
+        sent[-1].start()
+    for copy in sent:
+        copy.wait()
 
 
 def attention(meta, *arrays):
@@ -205,21 +224,25 @@
     return pl.pallas_call(
         kernel,
         in_specs=[pl.BlockSpec(memory_space=pltpu.SMEM)] + [hbm] * 8 + [vmem] * 10 + [hbm],
-        out_specs=(vmem,) * 5,
+        out_specs=(hbm,) * 5,
         out_shape=(shape,) * 5,
         scratch_shapes=[
             pltpu.VMEM((NB, 64, BK), BF16),
-            pltpu.VMEM((768, 3072), BF16),
             pltpu.VMEM((BK, ROWS), BF16),
             pltpu.VMEM((2, HEADS, FT, ROWS), BF16),
             pltpu.VMEM((2, HEADS * FT, BK), BF16),
             pltpu.VMEM((2, HEADS * FT, ROWS), F32),
             pltpu.VMEM((2 * FT, HEADS * HD), BF16),
             pltpu.VMEM((2, HEADS * FT, 1), F32),
+            pltpu.VMEM((HEADS, ROWS, BK), BF16),
+            pltpu.VMEM((BK, ROWS), BF16),
+            pltpu.VMEM((5, 2 * FT, HEADS * HD), BF16),
+            pltpu.VMEM((HEADS * HD, 4 * HEADS * HD), BF16),
             pltpu.SemaphoreType.DMA((32,)),
+            pltpu.SemaphoreType.DMA((5,)),
             pltpu.SemaphoreType.DMA,
         ],
-        compiler_params=pltpu.CompilerParams(vmem_limit_bytes=56 * 2**20),
+        compiler_params=pltpu.CompilerParams(vmem_limit_bytes=52 * 2**20),
     )(meta, *arrays)
 
 
@@ -282,7 +305,7 @@
             jax.ShapeDtypeStruct((ROWS, columns), BF16),
             jax.ShapeDtypeStruct((ROWS, columns), BF16),
         ],
-        compiler_params=pltpu.CompilerParams(vmem_limit_bytes=24 * 2**20),
+        compiler_params=pltpu.CompilerParams(vmem_limit_bytes=57 * 2**20),
         cost_estimate=pl.CostEstimate(
             flops=2 * ROWS * 3072 * 2400, bytes_accessed=3 * 3072 * 768 * 2, transcendentals=0
         ),
@@ -304,6 +327,7 @@
         in_specs=[pl.BlockSpec(memory_space=pltpu.SMEM)] + [vmem] * 4,
         out_specs=vmem,
         out_shape=jax.ShapeDtypeStruct((2, 32, BK), BF16),
+        compiler_params=pltpu.CompilerParams(vmem_limit_bytes=2 * 2**20),
         cost_estimate=pl.CostEstimate(flops=0, bytes_accessed=200000, transcendentals=0),
     )(z.astype(jnp.int32).reshape(1), *parts)
 

time: 191 us -> 179 us (0.937)
  local copies, waits for them, and re-layouts: 13.3 us -> 2.81 us
  Pallas kernels: 122 us -> 118 us
  waiting for transfers between devices: 30.1 us -> 32.6 us
    unnamed x52 -> x22, local copies, waits for them, and re-layouts: 11.5 us -> 1.51 us
    pallas_call x1, Pallas kernels: 117 us -> 110 us  [attention(): pl.pallas_call(kernel, in_specs=[pl.BlockSpec(memory_space=pltpu.SMEM)] +...]
    pallas_call x1, Pallas kernels: 3.55 us -> 8.68 us  [through(): pl.pallas_call(weights_kernel, grid_spec=pltpu.PrefetchScalarGridSpec(num...]
    ppermute x17, waiting for transfers between devices: 30.1 us -> 32.6 us  [permute(): lax.ppermute(x, axis, [(i, to(i)) for i in range(lax.axis_size(axis))])]
  transfers between devices with their start and end apart: 17 -> 17, of which waited for: 5 -> 5; matrix products, arithmetic and copies ran while one was open for 4% -> 4% of each run, Pallas kernels for 3% -> 5%
where the time goes in v3:
time: 179 us
  Pallas kernels  118 us (66%)
  waiting for transfers between devices  32.6 us (18%)
  starting transfers between devices  18.5 us (10%)
  other arithmetic  6.77 us (4%)
  local copies, waits for them, and re-layouts  2.81 us (2%)
    pallas_call x1, Pallas kernels, attention(): pl.pallas_call(kernel, in_specs=[pl.BlockSpec(memory_space=pltpu.SMEM)] +...  110 us
    ppermute x17, waiting for transfers between devices, permute(): lax.ppermute(x, axis, [(i, to(i)) for i in range(lax.axis_size(axis))])  32.6 us
    ppermute x17, starting transfers between devices, permute(): lax.ppermute(x, axis, [(i, to(i)) for i in range(lax.axis_size(axis))])  18.5 us
    pallas_call x1, Pallas kernels, through(): pl.pallas_call(weights_kernel, grid_spec=pltpu.PrefetchScalarGridSpec(num...  8.68 us
  transfers between devices with their start and end apart: 17, of which 5 were waited for; matrix products, arithmetic and copies ran while one was open for 4% of the time, Pallas kernels for 5%

profile of v3, /device:TPU:1, one launch (start us, length us, event | category | flops | bytes accessed | tf_op | source)
XLA Modules:
  0.0 179.4 jit_solution(2212000906628225916)
XLA Ops:
  0.0 0.8 copy-done
  0.8 4.6 %collective-permute-start.2 = (bf16[32,384]{1,0:T(8,128)(2,1)S(1)}, bf16[32,384]{1,0:T(8,128)(2,1)S(1)}, u32[]{:S(2)}, u32[]{:S(2)}) collective-permute-start(bf16[32,384]{1,0:T(8,128)(2,1)S(1)} %constant_dynamic-slice_fusion.p0), channel_id=1, source_target_pairs={{0,12},{4,0},{8,4},{12,8},{16,28},{20,16},{24,20},{28,24},{32,44},... | collective-permute-start | bytes 73736 | tf_op jit(solution)/shard_map/ppermute | solution.py:250
  5.4 0.0 collective-permute-start.1
  5.4 0.7 collective-permute-start
  6.1 0.8 subtract_convert_fusion
  6.9 1.1 concatenate.24.p0.refs_11_
  8.1 0.0 copy-start.9
  8.1 1.6 collective-permute-start.13
  9.7 1.3 collective-permute-start.12
  11.0 0.1 fusion.4
  11.0 0.8 fusion.2
  11.9 0.8 multiply_sine_fusion
  12.6 0.8 fusion.3
  13.5 0.1 concatenate.23.meta
  13.6 0.5 collective-permute-start.11
  14.2 0.0 collective-permute-done.1.p2
  14.2 0.2 shard_map.154
  14.3 2.9 %collective-permute-start.3 = (bf16[2,32,768]{2,1,0:T(8,128)(2,1)S(1)}, bf16[2,32,768]{2,1,0:T(8,128)(2,1)S(1)}, u32[]{:S(2)}, u32[]{:S(2)}) collective-permute-start(bf16[2,32,768]{2,1,0:T(8,128)(2,1)S(1)} %shard_map.154), channel_id=1, source_target_pairs={{0,16},{4,20},{8,24},{12,28},{16,0},{20,4},{24,8},{28,12},{32,48},... | collective-permute-start | bytes 294920 | tf_op jit(solution)/shard_map/ppermute | solution.py:250
  17.3 0.1 fusion
  17.4 7.9 %collective-permute-done.3 = bf16[2,32,768]{2,1,0:T(8,128)(2,1)S(1)} collective-permute-done((bf16[2,32,768]{2,1,0:T(8,128)(2,1)S(1)}, bf16[2,32,768]{2,1,0:T(8,128)(2,1)S(1)}, u32[]{:S(2)}, u32[]{:S(2)}) %collective-permute-start.3) | collective-permute-done | bytes 98336 | tf_op jit(solution)/shard_map/ppermute | solution.py:250
  25.3 2.5 %collective-permute-start.9 = (bf16[2,2,32,768]{3,2,1,0:T(8,128)(2,1)S(1)}, bf16[2,2,32,768]{3,2,1,0:T(8,128)(2,1)S(1)}, u32[]{:S(2)}, u32[]{:S(2)}) collective-permute-start(bf16[2,2,32,768]{3,2,1,0:T(8,128)(2,1)S(1)} %pad_maximum_fusion.refs_0_), channel_id=1, source_target_pairs={{0,96},{4,100},{8,104},{12,108},{16,112},{20,116},{24,120},{28,124... | collective-permute-start | bytes 589832 | tf_op jit(solution)/shard_map/ppermute | solution.py:250
  27.9 0.5 collective-permute-start.7
  28.4 0.0 collective-permute-done.13.p3
  28.4 0.6 collective-permute-start.5
  29.1 0.1 maximum_multiply_fusion
  29.2 0.9 pad_maximum_fusion.1
  30.1 0.7 collective-permute-start.4
  30.8 5.5 %collective-permute-done.9.refs_6_ = bf16[2,2,32,768]{3,2,1,0:T(8,128)(2,1)S(1)} collective-permute-done((bf16[2,2,32,768]{3,2,1,0:T(8,128)(2,1)S(1)}, bf16[2,2,32,768]{3,2,1,0:T(8,128)(2,1)S(1)}, u32[]{:S(2)}, u32[]{:S(2)}) %collective-permute-start.9) | collective-permute-done | bytes 196640 | tf_op jit(solution)/shard_map/ppermute | solution.py:250
  36.3 0.9 collective-permute-start.10
  37.2 0.0 collective-permute-done.7.refs_4_
  37.2 0.1 collective-permute-start.8
  37.3 3.1 %collective-permute-done.5.refs_2_ = bf16[2,2,32,768]{3,2,1,0:T(8,128)(2,1)S(1)} collective-permute-done((bf16[2,2,32,768]{3,2,1,0:T(8,128)(2,1)S(1)}, bf16[2,2,32,768]{3,2,1,0:T(8,128)(2,1)S(1)}, u32[]{:S(2)}, u32[]{:S(2)}) %collective-permute-start.5) | collective-permute-done | bytes 196640 | tf_op jit(solution)/shard_map/ppermute | solution.py:250
  40.4 0.5 collective-permute-start.6
  40.9 0.0 collective-permute-done.11.p1
  40.9 0.7 copy-done.8
  41.6 8.7 %shard_map.155 = (bf16[1056,144]{1,0:T(8,128)(2,1)}, bf16[144,768]{1,0:T(8,128)(2,1)}, bf16[144,768]{1,0:T(8,128)(2,1)}) custom-call(s32[1]{0:T(128)} %bitcast.9.me, bf16[144,768]{1,0:T(8,128)(2,1)} %copy-done.3, bf16[144,768]{1,0:T(8,128)(2,1)} %copy-done.8, bf16[144,768]{1,0:T(8,128)(2,1)} %copy-done.7, bf16[144,768]{1,0:T(8,128)(2,1)} %copy-done.6, ...), custom_call_target="tpu_custom_call" | custom-call | flops 2123366400 | bytes 14155776 | tf_op jit(solution)/shard_map/pallas_call | solution.py:288
  50.3 0.0 collective-permute-done.10.refs_7_
  50.3 0.0 collective-permute-done.8.refs_5_
  50.3 109.6 %shard_map.156 = (bf16[384,768]{1,0:T(8,128)(2,1)}, bf16[384,768]{1,0:T(8,128)(2,1)}, bf16[384,768]{1,0:T(8,128)(2,1)}, bf16[384,768]{1,0:T(8,128)(2,1)}, bf16[384,768]{1,0:T(8,128)(2,1)}) custom-call(s32[8]{0:T(128)S(1)} %concatenate.23.meta, bf16[2,2,32,768]{3,2,1,0:T(8,128)(2,1)S(1)} %pad_maximum_fusion.refs_0_, ...), custom_call_target="tpu_custom_call" | custom-call | tf_op jit(solution)/shard_map/pallas_call | solution.py:224
  159.9 0.0 copy-start.4
  160.0 0.1 collective-permute-start.15
  160.1 0.5 collective-permute-start.14
  160.6 1.7 collective-permute-done.15
  162.3 1.2 add_convert_fusion.1
  163.5 0.5 collective-permute-start.16
  163.9 0.0 collective-permute-done.14
  163.9 14.4 %collective-permute-done.16 = bf16[384,768]{1,0:T(8,128)(2,1)S(1)} collective-permute-done((bf16[384,768]{1,0:T(8,128)(2,1)S(1)}, bf16[384,768]{1,0:T(8,128)(2,1)S(1)}, u32[]{:S(2)}, u32[]{:S(2)}) %collective-permute-start.16) | collective-permute-done | bytes 589856 | tf_op jit(solution)/shard_map/ppermute | solution.py:250
  178.3 1.1 add_convert_fusion
  (33 shorter events, 0.2 us)
Async XLA Ops:
  0.0 0.8 copy-start
  0.0 17.3 %copy-start.10 = (f32[192,48]{1,0:T(8,128)S(1)}, f32[192,48]{1,0:T(8,128)}, u32[]{:S(2)}) copy-start(f32[192,48]{1,0:T(8,128)} %constant.98.clone) | copy-start | bytes 110596
  0.8 12.8 %collective-permute-start.2 = (bf16[32,384]{1,0:T(8,128)(2,1)S(1)}, bf16[32,384]{1,0:T(8,128)(2,1)S(1)}, u32[]{:S(2)}, u32[]{:S(2)}) collective-permute-start(bf16[32,384]{1,0:T(8,128)(2,1)S(1)} %constant_dynamic-slice_fusion.p0), channel_id=1, source_target_pairs={{0,12},{4,0},{8,4},{12,8},{16,28},{20,16},{24,20},{28,24},{32,44},... | collective-permute-start | bytes 73736 | tf_op jit(solution)/shard_map/ppermute | solution.py:250
  5.4 8.8 %collective-permute-start.1 = (bf16[32,384]{1,0:T(8,128)(2,1)S(1)}, bf16[32,384]{1,0:T(8,128)(2,1)S(1)}, u32[]{:S(2)}, u32[]{:S(2)}) collective-permute-start(bf16[32,384]{1,0:T(8,128)(2,1)S(1)} %constant_dynamic-slice_fusion.p0), channel_id=1, source_target_pairs={{0,8},{4,12},{8,0},{12,4},{16,24},{20,28},{24,16},{28,20},{32,40},... | collective-permute-start | bytes 73736 | tf_op jit(solution)/shard_map/ppermute | solution.py:250
  5.4 8.8 %collective-permute-start = (bf16[32,384]{1,0:T(8,128)(2,1)S(1)}, bf16[32,384]{1,0:T(8,128)(2,1)S(1)}, u32[]{:S(2)}, u32[]{:S(2)}) collective-permute-start(bf16[32,384]{1,0:T(8,128)(2,1)S(1)} %constant_dynamic-slice_fusion.p0), channel_id=1, source_target_pairs={{0,4},{4,8},{8,12},{12,0},{16,20},{20,24},{24,28},{28,16},{32,36},... | collective-permute-start | bytes 73736 | tf_op jit(solution)/shard_map/ppermute | solution.py:250
  8.0 21.0 %copy-start.3 = (bf16[144,768]{1,0:T(8,128)(2,1)}, bf16[144,768]{1,0:T(8,128)(2,1)S(1)}, u32[]{:S(2)}) copy-start(bf16[144,768]{1,0:T(8,128)(2,1)S(1)} %concatenate.24.p0.refs_11_) | copy-start | bytes 663556
  8.1 21.0 %copy-start.9 = (f32[192,48]{1,0:T(8,128)S(1)}, f32[192,48]{1,0:T(8,128)}, u32[]{:S(2)}) copy-start(f32[192,48]{1,0:T(8,128)} %constant.97.clone) | copy-start | bytes 110596
  8.1 20.3 %collective-permute-start.13 = (bf16[144,768]{1,0:T(8,128)(2,1)S(1)}, bf16[144,768]{1,0:T(8,128)(2,1)S(1)}, u32[]{:S(2)}, u32[]{:S(2)}) collective-permute-start(bf16[144,768]{1,0:T(8,128)(2,1)S(1)} %concatenate.24.p0.refs_11_), channel_id=1, source_target_pairs={{0,3},{1,0},{2,1},{3,2},{4,7},{5,4},{6,5},{7,6},{8,11},{9,8},{10,9... | collective-permute-start | bytes 663560 | tf_op jit(solution)/shard_map/ppermute | solution.py:250
  9.7 20.4 %collective-permute-start.12 = (bf16[144,768]{1,0:T(8,128)(2,1)S(1)}, bf16[144,768]{1,0:T(8,128)(2,1)S(1)}, u32[]{:S(2)}, u32[]{:S(2)}) collective-permute-start(bf16[144,768]{1,0:T(8,128)(2,1)S(1)} %concatenate.24.p0.refs_11_), channel_id=1, source_target_pairs={{0,2},{1,3},{2,0},{3,1},{4,6},{5,7},{6,4},{7,5},{8,10},{9,11},{10,... | collective-permute-start | bytes 663560 | tf_op jit(solution)/shard_map/ppermute | solution.py:250
  13.6 27.3 %collective-permute-start.11 = (bf16[144,768]{1,0:T(8,128)(2,1)S(1)}, bf16[144,768]{1,0:T(8,128)(2,1)S(1)}, u32[]{:S(2)}, u32[]{:S(2)}) collective-permute-start(bf16[144,768]{1,0:T(8,128)(2,1)S(1)} %concatenate.24.p0.refs_11_), channel_id=1, source_target_pairs={{0,1},{1,2},{2,3},{3,0},{4,5},{5,6},{6,7},{7,4},{8,9},{9,10},{10,1... | collective-permute-start | bytes 663560 | tf_op jit(solution)/shard_map/ppermute | solution.py:250
  14.3 10.9 %collective-permute-start.3 = (bf16[2,32,768]{2,1,0:T(8,128)(2,1)S(1)}, bf16[2,32,768]{2,1,0:T(8,128)(2,1)S(1)}, u32[]{:S(2)}, u32[]{:S(2)}) collective-permute-start(bf16[2,32,768]{2,1,0:T(8,128)(2,1)S(1)} %shard_map.154), channel_id=1, source_target_pairs={{0,16},{4,20},{8,24},{12,28},{16,0},{20,4},{24,8},{28,12},{32,48},... | collective-permute-start | bytes 294920 | tf_op jit(solution)/shard_map/ppermute | solution.py:250
  25.3 11.0 %collective-permute-start.9 = (bf16[2,2,32,768]{3,2,1,0:T(8,128)(2,1)S(1)}, bf16[2,2,32,768]{3,2,1,0:T(8,128)(2,1)S(1)}, u32[]{:S(2)}, u32[]{:S(2)}) collective-permute-start(bf16[2,2,32,768]{3,2,1,0:T(8,128)(2,1)S(1)} %pad_maximum_fusion.refs_0_), channel_id=1, source_target_pairs={{0,96},{4,100},{8,104},{12,108},{16,112},{20,116},{24,120},{28,124... | collective-permute-start | bytes 589832 | tf_op jit(solution)/shard_map/ppermute | solution.py:250
  27.9 9.4 %collective-permute-start.7 = (bf16[2,2,32,768]{3,2,1,0:T(8,128)(2,1)S(1)}, bf16[2,2,32,768]{3,2,1,0:T(8,128)(2,1)S(1)}, u32[]{:S(2)}, u32[]{:S(2)}) collective-permute-start(bf16[2,2,32,768]{3,2,1,0:T(8,128)(2,1)S(1)} %pad_maximum_fusion.refs_0_), channel_id=1, source_target_pairs={{0,64},{4,68},{8,72},{12,76},{16,80},{20,84},{24,88},{28,92},{32,9... | collective-permute-start | bytes 589832 | tf_op jit(solution)/shard_map/ppermute | solution.py:250
  28.4 12.5 %copy-start.6 = (bf16[144,768]{1,0:T(8,128)(2,1)}, bf16[144,768]{1,0:T(8,128)(2,1)S(1)}, u32[]{:S(2)}) copy-start(bf16[144,768]{1,0:T(8,128)(2,1)S(1)} %collective-permute-done.13.p3) | copy-start | bytes 663556
  28.4 12.0 %collective-permute-start.5 = (bf16[2,2,32,768]{3,2,1,0:T(8,128)(2,1)S(1)}, bf16[2,2,32,768]{3,2,1,0:T(8,128)(2,1)S(1)}, u32[]{:S(2)}, u32[]{:S(2)}) collective-permute-start(bf16[2,2,32,768]{3,2,1,0:T(8,128)(2,1)S(1)} %pad_maximum_fusion.refs_0_), channel_id=1, source_target_pairs={{0,32},{4,36},{8,40},{12,44},{16,48},{20,52},{24,56},{28,60},{32,6... | collective-permute-start | bytes 589832 | tf_op jit(solution)/shard_map/ppermute | solution.py:250
  30.1 10.8 %copy-start.7 = (bf16[144,768]{1,0:T(8,128)(2,1)}, bf16[144,768]{1,0:T(8,128)(2,1)S(1)}, u32[]{:S(2)}) copy-start(bf16[144,768]{1,0:T(8,128)(2,1)S(1)} %collective-permute-done.12.p2) | copy-start | bytes 663556
  30.1 20.2 %collective-permute-start.4 = (bf16[2,2,32,768]{3,2,1,0:T(8,128)(2,1)S(1)}, bf16[2,2,32,768]{3,2,1,0:T(8,128)(2,1)S(1)}, u32[]{:S(2)}, u32[]{:S(2)}) collective-permute-start(bf16[2,2,32,768]{3,2,1,0:T(8,128)(2,1)S(1)} %pad_maximum_fusion.refs_0_), channel_id=1, source_target_pairs={{0,1},{1,0},{2,3},{3,2},{4,5},{5,4},{6,7},{7,6},{8,9},{9,8},{10,11... | collective-permute-start | bytes 589832 | tf_op jit(solution)/shard_map/ppermute | solution.py:250
  36.3 14.0 %collective-permute-start.10 = (bf16[2,2,32,768]{3,2,1,0:T(8,128)(2,1)S(1)}, bf16[2,2,32,768]{3,2,1,0:T(8,128)(2,1)S(1)}, u32[]{:S(2)}, u32[]{:S(2)}) collective-permute-start(bf16[2,2,32,768]{3,2,1,0:T(8,128)(2,1)S(1)} %collective-permute-done.9.refs_6_), channel_id=1, source_target_pairs={{0,1},{1,0},{2,3},{3,2},{4,5},{5,4},{6,7},{7,6},{8,9},{9,8},{10,11... | collective-permute-start | bytes 589832 | tf_op jit(solution)/shard_map/ppermute | solution.py:250
  37.2 13.1 %collective-permute-start.8 = (bf16[2,2,32,768]{3,2,1,0:T(8,128)(2,1)S(1)}, bf16[2,2,32,768]{3,2,1,0:T(8,128)(2,1)S(1)}, u32[]{:S(2)}, u32[]{:S(2)}) collective-permute-start(bf16[2,2,32,768]{3,2,1,0:T(8,128)(2,1)S(1)} %collective-permute-done.7.refs_4_), channel_id=1, source_target_pairs={{0,1},{1,0},{2,3},{3,2},{4,5},{5,4},{6,7},{7,6},{8,9},{9,8},{10,11... | collective-permute-start | bytes 589832 | tf_op jit(solution)/shard_map/ppermute | solution.py:250
  40.4 9.9 %collective-permute-start.6 = (bf16[2,2,32,768]{3,2,1,0:T(8,128)(2,1)S(1)}, bf16[2,2,32,768]{3,2,1,0:T(8,128)(2,1)S(1)}, u32[]{:S(2)}, u32[]{:S(2)}) collective-permute-start(bf16[2,2,32,768]{3,2,1,0:T(8,128)(2,1)S(1)} %collective-permute-done.5.refs_2_), channel_id=1, source_target_pairs={{0,1},{1,0},{2,3},{3,2},{4,5},{5,4},{6,7},{7,6},{8,9},{9,8},{10,11... | collective-permute-start | bytes 589832 | tf_op jit(solution)/shard_map/ppermute | solution.py:250
  40.9 0.7 copy-start.8
  41.6 8.7 %copy-start.1 = (f32[48,768]{1,0:T(8,128)S(1)}, f32[48,768]{1,0:T(8,128)}, u32[]{:S(2)}) copy-start(f32[48,768]{1,0:T(8,128)} %constant.93.clone.refs_13_) | copy-start | bytes 442372
  41.6 8.7 %copy-start.2 = (f32[48,768]{1,0:T(8,128)S(1)}, f32[48,768]{1,0:T(8,128)}, u32[]{:S(2)}) copy-start(f32[48,768]{1,0:T(8,128)} %constant.92.clone.refs_12_) | copy-start | bytes 442372
  159.9 18.4 %copy-start.4 = (bf16[384,768]{1,0:T(8,128)(2,1)S(1)}, bf16[384,768]{1,0:T(8,128)(2,1)}, u32[]{:S(2)}) copy-start(bf16[384,768]{1,0:T(8,128)(2,1)} %get-tuple-element.16) | copy-start | bytes 1769476
  160.0 18.4 %copy-start.5 = (bf16[384,768]{1,0:T(8,128)(2,1)S(1)}, bf16[384,768]{1,0:T(8,128)(2,1)}, u32[]{:S(2)}) copy-start(bf16[384,768]{1,0:T(8,128)(2,1)} %get-tuple-element.20) | copy-start | bytes 1769476
  160.0 2.3 %collective-permute-start.15 = (bf16[384,768]{1,0:T(8,128)(2,1)}, bf16[384,768]{1,0:T(8,128)(2,1)S(1)}, u32[]{:S(2)}, u32[]{:S(2)}) collective-permute-start(bf16[384,768]{1,0:T(8,128)(2,1)} %get-tuple-element.19), channel_id=1, source_target_pairs={{0,1},{1,0},{2,3},{3,2},{4,5},{5,4},{6,7},{7,6},{8,9},{9,8},{10,11... | collective-permute-start | bytes 1769480 | tf_op jit(solution)/shard_map/ppermute | solution.py:250
  160.1 3.9 %collective-permute-start.14 = (bf16[384,768]{1,0:T(8,128)(2,1)}, bf16[384,768]{1,0:T(8,128)(2,1)S(1)}, u32[]{:S(2)}, u32[]{:S(2)}) collective-permute-start(bf16[384,768]{1,0:T(8,128)(2,1)} %get-tuple-element.17), channel_id=1, source_target_pairs={{0,1},{1,0},{2,3},{3,2},{4,5},{5,4},{6,7},{7,6},{8,9},{9,8},{10,11... | collective-permute-start | bytes 1769480 | tf_op jit(solution)/shard_map/ppermute | solution.py:250
  163.5 14.9 %collective-permute-start.16 = (bf16[384,768]{1,0:T(8,128)(2,1)S(1)}, bf16[384,768]{1,0:T(8,128)(2,1)S(1)}, u32[]{:S(2)}, u32[]{:S(2)}) collective-permute-start(bf16[384,768]{1,0:T(8,128)(2,1)S(1)} %add_convert_fusion.1), channel_id=1, source_target_pairs={{0,2},{1,3},{2,0},{3,1},{4,6},{5,7},{6,4},{7,5},{8,10},{9,11},{10,... | collective-permute-start | bytes 1769480 | tf_op jit(solution)/shard_map/ppermute | solution.py:250

commit v4 on v3

--- a/solution.py
+++ b/solution.py
@@ -283,7 +283,7 @@
 def through(parts, gain, wq, wk, wv):
     columns = HEADS * HD
     whole = lambda *shape: pl.BlockSpec(shape, lambda k, me: (0,) * len(shape))
-    source = lambda k, me: (me[0] + 4 - k) % 4
+    source = lambda k, me: me[0] ^ k
     weight = pl.BlockSpec((columns, columns), lambda k, me: (source(k, me), 0))
     return pl.pallas_call(
         weights_kernel,
@@ -357,11 +357,11 @@
     parts = [half] + [permute(half, "seq", functools.partial(to_z, k)) for k in (1, 2, 3)]
     block = join(seq % 4, parts)
     pair = jnp.stack([block, permute(block, "seq", to_y)])
-    pieces = []
-    for k in range(4):
-        part = permute(pair, "seq", functools.partial(to_x, k)) if k else pair
-        pieces += [part, permute(part, "head", lambda i: i ^ 1)]
-    return pieces
+    return [pair] + [permute(pair, "seq", functools.partial(to_x, k)) for k in (1, 2, 3)]
+
+
+def swap(x, bit):
+    return permute(x, "head", lambda i: i ^ bit)
 
 
 def add(a, b):
@@ -387,15 +387,20 @@
     places = jnp.stack([seq // 8, (seq // 4) % 2, head % 2, head // 2]).astype(jnp.int32)
     meta = jnp.concatenate([ends, frames, places])
 
-    pieces = all_latents(latents)
+    halves = all_latents(latents)
 
     b0 = patch_bias.astype(BF16)
     b1 = (patch_bias - b0.astype(F32)).astype(BF16)
     b2 = (patch_bias - b0.astype(F32) - b1.astype(F32)).astype(BF16)
     rest = jnp.zeros((ROWS - 131, patch_bias.shape[0]), BF16)
     wide = jnp.concatenate([patch_weight, b0[None], b1[None], b2[None], rest], axis=0)
-    parts = [wide] + [permute(wide, "head", lambda i, k=k: (i + k) % 4) for k in (1, 2, 3)]
+    far_part = swap(wide, 2)
+    parts = [wide, swap(wide, 1), far_part, swap(far_part, 1)]
     mg, mq, mv = through(parts, norm_gain, query_weight, key_weight, value_weight)
+    others = [swap(halves[0], 1)] + [
+        swap(lax.optimization_barrier((part, mq))[0], 1) for part in halves[1:]
+    ]
+    pieces = [piece for pair in zip(halves, others) for piece in pair]
 
     w_t, _, _ = frequencies()
     spatial = spatial_angles()
@@ -419,7 +424,6 @@
     near, near_other, far, far_other, tokens = attention(
         meta, *pieces, mg, mq, mv, wide, cs, ss, ct, st, cq, sq, out_weight
     )
-    swap = lambda x, bit: permute(x, "head", lambda i: i ^ bit)
     sent = swap(add(far, swap(far_other, 1)).astype(BF16), 2)
     kept = add(near, swap(near_other, 1)).astype(BF16)
     return (add(kept, sent) + tokens.astype(F32)).astype(BF16)

time: 179 us -> 167 us (0.933)
  waiting for transfers between devices: 32.6 us -> 19.5 us
    ppermute x17, waiting for transfers between devices: 32.6 us -> 19.5 us  [permute(): lax.ppermute(x, axis, [(i, to(i)) for i in range(lax.axis_size(axis))])]
where the time goes in v4:
time: 167 us; the launch traced here: 166 us
  Pallas kernels  118 us (71%)
  waiting for transfers between devices  19.5 us (12%)
  starting transfers between devices  18.6 us (11%)
  other arithmetic  6.77 us (4%)
  local copies, waits for them, and re-layouts  2.8 us (2%)
    pallas_call x1, Pallas kernels, attention(): pl.pallas_call(kernel, in_specs=[pl.BlockSpec(memory_space=pltpu.SMEM)] +...  109 us
    ppermute x17, waiting for transfers between devices, permute(): lax.ppermute(x, axis, [(i, to(i)) for i in range(lax.axis_size(axis))])  19.5 us
    ppermute x17, starting transfers between devices, permute(): lax.ppermute(x, axis, [(i, to(i)) for i in range(lax.axis_size(axis))])  18.6 us
    pallas_call x1, Pallas kernels, through(): pl.pallas_call(weights_kernel, grid_spec=pltpu.PrefetchScalarGridSpec(num...  8.67 us
  transfers between devices with their start and end apart: 17, of which 5 were waited for; matrix products, arithmetic and copies ran while one was open for 4% of the time, Pallas kernels for 5%

profile of v4, /device:TPU:1, one launch (start us, length us, event | category | flops | bytes accessed | tf_op | source)
XLA Modules:
  0.0 165.7 jit_solution(5815400185775536759)
XLA Ops:
  0.0 0.8 copy-done
  0.8 4.6 %collective-permute-start.2 = (bf16[32,384]{1,0:T(8,128)(2,1)S(1)}, bf16[32,384]{1,0:T(8,128)(2,1)S(1)}, u32[]{:S(2)}, u32[]{:S(2)}) collective-permute-start(bf16[32,384]{1,0:T(8,128)(2,1)S(1)} %constant_dynamic-slice_fusion.p0), channel_id=1, source_target_pairs={{0,12},{4,0},{8,4},{12,8},{16,28},{20,16},{24,20},{28,24},{32,44},... | collective-permute-start | bytes 73736 | tf_op jit(solution)/shard_map/ppermute | solution.py:250
  5.4 0.0 collective-permute-start.1
  5.4 0.7 collective-permute-start
  6.1 0.8 subtract_convert_fusion
  6.9 1.1 concatenate.24.p0.refs_11_
  8.1 1.4 collective-permute-start.7
  9.4 1.8 %collective-permute-start.6 = (bf16[144,768]{1,0:T(8,128)(2,1)S(1)}, bf16[144,768]{1,0:T(8,128)(2,1)S(1)}, u32[]{:S(2)}, u32[]{:S(2)}) collective-permute-start(bf16[144,768]{1,0:T(8,128)(2,1)S(1)} %concatenate.24.p0.refs_11_), channel_id=1, source_target_pairs={{0,1},{1,0},{2,3},{3,2},{4,5},{5,4},{6,7},{7,6},{8,9},{9,8},{10,11... | collective-permute-start | bytes 663560 | tf_op jit(solution)/shard_map/ppermute | solution.py:250
  11.2 0.1 fusion.4
  11.3 0.8 multiply_sine_fusion
  12.1 0.8 fusion.2
  12.9 0.8 fusion.3
  13.8 0.1 concatenate.23.meta
  13.9 0.0 collective-permute-done.2.p3
  13.9 0.0 collective-permute-done.1.p2
  13.9 0.0 collective-permute-done.p1
  13.9 0.2 shard_map.154
  14.1 2.7 %collective-permute-start.3 = (bf16[2,32,768]{2,1,0:T(8,128)(2,1)S(1)}, bf16[2,32,768]{2,1,0:T(8,128)(2,1)S(1)}, u32[]{:S(2)}, u32[]{:S(2)}) collective-permute-start(bf16[2,32,768]{2,1,0:T(8,128)(2,1)S(1)} %shard_map.154), channel_id=1, source_target_pairs={{0,16},{4,20},{8,24},{12,28},{16,0},{20,4},{24,8},{28,12},{32,48},... | collective-permute-start | bytes 294920 | tf_op jit(solution)/shard_map/ppermute | solution.py:250
  16.8 0.0 collective-permute-done.7.p2
  16.8 0.3 collective-permute-start.8
  17.1 0.1 fusion
  17.2 2.8 %collective-permute-done.3 = bf16[2,32,768]{2,1,0:T(8,128)(2,1)S(1)} collective-permute-done((bf16[2,32,768]{2,1,0:T(8,128)(2,1)S(1)}, bf16[2,32,768]{2,1,0:T(8,128)(2,1)S(1)}, u32[]{:S(2)}, u32[]{:S(2)}) %collective-permute-start.3) | collective-permute-done | bytes 98336 | tf_op jit(solution)/shard_map/ppermute | solution.py:250
  20.1 2.5 %collective-permute-start.12 = (bf16[2,2,32,768]{3,2,1,0:T(8,128)(2,1)S(1)}, bf16[2,2,32,768]{3,2,1,0:T(8,128)(2,1)S(1)}, u32[]{:S(2)}, u32[]{:S(2)}) collective-permute-start(bf16[2,2,32,768]{3,2,1,0:T(8,128)(2,1)S(1)} %pad_maximum_fusion.refs_0_), channel_id=1, source_target_pairs={{0,96},{4,100},{8,104},{12,108},{16,112},{20,116},{24,120},{28,124... | collective-permute-start | bytes 589832 | tf_op jit(solution)/shard_map/ppermute | solution.py:250
  22.6 0.5 collective-permute-start.10
  23.2 0.6 collective-permute-start.5
  23.8 0.0 collective-permute-done.6.p1
  23.8 1.6 collective-permute-start.4
  25.4 0.0 collective-permute-done.8.p3
  25.4 0.7 copy-done.8
  26.1 8.7 %shard_map.155 = (bf16[1056,144]{1,0:T(8,128)(2,1)}, bf16[144,768]{1,0:T(8,128)(2,1)}, bf16[144,768]{1,0:T(8,128)(2,1)}) custom-call(s32[1]{0:T(128)} %bitcast.9.me, bf16[144,768]{1,0:T(8,128)(2,1)} %copy-done.3, bf16[144,768]{1,0:T(8,128)(2,1)} %copy-done.7, bf16[144,768]{1,0:T(8,128)(2,1)} %copy-done.6, bf16[144,768]{1,0:T(8,128)(2,1)} %copy-done.8, ...), custom_call_target="tpu_custom_call" | custom-call | flops 2123366400 | bytes 14155776 | tf_op jit(solution)/shard_map/pallas_call | solution.py:288
  34.8 0.0 collective-permute-done.10.refs_4_
  34.8 0.4 collective-permute-done.5.refs_2_
  35.2 0.5 collective-permute-start.9
  35.7 0.0 collective-permute-start.11
  35.7 0.5 collective-permute-start.13
  36.2 0.1 maximum_multiply_fusion
  36.4 0.9 pad_maximum_fusion.1
  37.3 0.1 collective-permute-done.13.refs_7_
  37.4 108.9 %shard_map.156 = (bf16[384,768]{1,0:T(8,128)(2,1)}, bf16[384,768]{1,0:T(8,128)(2,1)}, bf16[384,768]{1,0:T(8,128)(2,1)}, bf16[384,768]{1,0:T(8,128)(2,1)}, bf16[384,768]{1,0:T(8,128)(2,1)}) custom-call(s32[8]{0:T(128)S(1)} %concatenate.23.meta, bf16[2,2,32,768]{3,2,1,0:T(8,128)(2,1)S(1)} %pad_maximum_fusion.refs_0_, ...), custom_call_target="tpu_custom_call" | custom-call | tf_op jit(solution)/shard_map/pallas_call | solution.py:224
  146.3 0.0 copy-start.4
  146.4 0.4 collective-permute-start.15
  146.8 0.2 collective-permute-start.14
  147.0 1.7 %collective-permute-done.15 = bf16[384,768]{1,0:T(8,128)(2,1)S(1)} collective-permute-done((bf16[384,768]{1,0:T(8,128)(2,1)}, bf16[384,768]{1,0:T(8,128)(2,1)S(1)}, u32[]{:S(2)}, u32[]{:S(2)}) %collective-permute-start.15) | collective-permute-done | bytes 589856 | tf_op jit(solution)/shard_map/ppermute | solution.py:250
  148.7 1.2 add_convert_fusion.1
  149.9 0.3 collective-permute-start.16
  150.1 0.0 collective-permute-done.14
  150.1 14.4 %collective-permute-done.16 = bf16[384,768]{1,0:T(8,128)(2,1)S(1)} collective-permute-done((bf16[384,768]{1,0:T(8,128)(2,1)S(1)}, bf16[384,768]{1,0:T(8,128)(2,1)S(1)}, u32[]{:S(2)}, u32[]{:S(2)}) %collective-permute-start.16) | collective-permute-done | bytes 589856 | tf_op jit(solution)/shard_map/ppermute | solution.py:250
  164.5 1.1 add_convert_fusion
  (33 shorter events, 0.2 us)
Async XLA Ops:
  0.0 0.8 copy-start
  0.0 17.1 %copy-start.10 = (f32[192,48]{1,0:T(8,128)S(1)}, f32[192,48]{1,0:T(8,128)}, u32[]{:S(2)}) copy-start(f32[192,48]{1,0:T(8,128)} %constant.98.clone) | copy-start | bytes 110596
  0.8 13.1 %collective-permute-start.2 = (bf16[32,384]{1,0:T(8,128)(2,1)S(1)}, bf16[32,384]{1,0:T(8,128)(2,1)S(1)}, u32[]{:S(2)}, u32[]{:S(2)}) collective-permute-start(bf16[32,384]{1,0:T(8,128)(2,1)S(1)} %constant_dynamic-slice_fusion.p0), channel_id=1, source_target_pairs={{0,12},{4,0},{8,4},{12,8},{16,28},{20,16},{24,20},{28,24},{32,44},... | collective-permute-start | bytes 73736 | tf_op jit(solution)/shard_map/ppermute | solution.py:250
  5.4 8.5 %collective-permute-start.1 = (bf16[32,384]{1,0:T(8,128)(2,1)S(1)}, bf16[32,384]{1,0:T(8,128)(2,1)S(1)}, u32[]{:S(2)}, u32[]{:S(2)}) collective-permute-start(bf16[32,384]{1,0:T(8,128)(2,1)S(1)} %constant_dynamic-slice_fusion.p0), channel_id=1, source_target_pairs={{0,8},{4,12},{8,0},{12,4},{16,24},{20,28},{24,16},{28,20},{32,40},... | collective-permute-start | bytes 73736 | tf_op jit(solution)/shard_map/ppermute | solution.py:250
  5.4 8.5 %collective-permute-start = (bf16[32,384]{1,0:T(8,128)(2,1)S(1)}, bf16[32,384]{1,0:T(8,128)(2,1)S(1)}, u32[]{:S(2)}, u32[]{:S(2)}) collective-permute-start(bf16[32,384]{1,0:T(8,128)(2,1)S(1)} %constant_dynamic-slice_fusion.p0), channel_id=1, source_target_pairs={{0,4},{4,8},{8,12},{12,0},{16,20},{20,24},{24,28},{28,16},{32,36},... | collective-permute-start | bytes 73736 | tf_op jit(solution)/shard_map/ppermute | solution.py:250
  8.0 17.4 %copy-start.3 = (bf16[144,768]{1,0:T(8,128)(2,1)}, bf16[144,768]{1,0:T(8,128)(2,1)S(1)}, u32[]{:S(2)}) copy-start(bf16[144,768]{1,0:T(8,128)(2,1)S(1)} %concatenate.24.p0.refs_11_) | copy-start | bytes 663556
  8.1 8.7 %collective-permute-start.7 = (bf16[144,768]{1,0:T(8,128)(2,1)S(1)}, bf16[144,768]{1,0:T(8,128)(2,1)S(1)}, u32[]{:S(2)}, u32[]{:S(2)}) collective-permute-start(bf16[144,768]{1,0:T(8,128)(2,1)S(1)} %concatenate.24.p0.refs_11_), channel_id=1, source_target_pairs={{0,2},{1,3},{2,0},{3,1},{4,6},{5,7},{6,4},{7,5},{8,10},{9,11},{10,... | collective-permute-start | bytes 663560 | tf_op jit(solution)/shard_map/ppermute | solution.py:250
  9.4 14.3 %collective-permute-start.6 = (bf16[144,768]{1,0:T(8,128)(2,1)S(1)}, bf16[144,768]{1,0:T(8,128)(2,1)S(1)}, u32[]{:S(2)}, u32[]{:S(2)}) collective-permute-start(bf16[144,768]{1,0:T(8,128)(2,1)S(1)} %concatenate.24.p0.refs_11_), channel_id=1, source_target_pairs={{0,1},{1,0},{2,3},{3,2},{4,5},{5,4},{6,7},{7,6},{8,9},{9,8},{10,11... | collective-permute-start | bytes 663560 | tf_op jit(solution)/shard_map/ppermute | solution.py:250
  14.1 6.0 %collective-permute-start.3 = (bf16[2,32,768]{2,1,0:T(8,128)(2,1)S(1)}, bf16[2,32,768]{2,1,0:T(8,128)(2,1)S(1)}, u32[]{:S(2)}, u32[]{:S(2)}) collective-permute-start(bf16[2,32,768]{2,1,0:T(8,128)(2,1)S(1)} %shard_map.154), channel_id=1, source_target_pairs={{0,16},{4,20},{8,24},{12,28},{16,0},{20,4},{24,8},{28,12},{32,48},... | collective-permute-start | bytes 294920 | tf_op jit(solution)/shard_map/ppermute | solution.py:250
  16.8 8.6 %copy-start.6 = (bf16[144,768]{1,0:T(8,128)(2,1)}, bf16[144,768]{1,0:T(8,128)(2,1)S(1)}, u32[]{:S(2)}) copy-start(bf16[144,768]{1,0:T(8,128)(2,1)S(1)} %collective-permute-done.7.p2) | copy-start | bytes 663556
  16.8 8.6 %collective-permute-start.8 = (bf16[144,768]{1,0:T(8,128)(2,1)S(1)}, bf16[144,768]{1,0:T(8,128)(2,1)S(1)}, u32[]{:S(2)}, u32[]{:S(2)}) collective-permute-start(bf16[144,768]{1,0:T(8,128)(2,1)S(1)} %collective-permute-done.7.p2), channel_id=1, source_target_pairs={{0,1},{1,0},{2,3},{3,2},{4,5},{5,4},{6,7},{7,6},{8,9},{9,8},{10,11... | collective-permute-start | bytes 663560 | tf_op jit(solution)/shard_map/ppermute | solution.py:250
  20.1 14.7 %collective-permute-start.12 = (bf16[2,2,32,768]{3,2,1,0:T(8,128)(2,1)S(1)}, bf16[2,2,32,768]{3,2,1,0:T(8,128)(2,1)S(1)}, u32[]{:S(2)}, u32[]{:S(2)}) collective-permute-start(bf16[2,2,32,768]{3,2,1,0:T(8,128)(2,1)S(1)} %pad_maximum_fusion.refs_0_), channel_id=1, source_target_pairs={{0,96},{4,100},{8,104},{12,108},{16,112},{20,116},{24,120},{28,124... | collective-permute-start | bytes 589832 | tf_op jit(solution)/shard_map/ppermute | solution.py:250
  22.6 12.1 %collective-permute-start.10 = (bf16[2,2,32,768]{3,2,1,0:T(8,128)(2,1)S(1)}, bf16[2,2,32,768]{3,2,1,0:T(8,128)(2,1)S(1)}, u32[]{:S(2)}, u32[]{:S(2)}) collective-permute-start(bf16[2,2,32,768]{3,2,1,0:T(8,128)(2,1)S(1)} %pad_maximum_fusion.refs_0_), channel_id=1, source_target_pairs={{0,64},{4,68},{8,72},{12,76},{16,80},{20,84},{24,88},{28,92},{32,9... | collective-permute-start | bytes 589832 | tf_op jit(solution)/shard_map/ppermute | solution.py:250
  23.2 12.0 %collective-permute-start.5 = (bf16[2,2,32,768]{3,2,1,0:T(8,128)(2,1)S(1)}, bf16[2,2,32,768]{3,2,1,0:T(8,128)(2,1)S(1)}, u32[]{:S(2)}, u32[]{:S(2)}) collective-permute-start(bf16[2,2,32,768]{3,2,1,0:T(8,128)(2,1)S(1)} %pad_maximum_fusion.refs_0_), channel_id=1, source_target_pairs={{0,32},{4,36},{8,40},{12,44},{16,48},{20,52},{24,56},{28,60},{32,6... | collective-permute-start | bytes 589832 | tf_op jit(solution)/shard_map/ppermute | solution.py:250
  23.8 1.6 copy-start.7
  23.8 13.5 %collective-permute-start.4 = (bf16[2,2,32,768]{3,2,1,0:T(8,128)(2,1)S(1)}, bf16[2,2,32,768]{3,2,1,0:T(8,128)(2,1)S(1)}, u32[]{:S(2)}, u32[]{:S(2)}) collective-permute-start(bf16[2,2,32,768]{3,2,1,0:T(8,128)(2,1)S(1)} %pad_maximum_fusion.refs_0_), channel_id=1, source_target_pairs={{0,1},{1,0},{2,3},{3,2},{4,5},{5,4},{6,7},{7,6},{8,9},{9,8},{10,11... | collective-permute-start | bytes 589832 | tf_op jit(solution)/shard_map/ppermute | solution.py:250
  25.4 0.7 copy-start.8
  26.1 10.1 %copy-start.9 = (f32[192,48]{1,0:T(8,128)S(1)}, f32[192,48]{1,0:T(8,128)}, u32[]{:S(2)}) copy-start(f32[192,48]{1,0:T(8,128)} %constant.97.clone) | copy-start | bytes 110596
  34.8 2.6 %copy-start.1 = (f32[48,768]{1,0:T(8,128)S(1)}, f32[48,768]{1,0:T(8,128)}, u32[]{:S(2)}) copy-start(f32[48,768]{1,0:T(8,128)} %constant.93.clone.refs_13_) | copy-start | bytes 442372
  34.8 2.6 %copy-start.2 = (f32[48,768]{1,0:T(8,128)S(1)}, f32[48,768]{1,0:T(8,128)}, u32[]{:S(2)}) copy-start(f32[48,768]{1,0:T(8,128)} %constant.92.clone.refs_12_) | copy-start | bytes 442372
  35.2 2.1 %collective-permute-start.9 = (bf16[2,2,32,768]{3,2,1,0:T(8,128)(2,1)S(1)}, bf16[2,2,32,768]{3,2,1,0:T(8,128)(2,1)S(1)}, u32[]{:S(2)}, u32[]{:S(2)}) collective-permute-start(bf16[2,2,32,768]{3,2,1,0:T(8,128)(2,1)S(1)} %collective-permute-done.5.refs_2_), channel_id=1, source_target_pairs={{0,1},{1,0},{2,3},{3,2},{4,5},{5,4},{6,7},{7,6},{8,9},{9,8},{10,11... | collective-permute-start | bytes 589832 | tf_op jit(solution)/shard_map/ppermute | solution.py:250
  35.7 1.6 collective-permute-start.11
  35.7 1.7 %collective-permute-start.13 = (bf16[2,2,32,768]{3,2,1,0:T(8,128)(2,1)S(1)}, bf16[2,2,32,768]{3,2,1,0:T(8,128)(2,1)S(1)}, u32[]{:S(2)}, u32[]{:S(2)}) collective-permute-start(bf16[2,2,32,768]{3,2,1,0:T(8,128)(2,1)S(1)} %collective-permute-done.12.refs_6_), channel_id=1, source_target_pairs={{0,1},{1,0},{2,3},{3,2},{4,5},{5,4},{6,7},{7,6},{8,9},{9,8},{10,11... | collective-permute-start | bytes 589832 | tf_op jit(solution)/shard_map/ppermute | solution.py:250
  146.3 18.2 %copy-start.4 = (bf16[384,768]{1,0:T(8,128)(2,1)S(1)}, bf16[384,768]{1,0:T(8,128)(2,1)}, u32[]{:S(2)}) copy-start(bf16[384,768]{1,0:T(8,128)(2,1)} %get-tuple-element.22) | copy-start | bytes 1769476
  146.4 18.2 %copy-start.5 = (bf16[384,768]{1,0:T(8,128)(2,1)S(1)}, bf16[384,768]{1,0:T(8,128)(2,1)}, u32[]{:S(2)}) copy-start(bf16[384,768]{1,0:T(8,128)(2,1)} %get-tuple-element.26) | copy-start | bytes 1769476
  146.4 2.3 %collective-permute-start.15 = (bf16[384,768]{1,0:T(8,128)(2,1)}, bf16[384,768]{1,0:T(8,128)(2,1)S(1)}, u32[]{:S(2)}, u32[]{:S(2)}) collective-permute-start(bf16[384,768]{1,0:T(8,128)(2,1)} %get-tuple-element.25), channel_id=1, source_target_pairs={{0,1},{1,0},{2,3},{3,2},{4,5},{5,4},{6,7},{7,6},{8,9},{9,8},{10,11... | collective-permute-start | bytes 1769480 | tf_op jit(solution)/shard_map/ppermute | solution.py:250
  146.8 3.4 %collective-permute-start.14 = (bf16[384,768]{1,0:T(8,128)(2,1)}, bf16[384,768]{1,0:T(8,128)(2,1)S(1)}, u32[]{:S(2)}, u32[]{:S(2)}) collective-permute-start(bf16[384,768]{1,0:T(8,128)(2,1)} %get-tuple-element.23), channel_id=1, source_target_pairs={{0,1},{1,0},{2,3},{3,2},{4,5},{5,4},{6,7},{7,6},{8,9},{9,8},{10,11... | collective-permute-start | bytes 1769480 | tf_op jit(solution)/shard_map/ppermute | solution.py:250
  149.9 14.7 %collective-permute-start.16 = (bf16[384,768]{1,0:T(8,128)(2,1)S(1)}, bf16[384,768]{1,0:T(8,128)(2,1)S(1)}, u32[]{:S(2)}, u32[]{:S(2)}) collective-permute-start(bf16[384,768]{1,0:T(8,128)(2,1)S(1)} %add_convert_fusion.1), channel_id=1, source_target_pairs={{0,2},{1,3},{2,0},{3,1},{4,6},{5,7},{6,4},{7,5},{8,10},{9,11},{10,... | collective-permute-start | bytes 1769480 | tf_op jit(solution)/shard_map/ppermute | solution.py:250

commit v5 on v4

--- a/solution.py
+++ b/solution.py
@@ -52,20 +52,24 @@
     return jnp.dot(a, b, preferred_element_type=F32)
 
 
-def kernel(
-    meta,
-    *refs,
-):
+def kernel(seq_ref, head_ref, span_ref, *refs):
     pieces, refs = refs[:8], refs[8:]
-    (mg_ref, mq_ref, mv_ref, pw_ref, cs_ref, ss_ref, ct_ref, st_ref, cq_ref, sq_ref, wo_ref) = refs[:11]
-    (outs, tokens_ref), refs = (refs[11:15], refs[15]), refs[16:]
+    (mg_ref, mq_ref, mv_ref, pw_ref, cs_ref, ss_ref, ct_ref, st_ref, cq_ref, sq_ref, tq_ref, wo_ref) = refs[:12]
+    (outs, tokens_ref), refs = (refs[12:16], refs[16]), refs[17:]
     raw_ref, own_ref, q_ref, w_ref, u_ref, ho_ref, m_ref, k_ref, v_ref, res_ref, wide_ref, sems, out_sems, wide_sem = refs
-    end_early, end_late = meta[0], meta[1]
+    seq, head = seq_ref[0], head_ref[0]
+    own_frames = (seq, FRAMES - 1 - seq)
+
+    def end_of(frame):
+        count = lambda g, seen: seen + (span_ref[g] <= span_ref[frame]).astype(jnp.int32)
+        return lax.fori_loop(0, FRAMES, count, 0)
+
+    end_early, end_late = end_of(own_frames[0]), end_of(own_frames[1])
     blocks_early = (end_early + BF - 1) // BF
     blocks_late = (end_late + BF - 1) // BF
     wide_copy = pltpu.make_async_copy(wo_ref, wide_ref, wide_sem)
     wide_copy.start()
-    x_at, y_at, core, chip = meta[4], meta[5], meta[6], meta[7]
+    x_at, y_at, core, chip = seq // 8, (seq // 4) % 2, head % 2, head // 2
 
     copies = []
     for k in range(4):
@@ -132,7 +136,7 @@
         return keys, lambda: scaled(x, r)
 
     for i in range(2):
-        frame = meta[2 + i]
+        frame = own_frames[i]
         rows = pl.ds(pl.multiple_of((frame % BF) * FT, FT), FT)
         x = features(frame // BF)
         own_ref[...] = x.T
@@ -141,9 +145,11 @@
         own = own_ref[rows, :]
         lane = lax.broadcasted_iota(jnp.int32, (FT, ROWS - 128), 1)
         select = (lane == i).astype(F32).astype(BF16)
+        cos = cq_ref[...] + tq_ref[0, pl.ds(frame, 1), :]
+        sin = sq_ref[...] + tq_ref[1, pl.ds(frame, 1), :]
         for h in range(HEADS):
             pre = dot(own, mq_ref[:, pl.ds(h * HD, HD)])
-            rotated = pre * cq_ref[i] + pltpu.roll(pre, 64, 1) * sq_ref[i]
+            rotated = pre * cos + pltpu.roll(pre, 64, 1) * sin
             q_ref[i, h] = jnp.concatenate([rotated.astype(BF16), select], axis=1)
 
     tokens_copy = pltpu.make_async_copy(res_ref.at[4], tokens_ref, out_sems.at[4])
@@ -173,9 +179,20 @@
     lax.fori_loop(0, blocks_early, functools.partial(visit, (0, 1)), 0)
     lax.fori_loop(blocks_early, blocks_late, functools.partial(visit, (1,)), 0)
 
-    total = u_ref[:, :, 129:130]
-    good = jnp.where((total >= LOW) & (total <= HIGH), 1.0, 0.0)
-    bad = jnp.min(good) < 0.5
+    def finish():
+        good = jnp.ones((FT, 1), F32)
+        for i in range(2):
+            for h in range(HEADS):
+                u = u_ref[i, pl.ds(h * FT, FT)]
+                total = u[:, 129:130]
+                good = jnp.where((total >= LOW) & (total <= HIGH), good, 0.0)
+                mixed = (u / total).astype(BF16)
+                ho_ref[pl.ds(i * FT, FT), pl.ds(h * HD, HD)] = dot(
+                    mixed, mv_ref[:, pl.ds(h * HD, HD)]
+                ).astype(BF16)
+        return jnp.min(good) > 0.5
+
+    bad = jnp.logical_not(finish())
 
     @pl.when(bad)
     def _():
@@ -197,14 +214,8 @@
             return carry
 
         lax.fori_loop(0, blocks_late, visit_again, 0)
-
-    for i in range(2):
-        for h in range(HEADS):
-            u = u_ref[i, pl.ds(h * FT, FT)]
-            mixed = (u / u[:, 129:130]).astype(BF16)
-            ho_ref[pl.ds(i * FT, FT), pl.ds(h * HD, HD)] = dot(
-                mixed, mv_ref[:, pl.ds(h * HD, HD)]
-            ).astype(BF16)
+        finish()
+
     sent = [tokens_copy]
     wide_copy.wait()
     for n in (3, 2, 1, 0):
@@ -217,13 +228,13 @@
         copy.wait()
 
 
-def attention(meta, *arrays):
+def attention(*arrays):
     vmem = pl.BlockSpec(memory_space=pltpu.VMEM)
     hbm = pl.BlockSpec(memory_space=pl.ANY)
     shape = jax.ShapeDtypeStruct((2 * FT, 768), BF16)
     return pl.pallas_call(
         kernel,
-        in_specs=[pl.BlockSpec(memory_space=pltpu.SMEM)] + [hbm] * 8 + [vmem] * 10 + [hbm],
+        in_specs=[pl.BlockSpec(memory_space=pltpu.SMEM)] * 3 + [hbm] * 8 + [vmem] * 11 + [hbm],
         out_specs=(hbm,) * 5,
         out_shape=(shape,) * 5,
         scratch_shapes=[
@@ -243,7 +254,7 @@
             pltpu.SemaphoreType.DMA,
         ],
         compiler_params=pltpu.CompilerParams(vmem_limit_bytes=52 * 2**20),
-    )(meta, *arrays)
+    )(*arrays)
 
 
 def permute(x, axis, to):
@@ -312,6 +323,29 @@
     )(lax.axis_index("head").astype(jnp.int32).reshape(1), *parts, gain.reshape(4, 1, columns), wq, wk, wv)
 
 
+def widen_kernel(weight, bias, out):
+    out[:128] = weight[...]
+    b = bias[...]
+    row = lax.broadcasted_iota(jnp.int32, (ROWS - 128, b.shape[1]), 0)
+    b0 = b.astype(BF16).astype(F32)
+    b1 = (b - b0).astype(BF16).astype(F32)
+    b2 = b - b0 - b1
+    parts = jnp.where(row == 0, b0, jnp.where(row == 1, b1, jnp.where(row == 2, b2, 0.0)))
+    out[128:] = parts.astype(BF16)
+
+
+def widen(weight, bias):
+    vmem = pl.BlockSpec(memory_space=pltpu.VMEM)
+    return pl.pallas_call(
+        widen_kernel,
+        in_specs=[vmem] * 2,
+        out_specs=vmem,
+        out_shape=jax.ShapeDtypeStruct((ROWS, weight.shape[1]), BF16),
+        compiler_params=pltpu.CompilerParams(vmem_limit_bytes=2 * 2**20),
+        cost_estimate=pl.CostEstimate(flops=0, bytes_accessed=400000, transcendentals=0),
+    )(weight, bias.reshape(1, -1))
+
+
 def join_kernel(z, p0, p1, p2, p3, out):
     for place in range(4):
         k = (z[0] + 4 - place) % 4
@@ -332,8 +366,8 @@
     )(z.astype(jnp.int32).reshape(1), *parts)
 
 
-def all_latents(latents):
-    seq, core = lax.axis_index("seq"), lax.axis_index("head") % 2
+def all_latents(half):
+    seq = lax.axis_index("seq")
 
     def place(i):
         return i // 8, (i // 4) % 2, i % 4
@@ -353,7 +387,6 @@
         x, y, z = place(i)
         return at((x + k) % 4, y, z)
 
-    half = lax.dynamic_slice_in_dim(latents, core * 32, 32, 0)
     parts = [half] + [permute(half, "seq", functools.partial(to_z, k)) for k in (1, 2, 3)]
     block = join(seq % 4, parts)
     pair = jnp.stack([block, permute(block, "seq", to_y)])
@@ -380,20 +413,11 @@
     out_weight,
 ):
     seq = lax.axis_index("seq")
-    frames = jnp.stack([seq, FRAMES - 1 - seq]).astype(jnp.int32)
-    own_span = jnp.sum(jnp.where(frames[:, None] == jnp.arange(FRAMES)[None], span_ids[None], 0), axis=1)
-    ends = jnp.sum((span_ids[None, :] <= own_span[:, None]).astype(jnp.int32), axis=1)
     head = lax.axis_index("head")
-    places = jnp.stack([seq // 8, (seq // 4) % 2, head % 2, head // 2]).astype(jnp.int32)
-    meta = jnp.concatenate([ends, frames, places])
-
-    halves = all_latents(latents)
-
-    b0 = patch_bias.astype(BF16)
-    b1 = (patch_bias - b0.astype(F32)).astype(BF16)
-    b2 = (patch_bias - b0.astype(F32) - b1.astype(F32)).astype(BF16)
-    rest = jnp.zeros((ROWS - 131, patch_bias.shape[0]), BF16)
-    wide = jnp.concatenate([patch_weight, b0[None], b1[None], b2[None], rest], axis=0)
+    half = lax.dynamic_slice_in_dim(latents, (head % 2) * 32, 32, 0)
+    halves = all_latents(half)
+
+    wide = widen(lax.optimization_barrier((patch_weight, half))[0], patch_bias)
     far_part = swap(wide, 2)
     parts = [wide, swap(wide, 1), far_part, swap(far_part, 1)]
     mg, mq, mv = through(parts, norm_gain, query_weight, key_weight, value_weight)
@@ -410,19 +434,23 @@
     by_block = np.repeat(temporal.reshape(NB, BF, 16).transpose(0, 2, 1), FT, axis=2)
     ct = jnp.asarray(np.cos(by_block), F32)
     st = jnp.asarray(np.sin(by_block), F32)
-    angle = frames.astype(F32)[:, None] * jnp.asarray(w_t, F32)[None]
-
-    def of_queries(turn, space):
-        own = jnp.broadcast_to(turn[:, None, :], (2, FT, 16))
-        return jnp.concatenate([own, jnp.broadcast_to(jnp.asarray(space, F32)[None], (2, FT, 48))], axis=2) * SCALE
-
-    cq = of_queries(jnp.cos(angle), np.cos(spatial))
-    sq = of_queries(jnp.sin(angle), np.sin(spatial))
-    cq = jnp.concatenate([cq, cq], axis=2)
-    sq = jnp.concatenate([-sq, sq], axis=2)
+    nothing = np.zeros((FT, 16))
+    cq = np.concatenate([nothing, np.cos(spatial)], axis=1)
+    sq = np.concatenate([nothing, np.sin(spatial)], axis=1)
+    rest = np.zeros((FRAMES, 48))
+    tc = np.concatenate([np.cos(temporal), rest], axis=1)
+    ts = np.concatenate([np.sin(temporal), rest], axis=1)
+    cq = jnp.asarray(np.concatenate([cq, cq], axis=1) * SCALE, F32)
+    sq = jnp.asarray(np.concatenate([-sq, sq], axis=1) * SCALE, F32)
+    tq = np.stack([np.concatenate([tc, tc], axis=1), np.concatenate([-ts, ts], axis=1)])
+    tq = jnp.asarray(tq * SCALE, F32)
 
     near, near_other, far, far_other, tokens = attention(
-        meta, *pieces, mg, mq, mv, wide, cs, ss, ct, st, cq, sq, out_weight
+        seq.astype(jnp.int32).reshape(1),
+        head.astype(jnp.int32).reshape(1),
+        span_ids,
+        *pieces,
+        *(mg, mq, mv, wide, cs, ss, ct, st, cq, sq, tq, out_weight),
     )
     sent = swap(add(far, swap(far_other, 1)).astype(BF16), 2)
     kept = add(near, swap(near_other, 1)).astype(BF16)

time: 167 us -> 168 us (level)
  other arithmetic: 6.77 us -> 2.32 us
  starting transfers between devices: 18.6 us -> 20.9 us
  Pallas kernels: 118 us -> 120 us
  waiting for transfers between devices: 19.5 us -> 21.5 us
    ppermute x17, starting transfers between devices: 18.6 us -> 20.9 us  [permute(): lax.ppermute(x, axis, [(i, to(i)) for i in range(lax.axis_size(axis))])]
    ppermute x17, waiting for transfers between devices: 19.5 us -> 21.5 us  [permute(): lax.ppermute(x, axis, [(i, to(i)) for i in range(lax.axis_size(axis))])]
    pallas_call x1 -> x2, Pallas kernels: 109 us -> 111 us  [the longest x1 111 us: attention(): pl.pallas_call(kernel, in_specs=[pl.BlockSpec(memory_space=pltpu.SMEM)] *...]
  transfers between devices with their start and end apart: 17 -> 17, of which waited for: 5 -> 7; matrix products, arithmetic and copies ran while one was open for 4% -> 1% of each run, Pallas kernels for 5% -> 5%
where the time goes in v5:
time: 168 us
  Pallas kernels  120 us (71%)
  waiting for transfers between devices  21.5 us (13%)
  starting transfers between devices  20.9 us (12%)
  local copies, waits for them, and re-layouts  3.13 us (2%)
  other arithmetic  2.32 us (1%)
    pallas_call x1, Pallas kernels, attention(): pl.pallas_call(kernel, in_specs=[pl.BlockSpec(memory_space=pltpu.SMEM)] *...  111 us
    ppermute x17, waiting for transfers between devices, permute(): lax.ppermute(x, axis, [(i, to(i)) for i in range(lax.axis_size(axis))])  21.5 us
    ppermute x17, starting transfers between devices, permute(): lax.ppermute(x, axis, [(i, to(i)) for i in range(lax.axis_size(axis))])  20.9 us
    pallas_call x1, Pallas kernels, through(): pl.pallas_call(weights_kernel, grid_spec=pltpu.PrefetchScalarGridSpec(num...  8.74 us
  transfers between devices with their start and end apart: 17, of which 7 were waited for; matrix products, arithmetic and copies ran while one was open for 1% of the time, Pallas kernels for 5%

profile of v5, /device:TPU:1, one launch (start us, length us, event | category | flops | bytes accessed | tf_op | source)
XLA Modules:
  0.0 167.6 jit_solution(17714266925030846289)
XLA Ops:
  0.0 0.7 reshape.19.bias
  0.7 0.1 copy-done
  0.8 0.9 copy-done.2
  1.8 2.2 %collective-permute-start.7 = (bf16[144,768]{1,0:T(8,128)(2,1)S(1)}, bf16[144,768]{1,0:T(8,128)(2,1)S(1)}, u32[]{:S(2)}, u32[]{:S(2)}) collective-permute-start(bf16[144,768]{1,0:T(8,128)(2,1)S(1)} %shard_map.155.p0.refs_11_), channel_id=1, source_target_pairs={{0,2},{1,3},{2,0},{3,1},{4,6},{5,7},{6,4},{7,5},{8,10},{9,11},{10,... | collective-permute-start | bytes 663560 | tf_op jit(solution)/shard_map/ppermute | solution.py:261
  4.0 3.8 %collective-permute-start.2 = (bf16[32,384]{1,0:T(8,128)(2,1)S(1)}, bf16[32,384]{1,0:T(8,128)(2,1)S(1)}, u32[]{:S(2)}, u32[]{:S(2)}) collective-permute-start(bf16[32,384]{1,0:T(8,128)(2,1)S(1)} %constant_dynamic-slice_fusion.p0), channel_id=1, source_target_pairs={{0,12},{4,0},{8,4},{12,8},{16,28},{20,16},{24,20},{28,24},{32,44},... | collective-permute-start | bytes 73736 | tf_op jit(solution)/shard_map/ppermute | solution.py:261
  7.8 0.0 collective-permute-start.1
  7.8 0.7 collective-permute-start
  8.5 1.8 %collective-permute-start.6 = (bf16[144,768]{1,0:T(8,128)(2,1)S(1)}, bf16[144,768]{1,0:T(8,128)(2,1)S(1)}, u32[]{:S(2)}, u32[]{:S(2)}) collective-permute-start(bf16[144,768]{1,0:T(8,128)(2,1)S(1)} %shard_map.155.p0.refs_11_), channel_id=1, source_target_pairs={{0,1},{1,0},{2,3},{3,2},{4,5},{5,4},{6,7},{7,6},{8,9},{9,8},{10,11... | collective-permute-start | bytes 663560 | tf_op jit(solution)/shard_map/ppermute | solution.py:261
  10.3 0.0 collective-permute-done.7.p2
  10.3 0.1 collective-permute-start.8
  10.4 0.0 collective-permute-done.2.p3
  10.4 1.6 collective-permute-done.1.p2
  11.9 0.0 collective-permute-done.p1
  11.9 0.2 shard_map.154
  12.1 2.7 %collective-permute-start.3 = (bf16[2,32,768]{2,1,0:T(8,128)(2,1)S(1)}, bf16[2,32,768]{2,1,0:T(8,128)(2,1)S(1)}, u32[]{:S(2)}, u32[]{:S(2)}) collective-permute-start(bf16[2,32,768]{2,1,0:T(8,128)(2,1)S(1)} %shard_map.154), channel_id=1, source_target_pairs={{0,16},{4,20},{8,24},{12,28},{16,0},{20,4},{24,8},{28,12},{32,48},... | collective-permute-start | bytes 294920 | tf_op jit(solution)/shard_map/ppermute | solution.py:261
  14.8 2.4 %collective-permute-done.3 = bf16[2,32,768]{2,1,0:T(8,128)(2,1)S(1)} collective-permute-done((bf16[2,32,768]{2,1,0:T(8,128)(2,1)S(1)}, bf16[2,32,768]{2,1,0:T(8,128)(2,1)S(1)}, u32[]{:S(2)}, u32[]{:S(2)}) %collective-permute-start.3) | collective-permute-done | bytes 98336 | tf_op jit(solution)/shard_map/ppermute | solution.py:261
  17.2 2.5 %collective-permute-start.12 = (bf16[2,2,32,768]{3,2,1,0:T(8,128)(2,1)S(1)}, bf16[2,2,32,768]{3,2,1,0:T(8,128)(2,1)S(1)}, u32[]{:S(2)}, u32[]{:S(2)}) collective-permute-start(bf16[2,2,32,768]{3,2,1,0:T(8,128)(2,1)S(1)} %pad_maximum_fusion.refs_0_), channel_id=1, source_target_pairs={{0,96},{4,100},{8,104},{12,108},{16,112},{20,116},{24,120},{28,124... | collective-permute-start | bytes 589832 | tf_op jit(solution)/shard_map/ppermute | solution.py:261
  19.7 0.5 collective-permute-start.10
  20.3 0.6 collective-permute-start.5
  20.9 0.0 collective-permute-done.6.p1
  20.9 4.4 %collective-permute-start.4 = (bf16[2,2,32,768]{3,2,1,0:T(8,128)(2,1)S(1)}, bf16[2,2,32,768]{3,2,1,0:T(8,128)(2,1)S(1)}, u32[]{:S(2)}, u32[]{:S(2)}) collective-permute-start(bf16[2,2,32,768]{3,2,1,0:T(8,128)(2,1)S(1)} %pad_maximum_fusion.refs_0_), channel_id=1, source_target_pairs={{0,1},{1,0},{2,3},{3,2},{4,5},{5,4},{6,7},{7,6},{8,9},{9,8},{10,11... | collective-permute-start | bytes 589832 | tf_op jit(solution)/shard_map/ppermute | solution.py:261
  25.2 0.0 collective-permute-done.8.p3
  25.3 0.0 copy-done.12
  25.3 0.7 copy-done.13
  25.9 0.0 copy-start.7
  26.0 0.0 copy-start.8
  26.0 8.7 %shard_map.156 = (bf16[1056,144]{1,0:T(8,128)(2,1)}, bf16[144,768]{1,0:T(8,128)(2,1)}, bf16[144,768]{1,0:T(8,128)(2,1)}) custom-call(s32[1]{0:T(128)} %bitcast.1.me.head_ref, bf16[144,768]{1,0:T(8,128)(2,1)} %copy-done.1, bf16[144,768]{1,0:T(8,128)(2,1)} %copy-done.12, bf16[144,768]{1,0:T(8,128)(2,1)} %copy-done.11, bf16[144,768]{1,0:T(8,128)(2,1)} %copy-done.13, ...), custom_call_target="tpu_custom_call" | custom-call | flops 2123366400 | bytes 14155776 | tf_op jit(solution)/shard_map/pallas_call | solution.py:299
  34.7 0.0 collective-permute-done.12.refs_6_
  34.7 0.0 collective-permute-done.10.refs_4_
  34.7 0.0 collective-permute-done.5.refs_2_
  34.7 0.1 collective-permute-start.9
  34.9 0.4 collective-permute-start.11
  35.3 0.1 collective-permute-start.13
  35.4 0.0 collective-permute-done.4.refs_1_
  35.4 0.8 collective-permute-done.9.refs_3_
  36.3 0.3 collective-permute-done.11.refs_5_
  36.5 0.3 collective-permute-done.13.refs_7_
  36.8 0.7 copy-done.14
  37.5 110.7 %shard_map.157 = (bf16[384,768]{1,0:T(8,128)(2,1)}, bf16[384,768]{1,0:T(8,128)(2,1)}, bf16[384,768]{1,0:T(8,128)(2,1)}, bf16[384,768]{1,0:T(8,128)(2,1)}, bf16[384,768]{1,0:T(8,128)(2,1)}) custom-call(s32[1]{0:T(128)} %bitcast.seq_ref, s32[1]{0:T(128)} %bitcast.1.me.head_ref, s32[64]{0:T(128)S(1)} %copy-done.8, ...), custom_call_target="tpu_custom_call" | custom-call | tf_op jit(solution)/shard_map/pallas_call | solution.py:235
  148.2 0.0 copy-start.9
  148.2 0.3 collective-permute-start.15
  148.5 0.3 collective-permute-start.14
  148.8 1.7 %collective-permute-done.15 = bf16[384,768]{1,0:T(8,128)(2,1)S(1)} collective-permute-done((bf16[384,768]{1,0:T(8,128)(2,1)}, bf16[384,768]{1,0:T(8,128)(2,1)S(1)}, u32[]{:S(2)}, u32[]{:S(2)}) %collective-permute-start.15) | collective-permute-done | bytes 589856 | tf_op jit(solution)/shard_map/ppermute | solution.py:261
  150.5 1.2 add_convert_fusion.1
  151.7 0.3 collective-permute-start.16
  152.0 0.0 collective-permute-done.14
  152.0 14.5 %collective-permute-done.16 = bf16[384,768]{1,0:T(8,128)(2,1)S(1)} collective-permute-done((bf16[384,768]{1,0:T(8,128)(2,1)S(1)}, bf16[384,768]{1,0:T(8,128)(2,1)S(1)}, u32[]{:S(2)}, u32[]{:S(2)}) %collective-permute-start.16) | collective-permute-done | bytes 589856 | tf_op jit(solution)/shard_map/ppermute | solution.py:261
  166.5 1.1 add_convert_fusion
  (25 shorter events, 0.1 us)
Async XLA Ops:
  0.0 0.8 copy-start
  0.8 0.9 copy-start.2
  1.8 23.5 %copy-start.1 = (bf16[144,768]{1,0:T(8,128)(2,1)}, bf16[144,768]{1,0:T(8,128)(2,1)S(1)}, u32[]{:S(2)}) copy-start(bf16[144,768]{1,0:T(8,128)(2,1)S(1)} %shard_map.155.p0.refs_11_) | copy-start | bytes 663556
  1.8 8.5 %collective-permute-start.7 = (bf16[144,768]{1,0:T(8,128)(2,1)S(1)}, bf16[144,768]{1,0:T(8,128)(2,1)S(1)}, u32[]{:S(2)}, u32[]{:S(2)}) collective-permute-start(bf16[144,768]{1,0:T(8,128)(2,1)S(1)} %shard_map.155.p0.refs_11_), channel_id=1, source_target_pairs={{0,2},{1,3},{2,0},{3,1},{4,6},{5,7},{6,4},{7,5},{8,10},{9,11},{10,... | collective-permute-start | bytes 663560 | tf_op jit(solution)/shard_map/ppermute | solution.py:261
  4.0 6.4 %collective-permute-start.2 = (bf16[32,384]{1,0:T(8,128)(2,1)S(1)}, bf16[32,384]{1,0:T(8,128)(2,1)S(1)}, u32[]{:S(2)}, u32[]{:S(2)}) collective-permute-start(bf16[32,384]{1,0:T(8,128)(2,1)S(1)} %constant_dynamic-slice_fusion.p0), channel_id=1, source_target_pairs={{0,12},{4,0},{8,4},{12,8},{16,28},{20,16},{24,20},{28,24},{32,44},... | collective-permute-start | bytes 73736 | tf_op jit(solution)/shard_map/ppermute | solution.py:261
  7.8 4.2 %collective-permute-start.1 = (bf16[32,384]{1,0:T(8,128)(2,1)S(1)}, bf16[32,384]{1,0:T(8,128)(2,1)S(1)}, u32[]{:S(2)}, u32[]{:S(2)}) collective-permute-start(bf16[32,384]{1,0:T(8,128)(2,1)S(1)} %constant_dynamic-slice_fusion.p0), channel_id=1, source_target_pairs={{0,8},{4,12},{8,0},{12,4},{16,24},{20,28},{24,16},{28,20},{32,40},... | collective-permute-start | bytes 73736 | tf_op jit(solution)/shard_map/ppermute | solution.py:261
  7.8 4.2 %collective-permute-start = (bf16[32,384]{1,0:T(8,128)(2,1)S(1)}, bf16[32,384]{1,0:T(8,128)(2,1)S(1)}, u32[]{:S(2)}, u32[]{:S(2)}) collective-permute-start(bf16[32,384]{1,0:T(8,128)(2,1)S(1)} %constant_dynamic-slice_fusion.p0), channel_id=1, source_target_pairs={{0,4},{4,8},{8,12},{12,0},{16,20},{20,24},{24,28},{28,16},{32,36},... | collective-permute-start | bytes 73736 | tf_op jit(solution)/shard_map/ppermute | solution.py:261
  8.5 12.4 %collective-permute-start.6 = (bf16[144,768]{1,0:T(8,128)(2,1)S(1)}, bf16[144,768]{1,0:T(8,128)(2,1)S(1)}, u32[]{:S(2)}, u32[]{:S(2)}) collective-permute-start(bf16[144,768]{1,0:T(8,128)(2,1)S(1)} %shard_map.155.p0.refs_11_), channel_id=1, source_target_pairs={{0,1},{1,0},{2,3},{3,2},{4,5},{5,4},{6,7},{7,6},{8,9},{9,8},{10,11... | collective-permute-start | bytes 663560 | tf_op jit(solution)/shard_map/ppermute | solution.py:261
  10.3 15.0 %copy-start.11 = (bf16[144,768]{1,0:T(8,128)(2,1)}, bf16[144,768]{1,0:T(8,128)(2,1)S(1)}, u32[]{:S(2)}) copy-start(bf16[144,768]{1,0:T(8,128)(2,1)S(1)} %collective-permute-done.7.p2) | copy-start | bytes 663556
  10.3 15.0 %collective-permute-start.8 = (bf16[144,768]{1,0:T(8,128)(2,1)S(1)}, bf16[144,768]{1,0:T(8,128)(2,1)S(1)}, u32[]{:S(2)}, u32[]{:S(2)}) collective-permute-start(bf16[144,768]{1,0:T(8,128)(2,1)S(1)} %collective-permute-done.7.p2), channel_id=1, source_target_pairs={{0,1},{1,0},{2,3},{3,2},{4,5},{5,4},{6,7},{7,6},{8,9},{9,8},{10,11... | collective-permute-start | bytes 663560 | tf_op jit(solution)/shard_map/ppermute | solution.py:261
  12.1 5.1 %collective-permute-start.3 = (bf16[2,32,768]{2,1,0:T(8,128)(2,1)S(1)}, bf16[2,32,768]{2,1,0:T(8,128)(2,1)S(1)}, u32[]{:S(2)}, u32[]{:S(2)}) collective-permute-start(bf16[2,32,768]{2,1,0:T(8,128)(2,1)S(1)} %shard_map.154), channel_id=1, source_target_pairs={{0,16},{4,20},{8,24},{12,28},{16,0},{20,4},{24,8},{28,12},{32,48},... | collective-permute-start | bytes 294920 | tf_op jit(solution)/shard_map/ppermute | solution.py:261
  17.2 17.5 %collective-permute-start.12 = (bf16[2,2,32,768]{3,2,1,0:T(8,128)(2,1)S(1)}, bf16[2,2,32,768]{3,2,1,0:T(8,128)(2,1)S(1)}, u32[]{:S(2)}, u32[]{:S(2)}) collective-permute-start(bf16[2,2,32,768]{3,2,1,0:T(8,128)(2,1)S(1)} %pad_maximum_fusion.refs_0_), channel_id=1, source_target_pairs={{0,96},{4,100},{8,104},{12,108},{16,112},{20,116},{24,120},{28,124... | collective-permute-start | bytes 589832 | tf_op jit(solution)/shard_map/ppermute | solution.py:261
  19.7 15.0 %collective-permute-start.10 = (bf16[2,2,32,768]{3,2,1,0:T(8,128)(2,1)S(1)}, bf16[2,2,32,768]{3,2,1,0:T(8,128)(2,1)S(1)}, u32[]{:S(2)}, u32[]{:S(2)}) collective-permute-start(bf16[2,2,32,768]{3,2,1,0:T(8,128)(2,1)S(1)} %pad_maximum_fusion.refs_0_), channel_id=1, source_target_pairs={{0,64},{4,68},{8,72},{12,76},{16,80},{20,84},{24,88},{28,92},{32,9... | collective-permute-start | bytes 589832 | tf_op jit(solution)/shard_map/ppermute | solution.py:261
  20.3 14.5 %collective-permute-start.5 = (bf16[2,2,32,768]{3,2,1,0:T(8,128)(2,1)S(1)}, bf16[2,2,32,768]{3,2,1,0:T(8,128)(2,1)S(1)}, u32[]{:S(2)}, u32[]{:S(2)}) collective-permute-start(bf16[2,2,32,768]{3,2,1,0:T(8,128)(2,1)S(1)} %pad_maximum_fusion.refs_0_), channel_id=1, source_target_pairs={{0,32},{4,36},{8,40},{12,44},{16,48},{20,52},{24,56},{28,60},{32,6... | collective-permute-start | bytes 589832 | tf_op jit(solution)/shard_map/ppermute | solution.py:261
  20.9 4.4 %copy-start.12 = (bf16[144,768]{1,0:T(8,128)(2,1)}, bf16[144,768]{1,0:T(8,128)(2,1)S(1)}, u32[]{:S(2)}) copy-start(bf16[144,768]{1,0:T(8,128)(2,1)S(1)} %collective-permute-done.6.p1) | copy-start | bytes 663556
  20.9 14.6 %collective-permute-start.4 = (bf16[2,2,32,768]{3,2,1,0:T(8,128)(2,1)S(1)}, bf16[2,2,32,768]{3,2,1,0:T(8,128)(2,1)S(1)}, u32[]{:S(2)}, u32[]{:S(2)}) collective-permute-start(bf16[2,2,32,768]{3,2,1,0:T(8,128)(2,1)S(1)} %pad_maximum_fusion.refs_0_), channel_id=1, source_target_pairs={{0,1},{1,0},{2,3},{3,2},{4,5},{5,4},{6,7},{7,6},{8,9},{9,8},{10,11... | collective-permute-start | bytes 589832 | tf_op jit(solution)/shard_map/ppermute | solution.py:261
  25.2 0.7 copy-start.13
  25.9 11.6 %copy-start.3 = (f32[48,768]{1,0:T(8,128)S(1)}, f32[48,768]{1,0:T(8,128)}, u32[]{:S(2)}) copy-start(f32[48,768]{1,0:T(8,128)} %constant.52.clone.refs_13_) | copy-start | bytes 442372
  25.9 11.6 %copy-start.4 = (f32[48,768]{1,0:T(8,128)S(1)}, f32[48,768]{1,0:T(8,128)}, u32[]{:S(2)}) copy-start(f32[48,768]{1,0:T(8,128)} %constant.51.clone.refs_12_) | copy-start | bytes 442372
  25.9 11.6 %copy-start.5 = (f32[192,128]{1,0:T(8,128)S(1)}, f32[192,128]{1,0:T(8,128)}, u32[]{:S(2)}) copy-start(f32[192,128]{1,0:T(8,128)} %constant.56.clone.refs_17_) | copy-start | bytes 294916
  25.9 11.6 %copy-start.6 = (f32[192,128]{1,0:T(8,128)S(1)}, f32[192,128]{1,0:T(8,128)}, u32[]{:S(2)}) copy-start(f32[192,128]{1,0:T(8,128)} %constant.55.clone.refs_16_) | copy-start | bytes 294916
  25.9 11.6 %copy-start.7 = (f32[2,64,128]{2,1,0:T(8,128)S(1)}, f32[2,64,128]{2,1,0:T(8,128)}, u32[]{:S(2)}) copy-start(f32[2,64,128]{2,1,0:T(8,128)} %constant.57.clone.refs_18_) | copy-start | bytes 196612
  26.0 11.6 %copy-start.8 = (s32[64]{0:T(128)S(1)}, s32[64]{0:T(128)}, u32[]{:S(2)}) copy-start(s32[64]{0:T(128)} %span_ref.1) | copy-start | bytes 772
  34.7 1.5 collective-permute-start.9
  34.9 1.7 collective-permute-start.11
  35.3 1.5 collective-permute-start.13
  36.8 0.7 copy-start.14
  148.2 18.3 %copy-start.9 = (bf16[384,768]{1,0:T(8,128)(2,1)S(1)}, bf16[384,768]{1,0:T(8,128)(2,1)}, u32[]{:S(2)}) copy-start(bf16[384,768]{1,0:T(8,128)(2,1)} %get-tuple-element.24) | copy-start | bytes 1769476
  148.2 18.3 %copy-start.10 = (bf16[384,768]{1,0:T(8,128)(2,1)S(1)}, bf16[384,768]{1,0:T(8,128)(2,1)}, u32[]{:S(2)}) copy-start(bf16[384,768]{1,0:T(8,128)(2,1)} %get-tuple-element.28) | copy-start | bytes 1769476
  148.2 2.3 %collective-permute-start.15 = (bf16[384,768]{1,0:T(8,128)(2,1)}, bf16[384,768]{1,0:T(8,128)(2,1)S(1)}, u32[]{:S(2)}, u32[]{:S(2)}) collective-permute-start(bf16[384,768]{1,0:T(8,128)(2,1)} %get-tuple-element.27), channel_id=1, source_target_pairs={{0,1},{1,0},{2,3},{3,2},{4,5},{5,4},{6,7},{7,6},{8,9},{9,8},{10,11... | collective-permute-start | bytes 1769480 | tf_op jit(solution)/shard_map/ppermute | solution.py:261
  148.5 3.5 %collective-permute-start.14 = (bf16[384,768]{1,0:T(8,128)(2,1)}, bf16[384,768]{1,0:T(8,128)(2,1)S(1)}, u32[]{:S(2)}, u32[]{:S(2)}) collective-permute-start(bf16[384,768]{1,0:T(8,128)(2,1)} %get-tuple-element.25), channel_id=1, source_target_pairs={{0,1},{1,0},{2,3},{3,2},{4,5},{5,4},{6,7},{7,6},{8,9},{9,8},{10,11... | collective-permute-start | bytes 1769480 | tf_op jit(solution)/shard_map/ppermute | solution.py:261
  151.7 14.8 %collective-permute-start.16 = (bf16[384,768]{1,0:T(8,128)(2,1)S(1)}, bf16[384,768]{1,0:T(8,128)(2,1)S(1)}, u32[]{:S(2)}, u32[]{:S(2)}) collective-permute-start(bf16[384,768]{1,0:T(8,128)(2,1)S(1)} %add_convert_fusion.1), channel_id=1, source_target_pairs={{0,2},{1,3},{2,0},{3,1},{4,6},{5,7},{6,4},{7,5},{8,10},{9,11},{10,... | collective-permute-start | bytes 1769480 | tf_op jit(solution)/shard_map/ppermute | solution.py:261

commit v6 on v5

--- a/solution.py
+++ b/solution.py
@@ -60,13 +60,6 @@
     seq, head = seq_ref[0], head_ref[0]
     own_frames = (seq, FRAMES - 1 - seq)
 
-    def end_of(frame):
-        count = lambda g, seen: seen + (span_ref[g] <= span_ref[frame]).astype(jnp.int32)
-        return lax.fori_loop(0, FRAMES, count, 0)
-
-    end_early, end_late = end_of(own_frames[0]), end_of(own_frames[1])
-    blocks_early = (end_early + BF - 1) // BF
-    blocks_late = (end_late + BF - 1) // BF
     wide_copy = pltpu.make_async_copy(wo_ref, wide_ref, wide_sem)
     wide_copy.start()
     x_at, y_at, core, chip = seq // 8, (seq // 4) % 2, head % 2, head // 2
@@ -88,6 +81,14 @@
                     )
     for copy in copies:
         copy.start()
+
+    def end_of(frame):
+        count = lambda g, seen: seen + (span_ref[g] <= span_ref[frame]).astype(jnp.int32)
+        return lax.fori_loop(0, FRAMES, count, 0, unroll=True)
+
+    end_early, end_late = end_of(own_frames[0]), end_of(own_frames[1])
+    blocks_early = (end_early + BF - 1) // BF
+    blocks_late = (end_late + BF - 1) // BF
     for copy in copies:
         copy.wait()
 
@@ -261,15 +262,17 @@
     return lax.ppermute(x, axis, [(i, to(i)) for i in range(lax.axis_size(axis))])
 
 
-def weights_kernel(me, p0, p1, p2, p3, gain, wq, wk, wv, mg_ref, mq_ref, mv_ref, aq, ak, av, ag):
+def weights_kernel(first, me, p0, p1, gain, wq, wk, wv, *refs):
     k = pl.program_id(0)
+    sums = refs[:4] if first else refs[7:]
 
     @pl.when(k == 0)
     def _():
-        for ref in (aq, ak, av, ag):
-            ref[...] = jnp.zeros_like(ref)
-
-    part = jnp.where(k < 2, jnp.where(k == 0, p0[...], p1[...]), jnp.where(k == 2, p2[...], p3[...]))
+        for n, ref in enumerate(sums):
+            ref[...] = jnp.zeros_like(ref) if first else refs[n][...]
+
+    aq, ak, av, ag = sums
+    part = jnp.where(k == 0, p0[...], p1[...])
     wide = part.astype(F32)
     bias = wide[128:129] + wide[129:130] + wide[130:131]
     row = lax.broadcasted_iota(jnp.int32, (ROWS - 128, part.shape[1]), 0)
@@ -279,8 +282,11 @@
     ak[...] += dot(gained, wk[...])
     av[...] += dot(gained, wv[...])
     ag[...] += lax.dot_general(part, part, (((1,), (1,)), ((), ())), preferred_element_type=F32)
-
-    @pl.when(k == 3)
+    if first:
+        return
+    mg_ref, mq_ref, mv_ref = refs[4:7]
+
+    @pl.when(k == 1)
     def _():
         mq_ref[...] = aq[...].astype(BF16)
         mv_ref[...] = av[...].astype(BF16)
@@ -291,59 +297,36 @@
         mg_ref[HEADS * HD + ROWS :, :] = (gram - high.astype(F32)).astype(BF16)
 
 
-def through(parts, gain, wq, wk, wv):
-    columns = HEADS * HD
+def through(parts, gain, wq, wk, wv, sums=()):
+    columns, first = HEADS * HD, not sums
     whole = lambda *shape: pl.BlockSpec(shape, lambda k, me: (0,) * len(shape))
-    source = lambda k, me: me[0] ^ k
+    source = lambda k, me: me[0] ^ (k if first else k + 2)
     weight = pl.BlockSpec((columns, columns), lambda k, me: (source(k, me), 0))
+    sizes = [(ROWS, columns)] * 3 + [(ROWS, ROWS)]
+    results = sizes if first else [(columns + 2 * ROWS, ROWS), (ROWS, columns), (ROWS, columns)]
     return pl.pallas_call(
-        weights_kernel,
+        functools.partial(weights_kernel, first),
         grid_spec=pltpu.PrefetchScalarGridSpec(
             num_scalar_prefetch=1,
-            grid=(4,),
-            in_specs=[whole(ROWS, columns)] * 4
+            grid=(2,),
+            in_specs=[whole(ROWS, columns)] * 2
             + [pl.BlockSpec((1, 1, columns), lambda k, me: (source(k, me), 0, 0))]
-            + [weight] * 3,
-            out_specs=[
-                whole(columns + 2 * ROWS, ROWS),
-                whole(ROWS, columns),
-                whole(ROWS, columns),
-            ],
-            scratch_shapes=[pltpu.VMEM((ROWS, columns), F32)] * 3 + [pltpu.VMEM((ROWS, ROWS), F32)],
+            + [weight] * 3
+            + ([] if first else [whole(*size) for size in sizes]),
+            out_specs=[whole(*size) for size in results],
+            scratch_shapes=[] if first else [pltpu.VMEM(size, F32) for size in sizes],
         ),
-        out_shape=[
-            jax.ShapeDtypeStruct((columns + 2 * ROWS, ROWS), BF16),
-            jax.ShapeDtypeStruct((ROWS, columns), BF16),
-            jax.ShapeDtypeStruct((ROWS, columns), BF16),
-        ],
+        out_shape=[jax.ShapeDtypeStruct(size, F32 if first else BF16) for size in results],
         compiler_params=pltpu.CompilerParams(vmem_limit_bytes=57 * 2**20),
         cost_estimate=pl.CostEstimate(
-            flops=2 * ROWS * 3072 * 2400, bytes_accessed=3 * 3072 * 768 * 2, transcendentals=0
+            flops=ROWS * 3072 * 2400, bytes_accessed=3 * 1536 * 768 * 2, transcendentals=0
         ),
-    )(lax.axis_index("head").astype(jnp.int32).reshape(1), *parts, gain.reshape(4, 1, columns), wq, wk, wv)
-
-
-def widen_kernel(weight, bias, out):
-    out[:128] = weight[...]
-    b = bias[...]
-    row = lax.broadcasted_iota(jnp.int32, (ROWS - 128, b.shape[1]), 0)
-    b0 = b.astype(BF16).astype(F32)
-    b1 = (b - b0).astype(BF16).astype(F32)
-    b2 = b - b0 - b1
-    parts = jnp.where(row == 0, b0, jnp.where(row == 1, b1, jnp.where(row == 2, b2, 0.0)))
-    out[128:] = parts.astype(BF16)
-
-
-def widen(weight, bias):
-    vmem = pl.BlockSpec(memory_space=pltpu.VMEM)
-    return pl.pallas_call(
-        widen_kernel,
-        in_specs=[vmem] * 2,
-        out_specs=vmem,
-        out_shape=jax.ShapeDtypeStruct((ROWS, weight.shape[1]), BF16),
-        compiler_params=pltpu.CompilerParams(vmem_limit_bytes=2 * 2**20),
-        cost_estimate=pl.CostEstimate(flops=0, bytes_accessed=400000, transcendentals=0),
-    )(weight, bias.reshape(1, -1))
+    )(
+        lax.axis_index("head").astype(jnp.int32).reshape(1),
+        *parts,
+        gain.reshape(4, 1, columns),
+        *(wq, wk, wv, *sums),
+    )
 
 
 def join_kernel(z, p0, p1, p2, p3, out):
@@ -366,7 +349,7 @@
     )(z.astype(jnp.int32).reshape(1), *parts)
 
 
-def all_latents(half):
+def all_latents(half, beside):
     seq = lax.axis_index("seq")
 
     def place(i):
@@ -389,7 +372,8 @@
 
     parts = [half] + [permute(half, "seq", functools.partial(to_z, k)) for k in (1, 2, 3)]
     block = join(seq % 4, parts)
-    pair = jnp.stack([block, permute(block, "seq", to_y)])
+    received = lax.optimization_barrier((permute(block, "seq", to_y), *beside))[0]
+    pair = jnp.stack([block, received])
     return [pair] + [permute(pair, "seq", functools.partial(to_x, k)) for k in (1, 2, 3)]
 
 
@@ -415,12 +399,17 @@
     seq = lax.axis_index("seq")
     head = lax.axis_index("head")
     half = lax.dynamic_slice_in_dim(latents, (head % 2) * 32, 32, 0)
-    halves = all_latents(half)
-
-    wide = widen(lax.optimization_barrier((patch_weight, half))[0], patch_bias)
+
+    b0 = patch_bias.astype(BF16)
+    b1 = (patch_bias - b0.astype(F32)).astype(BF16)
+    b2 = (patch_bias - b0.astype(F32) - b1.astype(F32)).astype(BF16)
+    rest = jnp.zeros((ROWS - 131, patch_bias.shape[0]), BF16)
+    wide = jnp.concatenate([patch_weight, b0[None], b1[None], b2[None], rest], axis=0)
     far_part = swap(wide, 2)
-    parts = [wide, swap(wide, 1), far_part, swap(far_part, 1)]
-    mg, mq, mv = through(parts, norm_gain, query_weight, key_weight, value_weight)
+    projections = norm_gain, query_weight, key_weight, value_weight
+    sums = through([wide, swap(wide, 1)], *projections)
+    halves = all_latents(half, sums)
+    mg, mq, mv = through([far_part, swap(far_part, 1)], *projections, tuple(sums))
     others = [swap(halves[0], 1)] + [
         swap(lax.optimization_barrier((part, mq))[0], 1) for part in halves[1:]
     ]

time: 168 us -> 171 us (1.018)
  waiting for transfers between devices: 21.5 us -> 25.1 us
  starting transfers between devices: 20.9 us -> 18.4 us
    ppermute x17, waiting for transfers between devices: 21.5 us -> 25.1 us  [permute(): lax.ppermute(x, axis, [(i, to(i)) for i in range(lax.axis_size(axis))])]
    ppermute x17, starting transfers between devices: 20.9 us -> 18.4 us  [permute(): lax.ppermute(x, axis, [(i, to(i)) for i in range(lax.axis_size(axis))])]
    pallas_call x2, Pallas kernels: 8.78 us -> 10.6 us  [through(): pl.pallas_call(functools.partial(weights_kernel, first), grid_spec=pltpu....]
  transfers between devices with their start and end apart: 17 -> 17, of which waited for: 7 -> 8; matrix products, arithmetic and copies ran while one was open for 1% -> 1% of each run, Pallas kernels for 5% -> 6%
where the time goes in v6:
time: 171 us; the launch traced here: 170 us
  Pallas kernels  120 us (70%)
  waiting for transfers between devices  25.1 us (15%)
  starting transfers between devices  18.4 us (11%)
  local copies, waits for them, and re-layouts  3.27 us (2%)
  other arithmetic  3.09 us (2%)
    pallas_call x1, Pallas kernels, attention(): pl.pallas_call(kernel, in_specs=[pl.BlockSpec(memory_space=pltpu.SMEM)] *...  109 us
    ppermute x17, waiting for transfers between devices, permute(): lax.ppermute(x, axis, [(i, to(i)) for i in range(lax.axis_size(axis))])  25.1 us
    ppermute x17, starting transfers between devices, permute(): lax.ppermute(x, axis, [(i, to(i)) for i in range(lax.axis_size(axis))])  18.4 us
    pallas_call x2, Pallas kernels, through(): pl.pallas_call(functools.partial(weights_kernel, first), grid_spec=pltpu....  10.6 us
  transfers between devices with their start and end apart: 17, of which 8 were waited for; matrix products, arithmetic and copies ran while one was open for 1% of the time, Pallas kernels for 6%

profile of v6, /device:TPU:1, one launch (start us, length us, event | category | flops | bytes accessed | tf_op | source)
XLA Modules:
  0.0 170.3 jit_solution(12558033942482470593)
XLA Ops:
  0.0 0.8 subtract_convert_fusion
  0.8 1.1 concatenate.3.p0.refs_11_
  2.0 2.2 %collective-permute-start.7 = (bf16[144,768]{1,0:T(8,128)(2,1)S(1)}, bf16[144,768]{1,0:T(8,128)(2,1)S(1)}, u32[]{:S(2)}, u32[]{:S(2)}) collective-permute-start(bf16[144,768]{1,0:T(8,128)(2,1)S(1)} %concatenate.3.p0.refs_11_), channel_id=1, source_target_pairs={{0,2},{1,3},{2,0},{3,1},{4,6},{5,7},{6,4},{7,5},{8,10},{9,11},{10,... | collective-permute-start | bytes 663560 | tf_op jit(solution)/shard_map/ppermute | solution.py:262
  4.2 1.0 collective-permute-start.4
  5.1 3.8 %collective-permute-start.2 = (bf16[32,384]{1,0:T(8,128)(2,1)S(1)}, bf16[32,384]{1,0:T(8,128)(2,1)S(1)}, u32[]{:S(2)}, u32[]{:S(2)}) collective-permute-start(bf16[32,384]{1,0:T(8,128)(2,1)S(1)} %constant_dynamic-slice_fusion.p0), channel_id=1, source_target_pairs={{0,12},{4,0},{8,4},{12,8},{16,28},{20,16},{24,20},{28,24},{32,44},... | collective-permute-start | bytes 73736 | tf_op jit(solution)/shard_map/ppermute | solution.py:262
  8.9 0.0 collective-permute-start.1
  8.9 0.7 collective-permute-start
  9.6 0.2 collective-permute-done.2.p3
  9.8 3.2 %collective-permute-done.1.p2 = bf16[32,384]{1,0:T(8,128)(2,1)S(1)} collective-permute-done((bf16[32,384]{1,0:T(8,128)(2,1)S(1)}, bf16[32,384]{1,0:T(8,128)(2,1)S(1)}, u32[]{:S(2)}, u32[]{:S(2)}) %collective-permute-start.1) | collective-permute-done | bytes 24608 | tf_op jit(solution)/shard_map/ppermute | solution.py:262
  13.1 0.0 collective-permute-done.p1
  13.1 0.2 shard_map.154
  13.2 2.7 %collective-permute-start.3 = (bf16[2,32,768]{2,1,0:T(8,128)(2,1)S(1)}, bf16[2,32,768]{2,1,0:T(8,128)(2,1)S(1)}, u32[]{:S(2)}, u32[]{:S(2)}) collective-permute-start(bf16[2,32,768]{2,1,0:T(8,128)(2,1)S(1)} %shard_map.154), channel_id=1, source_target_pairs={{0,16},{4,20},{8,24},{12,28},{16,0},{20,4},{24,8},{28,12},{32,48},... | collective-permute-start | bytes 294920 | tf_op jit(solution)/shard_map/ppermute | solution.py:262
  15.9 0.0 collective-permute-done.7.p0
  16.0 1.8 %collective-permute-start.8 = (bf16[144,768]{1,0:T(8,128)(2,1)S(1)}, bf16[144,768]{1,0:T(8,128)(2,1)S(1)}, u32[]{:S(2)}, u32[]{:S(2)}) collective-permute-start(bf16[144,768]{1,0:T(8,128)(2,1)S(1)} %collective-permute-done.7.p0), channel_id=1, source_target_pairs={{0,1},{1,0},{2,3},{3,2},{4,5},{5,4},{6,7},{7,6},{8,9},{9,8},{10,11... | collective-permute-start | bytes 663560 | tf_op jit(solution)/shard_map/ppermute | solution.py:262
  17.7 0.7 copy-done.12
  18.4 4.9 %shard_map.155 = (f32[144,768]{1,0:T(8,128)}, f32[144,768]{1,0:T(8,128)}, f32[144,768]{1,0:T(8,128)}, f32[144,144]{1,0:T(8,128)}) custom-call(s32[1]{0:T(128)} %bitcast.1.me.head_ref, bf16[144,768]{1,0:T(8,128)(2,1)} %copy-done.7, bf16[144,768]{1,0:T(8,128)(2,1)} %copy-done.12, f32[4,1,768]{2,1,0:T(1,128)} %bitcast.8, bf16[3072,768]{1,0:T(8,128)(2,1)} %wq.3, ...), custom_call_target="tpu_custom_call" | custom-call | flops 1061683200 | bytes 7077888 | tf_op jit(solution)/shard_map/pallas_call | solution.py:307
  23.3 0.0 collective-permute-done.3
  23.4 0.0 copy-start.1
  23.4 0.0 copy-start.2
  23.4 0.0 copy-start.3
  23.4 0.0 copy-start.4
  23.4 0.0 copy-start.5
  23.4 0.0 copy-start.6
  23.5 2.5 %collective-permute-start.12 = (bf16[2,2,32,768]{3,2,1,0:T(8,128)(2,1)S(1)}, bf16[2,2,32,768]{3,2,1,0:T(8,128)(2,1)S(1)}, u32[]{:S(2)}, u32[]{:S(2)}) collective-permute-start(bf16[2,2,32,768]{3,2,1,0:T(8,128)(2,1)S(1)} %pad_maximum_fusion.refs_0_), channel_id=1, source_target_pairs={{0,96},{4,100},{8,104},{12,108},{16,112},{20,116},{24,120},{28,124... | collective-permute-start | bytes 589832 | tf_op jit(solution)/shard_map/ppermute | solution.py:262
  26.0 0.5 collective-permute-start.10
  26.5 0.6 collective-permute-start.6
  27.1 0.9 collective-permute-start.5
  28.0 0.0 collective-permute-done.8.p1
  28.0 0.7 copy-done.11
  28.7 5.7 %shard_map.156 = (bf16[1056,144]{1,0:T(8,128)(2,1)}, bf16[144,768]{1,0:T(8,128)(2,1)}, bf16[144,768]{1,0:T(8,128)(2,1)}) custom-call(s32[1]{0:T(128)} %bitcast.1.me.head_ref, bf16[144,768]{1,0:T(8,128)(2,1)} %copy-done.10, bf16[144,768]{1,0:T(8,128)(2,1)} %copy-done.11, f32[4,1,768]{2,1,0:T(1,128)} %bitcast.9, bf16[3072,768]{1,0:T(8,128)(2,1)} %wq.3, ...), custom_call_target="tpu_custom_call" | custom-call | flops 1061683200 | bytes 7077888 | tf_op jit(solution)/shard_map/pallas_call | solution.py:307
  34.4 0.0 collective-permute-done.10.refs_4_
  34.4 4.1 %collective-permute-done.6.refs_2_ = bf16[2,2,32,768]{3,2,1,0:T(8,128)(2,1)S(1)} collective-permute-done((bf16[2,2,32,768]{3,2,1,0:T(8,128)(2,1)S(1)}, bf16[2,2,32,768]{3,2,1,0:T(8,128)(2,1)S(1)}, u32[]{:S(2)}, u32[]{:S(2)}) %collective-permute-start.6) | collective-permute-done | bytes 196640 | tf_op jit(solution)/shard_map/ppermute | solution.py:262
  38.5 0.5 collective-permute-start.9
  39.0 0.0 collective-permute-start.11
  39.1 0.5 collective-permute-start.13
  39.6 0.6 collective-permute-done.9.refs_3_
  40.1 0.4 collective-permute-done.11.refs_5_
  40.5 0.3 collective-permute-done.13.refs_7_
  40.8 0.7 copy-done.13
  41.5 109.5 %shard_map.157 = (bf16[384,768]{1,0:T(8,128)(2,1)}, bf16[384,768]{1,0:T(8,128)(2,1)}, bf16[384,768]{1,0:T(8,128)(2,1)}, bf16[384,768]{1,0:T(8,128)(2,1)}, bf16[384,768]{1,0:T(8,128)(2,1)}) custom-call(s32[1]{0:T(128)} %bitcast.seq_ref, s32[1]{0:T(128)} %bitcast.1.me.head_ref, s32[64]{0:T(128)S(1)} %copy-done.6, ...), custom_call_target="tpu_custom_call" | custom-call | tf_op jit(solution)/shard_map/pallas_call | solution.py:236
  150.9 0.0 copy-start.8
  151.0 0.4 collective-permute-start.15
  151.4 0.2 collective-permute-start.14
  151.6 1.7 %collective-permute-done.15 = bf16[384,768]{1,0:T(8,128)(2,1)S(1)} collective-permute-done((bf16[384,768]{1,0:T(8,128)(2,1)}, bf16[384,768]{1,0:T(8,128)(2,1)S(1)}, u32[]{:S(2)}, u32[]{:S(2)}) %collective-permute-start.15) | collective-permute-done | bytes 589856 | tf_op jit(solution)/shard_map/ppermute | solution.py:262
  153.3 1.2 add_convert_fusion.1
  154.5 0.1 collective-permute-start.16
  154.6 14.6 %collective-permute-done.16 = bf16[384,768]{1,0:T(8,128)(2,1)S(1)} collective-permute-done((bf16[384,768]{1,0:T(8,128)(2,1)S(1)}, bf16[384,768]{1,0:T(8,128)(2,1)S(1)}, u32[]{:S(2)}, u32[]{:S(2)}) %collective-permute-start.16) | collective-permute-done | bytes 589856 | tf_op jit(solution)/shard_map/ppermute | solution.py:262
  169.2 1.1 add_convert_fusion
  (28 shorter events, 0.1 us)
Async XLA Ops:
  0.0 5.1 %copy-start = (bf16[64,384]{1,0:T(8,128)(2,1)S(1)}, bf16[64,384]{1,0:T(8,128)(2,1)}, u32[]{:S(2)}) copy-start(bf16[64,384]{1,0:T(8,128)(2,1)} %param.16) | copy-start | bytes 147460
  2.0 15.8 %copy-start.7 = (bf16[144,768]{1,0:T(8,128)(2,1)}, bf16[144,768]{1,0:T(8,128)(2,1)S(1)}, u32[]{:S(2)}) copy-start(bf16[144,768]{1,0:T(8,128)(2,1)S(1)} %concatenate.3.p0.refs_11_) | copy-start | bytes 663556
  2.0 14.0 %collective-permute-start.7 = (bf16[144,768]{1,0:T(8,128)(2,1)S(1)}, bf16[144,768]{1,0:T(8,128)(2,1)S(1)}, u32[]{:S(2)}, u32[]{:S(2)}) collective-permute-start(bf16[144,768]{1,0:T(8,128)(2,1)S(1)} %concatenate.3.p0.refs_11_), channel_id=1, source_target_pairs={{0,2},{1,3},{2,0},{3,1},{4,6},{5,7},{6,4},{7,5},{8,10},{9,11},{10,... | collective-permute-start | bytes 663560 | tf_op jit(solution)/shard_map/ppermute | solution.py:262
  4.2 13.6 %collective-permute-start.4 = (bf16[144,768]{1,0:T(8,128)(2,1)S(1)}, bf16[144,768]{1,0:T(8,128)(2,1)S(1)}, u32[]{:S(2)}, u32[]{:S(2)}) collective-permute-start(bf16[144,768]{1,0:T(8,128)(2,1)S(1)} %concatenate.3.p0.refs_11_), channel_id=1, source_target_pairs={{0,1},{1,0},{2,3},{3,2},{4,5},{5,4},{6,7},{7,6},{8,9},{9,8},{10,11... | collective-permute-start | bytes 663560 | tf_op jit(solution)/shard_map/ppermute | solution.py:262
  5.1 4.7 %collective-permute-start.2 = (bf16[32,384]{1,0:T(8,128)(2,1)S(1)}, bf16[32,384]{1,0:T(8,128)(2,1)S(1)}, u32[]{:S(2)}, u32[]{:S(2)}) collective-permute-start(bf16[32,384]{1,0:T(8,128)(2,1)S(1)} %constant_dynamic-slice_fusion.p0), channel_id=1, source_target_pairs={{0,12},{4,0},{8,4},{12,8},{16,28},{20,16},{24,20},{28,24},{32,44},... | collective-permute-start | bytes 73736 | tf_op jit(solution)/shard_map/ppermute | solution.py:262
  8.9 4.2 %collective-permute-start.1 = (bf16[32,384]{1,0:T(8,128)(2,1)S(1)}, bf16[32,384]{1,0:T(8,128)(2,1)S(1)}, u32[]{:S(2)}, u32[]{:S(2)}) collective-permute-start(bf16[32,384]{1,0:T(8,128)(2,1)S(1)} %constant_dynamic-slice_fusion.p0), channel_id=1, source_target_pairs={{0,8},{4,12},{8,0},{12,4},{16,24},{20,28},{24,16},{28,20},{32,40},... | collective-permute-start | bytes 73736 | tf_op jit(solution)/shard_map/ppermute | solution.py:262
  8.9 4.2 %collective-permute-start = (bf16[32,384]{1,0:T(8,128)(2,1)S(1)}, bf16[32,384]{1,0:T(8,128)(2,1)S(1)}, u32[]{:S(2)}, u32[]{:S(2)}) collective-permute-start(bf16[32,384]{1,0:T(8,128)(2,1)S(1)} %constant_dynamic-slice_fusion.p0), channel_id=1, source_target_pairs={{0,4},{4,8},{8,12},{12,0},{16,20},{20,24},{24,28},{28,16},{32,36},... | collective-permute-start | bytes 73736 | tf_op jit(solution)/shard_map/ppermute | solution.py:262
  13.2 10.1 %collective-permute-start.3 = (bf16[2,32,768]{2,1,0:T(8,128)(2,1)S(1)}, bf16[2,32,768]{2,1,0:T(8,128)(2,1)S(1)}, u32[]{:S(2)}, u32[]{:S(2)}) collective-permute-start(bf16[2,32,768]{2,1,0:T(8,128)(2,1)S(1)} %shard_map.154), channel_id=1, source_target_pairs={{0,16},{4,20},{8,24},{12,28},{16,0},{20,4},{24,8},{28,12},{32,48},... | collective-permute-start | bytes 294920 | tf_op jit(solution)/shard_map/ppermute | solution.py:262
  15.9 7.4 %copy-start.10 = (bf16[144,768]{1,0:T(8,128)(2,1)}, bf16[144,768]{1,0:T(8,128)(2,1)S(1)}, u32[]{:S(2)}) copy-start(bf16[144,768]{1,0:T(8,128)(2,1)S(1)} %collective-permute-done.7.p0) | copy-start | bytes 663556
  16.0 12.1 %collective-permute-start.8 = (bf16[144,768]{1,0:T(8,128)(2,1)S(1)}, bf16[144,768]{1,0:T(8,128)(2,1)S(1)}, u32[]{:S(2)}, u32[]{:S(2)}) collective-permute-start(bf16[144,768]{1,0:T(8,128)(2,1)S(1)} %collective-permute-done.7.p0), channel_id=1, source_target_pairs={{0,1},{1,0},{2,3},{3,2},{4,5},{5,4},{6,7},{7,6},{8,9},{9,8},{10,11... | collective-permute-start | bytes 663560 | tf_op jit(solution)/shard_map/ppermute | solution.py:262
  17.7 0.7 copy-start.12
  23.4 18.1 %copy-start.1 = (f32[48,768]{1,0:T(8,128)S(1)}, f32[48,768]{1,0:T(8,128)}, u32[]{:S(2)}) copy-start(f32[48,768]{1,0:T(8,128)} %constant.54.clone.refs_13_) | copy-start | bytes 442372
  23.4 18.0 %copy-start.2 = (f32[48,768]{1,0:T(8,128)S(1)}, f32[48,768]{1,0:T(8,128)}, u32[]{:S(2)}) copy-start(f32[48,768]{1,0:T(8,128)} %constant.53.clone.refs_12_) | copy-start | bytes 442372
  23.4 18.0 %copy-start.3 = (f32[192,128]{1,0:T(8,128)S(1)}, f32[192,128]{1,0:T(8,128)}, u32[]{:S(2)}) copy-start(f32[192,128]{1,0:T(8,128)} %constant.58.clone.refs_17_) | copy-start | bytes 294916
  23.4 18.0 %copy-start.4 = (f32[192,128]{1,0:T(8,128)S(1)}, f32[192,128]{1,0:T(8,128)}, u32[]{:S(2)}) copy-start(f32[192,128]{1,0:T(8,128)} %constant.57.clone.refs_16_) | copy-start | bytes 294916
  23.4 18.0 %copy-start.5 = (f32[2,64,128]{2,1,0:T(8,128)S(1)}, f32[2,64,128]{2,1,0:T(8,128)}, u32[]{:S(2)}) copy-start(f32[2,64,128]{2,1,0:T(8,128)} %constant.59.clone.refs_18_) | copy-start | bytes 196612
  23.4 18.0 %copy-start.6 = (s32[64]{0:T(128)S(1)}, s32[64]{0:T(128)}, u32[]{:S(2)}) copy-start(s32[64]{0:T(128)} %span_ref.1) | copy-start | bytes 772
  23.5 11.0 %collective-permute-start.12 = (bf16[2,2,32,768]{3,2,1,0:T(8,128)(2,1)S(1)}, bf16[2,2,32,768]{3,2,1,0:T(8,128)(2,1)S(1)}, u32[]{:S(2)}, u32[]{:S(2)}) collective-permute-start(bf16[2,2,32,768]{3,2,1,0:T(8,128)(2,1)S(1)} %pad_maximum_fusion.refs_0_), channel_id=1, source_target_pairs={{0,96},{4,100},{8,104},{12,108},{16,112},{20,116},{24,120},{28,124... | collective-permute-start | bytes 589832 | tf_op jit(solution)/shard_map/ppermute | solution.py:262
  26.0 8.4 %collective-permute-start.10 = (bf16[2,2,32,768]{3,2,1,0:T(8,128)(2,1)S(1)}, bf16[2,2,32,768]{3,2,1,0:T(8,128)(2,1)S(1)}, u32[]{:S(2)}, u32[]{:S(2)}) collective-permute-start(bf16[2,2,32,768]{3,2,1,0:T(8,128)(2,1)S(1)} %pad_maximum_fusion.refs_0_), channel_id=1, source_target_pairs={{0,64},{4,68},{8,72},{12,76},{16,80},{20,84},{24,88},{28,92},{32,9... | collective-permute-start | bytes 589832 | tf_op jit(solution)/shard_map/ppermute | solution.py:262
  26.5 12.0 %collective-permute-start.6 = (bf16[2,2,32,768]{3,2,1,0:T(8,128)(2,1)S(1)}, bf16[2,2,32,768]{3,2,1,0:T(8,128)(2,1)S(1)}, u32[]{:S(2)}, u32[]{:S(2)}) collective-permute-start(bf16[2,2,32,768]{3,2,1,0:T(8,128)(2,1)S(1)} %pad_maximum_fusion.refs_0_), channel_id=1, source_target_pairs={{0,32},{4,36},{8,40},{12,44},{16,48},{20,52},{24,56},{28,60},{32,6... | collective-permute-start | bytes 589832 | tf_op jit(solution)/shard_map/ppermute | solution.py:262
  27.1 12.4 %collective-permute-start.5 = (bf16[2,2,32,768]{3,2,1,0:T(8,128)(2,1)S(1)}, bf16[2,2,32,768]{3,2,1,0:T(8,128)(2,1)S(1)}, u32[]{:S(2)}, u32[]{:S(2)}) collective-permute-start(bf16[2,2,32,768]{3,2,1,0:T(8,128)(2,1)S(1)} %pad_maximum_fusion.refs_0_), channel_id=1, source_target_pairs={{0,1},{1,0},{2,3},{3,2},{4,5},{5,4},{6,7},{7,6},{8,9},{9,8},{10,11... | collective-permute-start | bytes 589832 | tf_op jit(solution)/shard_map/ppermute | solution.py:262
  28.0 0.7 copy-start.11
  38.5 1.6 collective-permute-start.9
  39.0 1.4 collective-permute-start.11
  39.1 1.7 %collective-permute-start.13 = (bf16[2,2,32,768]{3,2,1,0:T(8,128)(2,1)S(1)}, bf16[2,2,32,768]{3,2,1,0:T(8,128)(2,1)S(1)}, u32[]{:S(2)}, u32[]{:S(2)}) collective-permute-start(bf16[2,2,32,768]{3,2,1,0:T(8,128)(2,1)S(1)} %collective-permute-done.12.refs_6_), channel_id=1, source_target_pairs={{0,1},{1,0},{2,3},{3,2},{4,5},{5,4},{6,7},{7,6},{8,9},{9,8},{10,11... | collective-permute-start | bytes 589832 | tf_op jit(solution)/shard_map/ppermute | solution.py:262
  40.8 0.7 copy-start.13
  150.9 18.2 %copy-start.8 = (bf16[384,768]{1,0:T(8,128)(2,1)S(1)}, bf16[384,768]{1,0:T(8,128)(2,1)}, u32[]{:S(2)}) copy-start(bf16[384,768]{1,0:T(8,128)(2,1)} %get-tuple-element.32) | copy-start | bytes 1769476
  151.0 18.2 %copy-start.9 = (bf16[384,768]{1,0:T(8,128)(2,1)S(1)}, bf16[384,768]{1,0:T(8,128)(2,1)}, u32[]{:S(2)}) copy-start(bf16[384,768]{1,0:T(8,128)(2,1)} %get-tuple-element.36) | copy-start | bytes 1769476
  151.0 2.3 %collective-permute-start.15 = (bf16[384,768]{1,0:T(8,128)(2,1)}, bf16[384,768]{1,0:T(8,128)(2,1)S(1)}, u32[]{:S(2)}, u32[]{:S(2)}) collective-permute-start(bf16[384,768]{1,0:T(8,128)(2,1)} %get-tuple-element.35), channel_id=1, source_target_pairs={{0,1},{1,0},{2,3},{3,2},{4,5},{5,4},{6,7},{7,6},{8,9},{9,8},{10,11... | collective-permute-start | bytes 1769480 | tf_op jit(solution)/shard_map/ppermute | solution.py:262
  151.4 3.2 %collective-permute-start.14 = (bf16[384,768]{1,0:T(8,128)(2,1)}, bf16[384,768]{1,0:T(8,128)(2,1)S(1)}, u32[]{:S(2)}, u32[]{:S(2)}) collective-permute-start(bf16[384,768]{1,0:T(8,128)(2,1)} %get-tuple-element.33), channel_id=1, source_target_pairs={{0,1},{1,0},{2,3},{3,2},{4,5},{5,4},{6,7},{7,6},{8,9},{9,8},{10,11... | collective-permute-start | bytes 1769480 | tf_op jit(solution)/shard_map/ppermute | solution.py:262
  154.5 14.7 %collective-permute-start.16 = (bf16[384,768]{1,0:T(8,128)(2,1)S(1)}, bf16[384,768]{1,0:T(8,128)(2,1)S(1)}, u32[]{:S(2)}, u32[]{:S(2)}) collective-permute-start(bf16[384,768]{1,0:T(8,128)(2,1)S(1)} %add_convert_fusion.1), channel_id=1, source_target_pairs={{0,2},{1,3},{2,0},{3,1},{4,6},{5,7},{6,4},{7,5},{8,10},{9,11},{10,... | collective-permute-start | bytes 1769480 | tf_op jit(solution)/shard_map/ppermute | solution.py:262

commit v7 on v5

--- a/solution.py
+++ b/solution.py
@@ -55,18 +55,11 @@
 def kernel(seq_ref, head_ref, span_ref, *refs):
     pieces, refs = refs[:8], refs[8:]
     (mg_ref, mq_ref, mv_ref, pw_ref, cs_ref, ss_ref, ct_ref, st_ref, cq_ref, sq_ref, tq_ref, wo_ref) = refs[:12]
-    (outs, tokens_ref), refs = (refs[12:16], refs[16]), refs[17:]
+    (outs, tokens_ref), refs = (refs[12:18], refs[18]), refs[19:]
     raw_ref, own_ref, q_ref, w_ref, u_ref, ho_ref, m_ref, k_ref, v_ref, res_ref, wide_ref, sems, out_sems, wide_sem = refs
     seq, head = seq_ref[0], head_ref[0]
     own_frames = (seq, FRAMES - 1 - seq)
 
-    def end_of(frame):
-        count = lambda g, seen: seen + (span_ref[g] <= span_ref[frame]).astype(jnp.int32)
-        return lax.fori_loop(0, FRAMES, count, 0)
-
-    end_early, end_late = end_of(own_frames[0]), end_of(own_frames[1])
-    blocks_early = (end_early + BF - 1) // BF
-    blocks_late = (end_late + BF - 1) // BF
     wide_copy = pltpu.make_async_copy(wo_ref, wide_ref, wide_sem)
     wide_copy.start()
     x_at, y_at, core, chip = seq // 8, (seq // 4) % 2, head % 2, head // 2
@@ -88,6 +81,14 @@
                     )
     for copy in copies:
         copy.start()
+
+    def end_of(frame):
+        count = lambda g, seen: seen + (span_ref[g] <= span_ref[frame]).astype(jnp.int32)
+        return lax.fori_loop(0, FRAMES, count, 0, unroll=True)
+
+    end_early, end_late = end_of(own_frames[0]), end_of(own_frames[1])
+    blocks_early = (end_early + BF - 1) // BF
+    blocks_late = (end_late + BF - 1) // BF
     for copy in copies:
         copy.wait()
 
@@ -152,7 +153,7 @@
             rotated = pre * cos + pltpu.roll(pre, 64, 1) * sin
             q_ref[i, h] = jnp.concatenate([rotated.astype(BF16), select], axis=1)
 
-    tokens_copy = pltpu.make_async_copy(res_ref.at[4], tokens_ref, out_sems.at[4])
+    tokens_copy = pltpu.make_async_copy(res_ref.at[4], tokens_ref, out_sems.at[6])
     tokens_copy.start()
     u_ref[...] = jnp.zeros_like(u_ref)
 
@@ -222,8 +223,10 @@
         group = (chip ^ (n // 2)) * 2 + (core ^ (n % 2))
         columns = pl.ds(pl.multiple_of(group * 768, 768), 768)
         res_ref[n] = dot(ho_ref[...], wide_ref[:, columns]).astype(BF16)
-        sent.append(pltpu.make_async_copy(res_ref.at[n], outs[n], out_sems.at[n]))
-        sent[-1].start()
+        for i, target in enumerate(outs[2 * n - 2 : 2 * n] if n > 1 else outs[n : n + 1]):
+            source = res_ref.at[n, pl.ds(i * FT, FT)] if n > 1 else res_ref.at[n]
+            sent.append(pltpu.make_async_copy(source, target, out_sems.at[len(sent) - 1]))
+            sent[-1].start()
     for copy in sent:
         copy.wait()
 
@@ -232,11 +235,12 @@
     vmem = pl.BlockSpec(memory_space=pltpu.VMEM)
     hbm = pl.BlockSpec(memory_space=pl.ANY)
     shape = jax.ShapeDtypeStruct((2 * FT, 768), BF16)
+    frame = jax.ShapeDtypeStruct((FT, 768), BF16)
     return pl.pallas_call(
         kernel,
         in_specs=[pl.BlockSpec(memory_space=pltpu.SMEM)] * 3 + [hbm] * 8 + [vmem] * 11 + [hbm],
-        out_specs=(hbm,) * 5,
-        out_shape=(shape,) * 5,
+        out_specs=(hbm,) * 7,
+        out_shape=(shape,) * 2 + (frame,) * 4 + (shape,),
         scratch_shapes=[
             pltpu.VMEM((NB, 64, BK), BF16),
             pltpu.VMEM((BK, ROWS), BF16),
@@ -250,7 +254,7 @@
             pltpu.VMEM((5, 2 * FT, HEADS * HD), BF16),
             pltpu.VMEM((HEADS * HD, 4 * HEADS * HD), BF16),
             pltpu.SemaphoreType.DMA((32,)),
-            pltpu.SemaphoreType.DMA((5,)),
+            pltpu.SemaphoreType.DMA((7,)),
             pltpu.SemaphoreType.DMA,
         ],
         compiler_params=pltpu.CompilerParams(vmem_limit_bytes=52 * 2**20),
@@ -318,32 +322,9 @@
         ],
         compiler_params=pltpu.CompilerParams(vmem_limit_bytes=57 * 2**20),
         cost_estimate=pl.CostEstimate(
-            flops=2 * ROWS * 3072 * 2400, bytes_accessed=3 * 3072 * 768 * 2, transcendentals=0
+            flops=2 * ROWS * 3072 * 240, bytes_accessed=3 * 3072 * 768, transcendentals=0
         ),
     )(lax.axis_index("head").astype(jnp.int32).reshape(1), *parts, gain.reshape(4, 1, columns), wq, wk, wv)
-
-
-def widen_kernel(weight, bias, out):
-    out[:128] = weight[...]
-    b = bias[...]
-    row = lax.broadcasted_iota(jnp.int32, (ROWS - 128, b.shape[1]), 0)
-    b0 = b.astype(BF16).astype(F32)
-    b1 = (b - b0).astype(BF16).astype(F32)
-    b2 = b - b0 - b1
-    parts = jnp.where(row == 0, b0, jnp.where(row == 1, b1, jnp.where(row == 2, b2, 0.0)))
-    out[128:] = parts.astype(BF16)
-
-
-def widen(weight, bias):
-    vmem = pl.BlockSpec(memory_space=pltpu.VMEM)
-    return pl.pallas_call(
-        widen_kernel,
-        in_specs=[vmem] * 2,
-        out_specs=vmem,
-        out_shape=jax.ShapeDtypeStruct((ROWS, weight.shape[1]), BF16),
-        compiler_params=pltpu.CompilerParams(vmem_limit_bytes=2 * 2**20),
-        cost_estimate=pl.CostEstimate(flops=0, bytes_accessed=400000, transcendentals=0),
-    )(weight, bias.reshape(1, -1))
 
 
 def join_kernel(z, p0, p1, p2, p3, out):
@@ -417,7 +398,11 @@
     half = lax.dynamic_slice_in_dim(latents, (head % 2) * 32, 32, 0)
     halves = all_latents(half)
 
-    wide = widen(lax.optimization_barrier((patch_weight, half))[0], patch_bias)
+    b0 = patch_bias.astype(BF16)
+    b1 = (patch_bias - b0.astype(F32)).astype(BF16)
+    b2 = (patch_bias - b0.astype(F32) - b1.astype(F32)).astype(BF16)
+    rest = jnp.zeros((ROWS - 131, patch_bias.shape[0]), BF16)
+    wide = jnp.concatenate([patch_weight, b0[None], b1[None], b2[None], rest], axis=0)
     far_part = swap(wide, 2)
     parts = [wide, swap(wide, 1), far_part, swap(far_part, 1)]
     mg, mq, mv = through(parts, norm_gain, query_weight, key_weight, value_weight)
@@ -445,16 +430,16 @@
     tq = np.stack([np.concatenate([tc, tc], axis=1), np.concatenate([-ts, ts], axis=1)])
     tq = jnp.asarray(tq * SCALE, F32)
 
-    near, near_other, far, far_other, tokens = attention(
+    near, near_other, *far, tokens = attention(
         seq.astype(jnp.int32).reshape(1),
         head.astype(jnp.int32).reshape(1),
         span_ids,
         *pieces,
         *(mg, mq, mv, wide, cs, ss, ct, st, cq, sq, tq, out_weight),
     )
-    sent = swap(add(far, swap(far_other, 1)).astype(BF16), 2)
+    sent = [swap(add(far[i], swap(far[i + 2], 1)).astype(BF16), 2) for i in range(2)]
     kept = add(near, swap(near_other, 1)).astype(BF16)
-    return (add(kept, sent) + tokens.astype(F32)).astype(BF16)
+    return (add(kept, jnp.concatenate(sent)) + tokens.astype(F32)).astype(BF16)
 
 
 def solution(mesh):

time: 168 us -> 166 us (0.988)
  waiting for transfers between devices: 21.5 us -> 18 us
  Pallas kernels: 120 us -> 118 us
  starting transfers between devices: 20.9 us -> 22.9 us
    ppermute x17 -> x19, waiting for transfers between devices: 21.5 us -> 18 us  [permute(): lax.ppermute(x, axis, [(i, to(i)) for i in range(lax.axis_size(axis))])]
    ppermute x17 -> x19, starting transfers between devices: 20.9 us -> 22.9 us  [permute(): lax.ppermute(x, axis, [(i, to(i)) for i in range(lax.axis_size(axis))])]
    convert_element_type x2 -> x4, other arithmetic: 2.3 us -> 3.94 us  [the longest x2 2.07 us: local(): add(far[i], swap(far[i + 2], 1)).astype(BF16)]
  transfers between devices with their start and end apart: 17 -> 19, of which waited for: 7 -> 8; matrix products, arithmetic and copies ran while one was open for 1% -> 1% of each run, Pallas kernels for 5% -> 5%
where the time goes in v7:
time: 166 us
  Pallas kernels  118 us (71%)
  starting transfers between devices  22.9 us (14%)
  waiting for transfers between devices  18 us (11%)
  other arithmetic  3.96 us (2%)
  local copies, waits for them, and re-layouts  2.57 us (2%)
    pallas_call x1, Pallas kernels, attention(): pl.pallas_call(kernel, in_specs=[pl.BlockSpec(memory_space=pltpu.SMEM)] *...  109 us
    ppermute x19, starting transfers between devices, permute(): lax.ppermute(x, axis, [(i, to(i)) for i in range(lax.axis_size(axis))])  22.9 us
    ppermute x19, waiting for transfers between devices, permute(): lax.ppermute(x, axis, [(i, to(i)) for i in range(lax.axis_size(axis))])  18 us
    pallas_call x1, Pallas kernels, through(): pl.pallas_call(weights_kernel, grid_spec=pltpu.PrefetchScalarGridSpec(num...  8.76 us
  transfers between devices with their start and end apart: 19, of which 8 were waited for; matrix products, arithmetic and copies ran while one was open for 1% of the time, Pallas kernels for 5%

profile of v7, /device:TPU:1, one launch (start us, length us, event | category | flops | bytes accessed | tf_op | source)
XLA Modules:
  0.0 165.7 jit_solution(3840021151844224270)
XLA Ops:
  0.0 0.8 subtract_convert_fusion
  0.8 1.1 concatenate.6.p0.refs_11_
  2.0 2.2 %collective-permute-start.7 = (bf16[144,768]{1,0:T(8,128)(2,1)S(1)}, bf16[144,768]{1,0:T(8,128)(2,1)S(1)}, u32[]{:S(2)}, u32[]{:S(2)}) collective-permute-start(bf16[144,768]{1,0:T(8,128)(2,1)S(1)} %concatenate.6.p0.refs_11_), channel_id=1, source_target_pairs={{0,2},{1,3},{2,0},{3,1},{4,6},{5,7},{6,4},{7,5},{8,10},{9,11},{10,... | collective-permute-start | bytes 663560 | tf_op jit(solution)/shard_map/ppermute | solution.py:265
  4.2 3.8 %collective-permute-start.2 = (bf16[32,384]{1,0:T(8,128)(2,1)S(1)}, bf16[32,384]{1,0:T(8,128)(2,1)S(1)}, u32[]{:S(2)}, u32[]{:S(2)}) collective-permute-start(bf16[32,384]{1,0:T(8,128)(2,1)S(1)} %constant_dynamic-slice_fusion.p0), channel_id=1, source_target_pairs={{0,12},{4,0},{8,4},{12,8},{16,28},{20,16},{24,20},{28,24},{32,44},... | collective-permute-start | bytes 73736 | tf_op jit(solution)/shard_map/ppermute | solution.py:265
  7.9 0.0 collective-permute-start.1
  7.9 0.7 collective-permute-start
  8.6 0.2 collective-permute-done.2.p3
  8.9 3.2 %collective-permute-done.1.p2 = bf16[32,384]{1,0:T(8,128)(2,1)S(1)} collective-permute-done((bf16[32,384]{1,0:T(8,128)(2,1)S(1)}, bf16[32,384]{1,0:T(8,128)(2,1)S(1)}, u32[]{:S(2)}, u32[]{:S(2)}) %collective-permute-start.1) | collective-permute-done | bytes 24608 | tf_op jit(solution)/shard_map/ppermute | solution.py:265
  12.1 0.0 collective-permute-done.p1
  12.1 0.2 shard_map.154
  12.3 2.7 %collective-permute-start.3 = (bf16[2,32,768]{2,1,0:T(8,128)(2,1)S(1)}, bf16[2,32,768]{2,1,0:T(8,128)(2,1)S(1)}, u32[]{:S(2)}, u32[]{:S(2)}) collective-permute-start(bf16[2,32,768]{2,1,0:T(8,128)(2,1)S(1)} %shard_map.154), channel_id=1, source_target_pairs={{0,16},{4,20},{8,24},{12,28},{16,0},{20,4},{24,8},{28,12},{32,48},... | collective-permute-start | bytes 294920 | tf_op jit(solution)/shard_map/ppermute | solution.py:265
  15.0 2.7 %collective-permute-start.6 = (bf16[144,768]{1,0:T(8,128)(2,1)S(1)}, bf16[144,768]{1,0:T(8,128)(2,1)S(1)}, u32[]{:S(2)}, u32[]{:S(2)}) collective-permute-start(bf16[144,768]{1,0:T(8,128)(2,1)S(1)} %concatenate.6.p0.refs_11_), channel_id=1, source_target_pairs={{0,1},{1,0},{2,3},{3,2},{4,5},{5,4},{6,7},{7,6},{8,9},{9,8},{10,11... | collective-permute-start | bytes 663560 | tf_op jit(solution)/shard_map/ppermute | solution.py:265
  17.7 0.0 collective-permute-done.7.p2
  17.7 0.1 collective-permute-start.8
  17.7 0.0 collective-permute-done.3
  17.8 2.5 %collective-permute-start.12 = (bf16[2,2,32,768]{3,2,1,0:T(8,128)(2,1)S(1)}, bf16[2,2,32,768]{3,2,1,0:T(8,128)(2,1)S(1)}, u32[]{:S(2)}, u32[]{:S(2)}) collective-permute-start(bf16[2,2,32,768]{3,2,1,0:T(8,128)(2,1)S(1)} %pad_maximum_fusion.refs_0_), channel_id=1, source_target_pairs={{0,96},{4,100},{8,104},{12,108},{16,112},{20,116},{24,120},{28,124... | collective-permute-start | bytes 589832 | tf_op jit(solution)/shard_map/ppermute | solution.py:265
  20.3 0.5 collective-permute-start.10
  20.8 0.6 collective-permute-start.5
  21.4 0.0 collective-permute-done.6.p1
  21.5 4.0 %collective-permute-start.4 = (bf16[2,2,32,768]{3,2,1,0:T(8,128)(2,1)S(1)}, bf16[2,2,32,768]{3,2,1,0:T(8,128)(2,1)S(1)}, u32[]{:S(2)}, u32[]{:S(2)}) collective-permute-start(bf16[2,2,32,768]{3,2,1,0:T(8,128)(2,1)S(1)} %pad_maximum_fusion.refs_0_), channel_id=1, source_target_pairs={{0,1},{1,0},{2,3},{3,2},{4,5},{5,4},{6,7},{7,6},{8,9},{9,8},{10,11... | collective-permute-start | bytes 589832 | tf_op jit(solution)/shard_map/ppermute | solution.py:265
  25.4 0.0 collective-permute-done.8.p3
  25.4 0.7 copy-done.12
  26.1 0.0 copy-start.5
  26.2 0.0 copy-start.6
  26.2 8.8 %shard_map.155 = (bf16[1056,144]{1,0:T(8,128)(2,1)}, bf16[144,768]{1,0:T(8,128)(2,1)}, bf16[144,768]{1,0:T(8,128)(2,1)}) custom-call(s32[1]{0:T(128)} %bitcast.1.me.head_ref, bf16[144,768]{1,0:T(8,128)(2,1)} %copy-done.7, bf16[144,768]{1,0:T(8,128)(2,1)} %copy-done.11, bf16[144,768]{1,0:T(8,128)(2,1)} %copy-done.10, bf16[144,768]{1,0:T(8,128)(2,1)} %copy-done.12, ...), custom_call_target="tpu_custom_call" | custom-call | flops 212336640 | bytes 7077888 | tf_op jit(solution)/shard_map/pallas_call | solution.py:303
  34.9 0.0 collective-permute-done.12.refs_6_
  34.9 0.0 collective-permute-done.5.refs_2_
  34.9 0.1 collective-permute-start.9
  35.1 0.4 collective-permute-start.11
  35.5 0.1 collective-permute-start.13
  35.6 0.8 collective-permute-done.9.refs_3_
  36.5 0.3 collective-permute-done.11.refs_5_
  36.8 0.3 collective-permute-done.13.refs_7_
  37.0 0.7 copy-done.13
  37.7 109.2 %shard_map.156 = (bf16[384,768]{1,0:T(8,128)(2,1)}, bf16[384,768]{1,0:T(8,128)(2,1)}, bf16[192,768]{1,0:T(8,128)(2,1)}, bf16[192,768]{1,0:T(8,128)(2,1)}, bf16[1...) custom-call(s32[1]{0:T(128)} %bitcast.seq_ref, s32[1]{0:T(128)} %bitcast.1.me.head_ref, ...), custom_call_target="tpu_custom_call" | custom-call | tf_op jit(solution)/shard_map/pallas_call | solution.py:239
  147.0 0.0 copy-start.8
  147.0 0.3 collective-permute-start.15
  147.3 0.2 collective-permute-start.17
  147.6 0.3 collective-permute-start.14
  147.8 1.0 collective-permute-done.15
  148.9 1.0 add_convert_fusion.3
  149.9 0.3 collective-permute-start.16
  150.2 0.0 collective-permute-done.17
  150.2 1.0 add_convert_fusion.2
  151.2 1.4 collective-permute-start.18
  152.6 5.8 %collective-permute-done.16 = bf16[192,768]{1,0:T(8,128)(2,1)S(1)} collective-permute-done((bf16[192,768]{1,0:T(8,128)(2,1)S(1)}, bf16[192,768]{1,0:T(8,128)(2,1)S(1)}, u32[]{:S(2)}, u32[]{:S(2)}) %collective-permute-start.16) | collective-permute-done | bytes 294944 | tf_op jit(solution)/shard_map/ppermute | solution.py:265
  158.3 6.3 %collective-permute-done.18 = bf16[192,768]{1,0:T(8,128)(2,1)S(1)} collective-permute-done((bf16[192,768]{1,0:T(8,128)(2,1)S(1)}, bf16[192,768]{1,0:T(8,128)(2,1)S(1)}, u32[]{:S(2)}, u32[]{:S(2)}) %collective-permute-start.18) | collective-permute-done | bytes 294944 | tf_op jit(solution)/shard_map/ppermute | solution.py:265
  164.6 1.1 add_convert_fusion
  (32 shorter events, 0.1 us)
Async XLA Ops:
  0.0 4.2 %copy-start = (bf16[64,384]{1,0:T(8,128)(2,1)S(1)}, bf16[64,384]{1,0:T(8,128)(2,1)}, u32[]{:S(2)}) copy-start(bf16[64,384]{1,0:T(8,128)(2,1)} %param.16) | copy-start | bytes 147460
  2.0 23.5 %copy-start.7 = (bf16[144,768]{1,0:T(8,128)(2,1)}, bf16[144,768]{1,0:T(8,128)(2,1)S(1)}, u32[]{:S(2)}) copy-start(bf16[144,768]{1,0:T(8,128)(2,1)S(1)} %concatenate.6.p0.refs_11_) | copy-start | bytes 663556
  2.0 15.7 %collective-permute-start.7 = (bf16[144,768]{1,0:T(8,128)(2,1)S(1)}, bf16[144,768]{1,0:T(8,128)(2,1)S(1)}, u32[]{:S(2)}, u32[]{:S(2)}) collective-permute-start(bf16[144,768]{1,0:T(8,128)(2,1)S(1)} %concatenate.6.p0.refs_11_), channel_id=1, source_target_pairs={{0,2},{1,3},{2,0},{3,1},{4,6},{5,7},{6,4},{7,5},{8,10},{9,11},{10,... | collective-permute-start | bytes 663560 | tf_op jit(solution)/shard_map/ppermute | solution.py:265
  4.2 4.7 %collective-permute-start.2 = (bf16[32,384]{1,0:T(8,128)(2,1)S(1)}, bf16[32,384]{1,0:T(8,128)(2,1)S(1)}, u32[]{:S(2)}, u32[]{:S(2)}) collective-permute-start(bf16[32,384]{1,0:T(8,128)(2,1)S(1)} %constant_dynamic-slice_fusion.p0), channel_id=1, source_target_pairs={{0,12},{4,0},{8,4},{12,8},{16,28},{20,16},{24,20},{28,24},{32,44},... | collective-permute-start | bytes 73736 | tf_op jit(solution)/shard_map/ppermute | solution.py:265
  7.9 4.2 %collective-permute-start.1 = (bf16[32,384]{1,0:T(8,128)(2,1)S(1)}, bf16[32,384]{1,0:T(8,128)(2,1)S(1)}, u32[]{:S(2)}, u32[]{:S(2)}) collective-permute-start(bf16[32,384]{1,0:T(8,128)(2,1)S(1)} %constant_dynamic-slice_fusion.p0), channel_id=1, source_target_pairs={{0,8},{4,12},{8,0},{12,4},{16,24},{20,28},{24,16},{28,20},{32,40},... | collective-permute-start | bytes 73736 | tf_op jit(solution)/shard_map/ppermute | solution.py:265
  7.9 4.2 %collective-permute-start = (bf16[32,384]{1,0:T(8,128)(2,1)S(1)}, bf16[32,384]{1,0:T(8,128)(2,1)S(1)}, u32[]{:S(2)}, u32[]{:S(2)}) collective-permute-start(bf16[32,384]{1,0:T(8,128)(2,1)S(1)} %constant_dynamic-slice_fusion.p0), channel_id=1, source_target_pairs={{0,4},{4,8},{8,12},{12,0},{16,20},{20,24},{24,28},{28,16},{32,36},... | collective-permute-start | bytes 73736 | tf_op jit(solution)/shard_map/ppermute | solution.py:265
  12.3 5.5 %collective-permute-start.3 = (bf16[2,32,768]{2,1,0:T(8,128)(2,1)S(1)}, bf16[2,32,768]{2,1,0:T(8,128)(2,1)S(1)}, u32[]{:S(2)}, u32[]{:S(2)}) collective-permute-start(bf16[2,32,768]{2,1,0:T(8,128)(2,1)S(1)} %shard_map.154), channel_id=1, source_target_pairs={{0,16},{4,20},{8,24},{12,28},{16,0},{20,4},{24,8},{28,12},{32,48},... | collective-permute-start | bytes 294920 | tf_op jit(solution)/shard_map/ppermute | solution.py:265
  15.0 6.5 %collective-permute-start.6 = (bf16[144,768]{1,0:T(8,128)(2,1)S(1)}, bf16[144,768]{1,0:T(8,128)(2,1)S(1)}, u32[]{:S(2)}, u32[]{:S(2)}) collective-permute-start(bf16[144,768]{1,0:T(8,128)(2,1)S(1)} %concatenate.6.p0.refs_11_), channel_id=1, source_target_pairs={{0,1},{1,0},{2,3},{3,2},{4,5},{5,4},{6,7},{7,6},{8,9},{9,8},{10,11... | collective-permute-start | bytes 663560 | tf_op jit(solution)/shard_map/ppermute | solution.py:265
  17.7 7.8 %copy-start.10 = (bf16[144,768]{1,0:T(8,128)(2,1)}, bf16[144,768]{1,0:T(8,128)(2,1)S(1)}, u32[]{:S(2)}) copy-start(bf16[144,768]{1,0:T(8,128)(2,1)S(1)} %collective-permute-done.7.p2) | copy-start | bytes 663556
  17.7 7.8 %collective-permute-start.8 = (bf16[144,768]{1,0:T(8,128)(2,1)S(1)}, bf16[144,768]{1,0:T(8,128)(2,1)S(1)}, u32[]{:S(2)}, u32[]{:S(2)}) collective-permute-start(bf16[144,768]{1,0:T(8,128)(2,1)S(1)} %collective-permute-done.7.p2), channel_id=1, source_target_pairs={{0,1},{1,0},{2,3},{3,2},{4,5},{5,4},{6,7},{7,6},{8,9},{9,8},{10,11... | collective-permute-start | bytes 663560 | tf_op jit(solution)/shard_map/ppermute | solution.py:265
  17.8 17.2 %collective-permute-start.12 = (bf16[2,2,32,768]{3,2,1,0:T(8,128)(2,1)S(1)}, bf16[2,2,32,768]{3,2,1,0:T(8,128)(2,1)S(1)}, u32[]{:S(2)}, u32[]{:S(2)}) collective-permute-start(bf16[2,2,32,768]{3,2,1,0:T(8,128)(2,1)S(1)} %pad_maximum_fusion.refs_0_), channel_id=1, source_target_pairs={{0,96},{4,100},{8,104},{12,108},{16,112},{20,116},{24,120},{28,124... | collective-permute-start | bytes 589832 | tf_op jit(solution)/shard_map/ppermute | solution.py:265
  20.3 14.6 %collective-permute-start.10 = (bf16[2,2,32,768]{3,2,1,0:T(8,128)(2,1)S(1)}, bf16[2,2,32,768]{3,2,1,0:T(8,128)(2,1)S(1)}, u32[]{:S(2)}, u32[]{:S(2)}) collective-permute-start(bf16[2,2,32,768]{3,2,1,0:T(8,128)(2,1)S(1)} %pad_maximum_fusion.refs_0_), channel_id=1, source_target_pairs={{0,64},{4,68},{8,72},{12,76},{16,80},{20,84},{24,88},{28,92},{32,9... | collective-permute-start | bytes 589832 | tf_op jit(solution)/shard_map/ppermute | solution.py:265
  20.8 14.1 %collective-permute-start.5 = (bf16[2,2,32,768]{3,2,1,0:T(8,128)(2,1)S(1)}, bf16[2,2,32,768]{3,2,1,0:T(8,128)(2,1)S(1)}, u32[]{:S(2)}, u32[]{:S(2)}) collective-permute-start(bf16[2,2,32,768]{3,2,1,0:T(8,128)(2,1)S(1)} %pad_maximum_fusion.refs_0_), channel_id=1, source_target_pairs={{0,32},{4,36},{8,40},{12,44},{16,48},{20,52},{24,56},{28,60},{32,6... | collective-permute-start | bytes 589832 | tf_op jit(solution)/shard_map/ppermute | solution.py:265
  21.5 4.0 %copy-start.11 = (bf16[144,768]{1,0:T(8,128)(2,1)}, bf16[144,768]{1,0:T(8,128)(2,1)S(1)}, u32[]{:S(2)}) copy-start(bf16[144,768]{1,0:T(8,128)(2,1)S(1)} %collective-permute-done.6.p1) | copy-start | bytes 663556
  21.5 14.2 %collective-permute-start.4 = (bf16[2,2,32,768]{3,2,1,0:T(8,128)(2,1)S(1)}, bf16[2,2,32,768]{3,2,1,0:T(8,128)(2,1)S(1)}, u32[]{:S(2)}, u32[]{:S(2)}) collective-permute-start(bf16[2,2,32,768]{3,2,1,0:T(8,128)(2,1)S(1)} %pad_maximum_fusion.refs_0_), channel_id=1, source_target_pairs={{0,1},{1,0},{2,3},{3,2},{4,5},{5,4},{6,7},{7,6},{8,9},{9,8},{10,11... | collective-permute-start | bytes 589832 | tf_op jit(solution)/shard_map/ppermute | solution.py:265
  25.4 0.7 copy-start.12
  26.1 11.6 %copy-start.1 = (f32[48,768]{1,0:T(8,128)S(1)}, f32[48,768]{1,0:T(8,128)}, u32[]{:S(2)}) copy-start(f32[48,768]{1,0:T(8,128)} %constant.54.clone.refs_13_) | copy-start | bytes 442372
  26.1 11.6 %copy-start.2 = (f32[48,768]{1,0:T(8,128)S(1)}, f32[48,768]{1,0:T(8,128)}, u32[]{:S(2)}) copy-start(f32[48,768]{1,0:T(8,128)} %constant.53.clone.refs_12_) | copy-start | bytes 442372
  26.1 11.6 %copy-start.3 = (f32[192,128]{1,0:T(8,128)S(1)}, f32[192,128]{1,0:T(8,128)}, u32[]{:S(2)}) copy-start(f32[192,128]{1,0:T(8,128)} %constant.58.clone.refs_17_) | copy-start | bytes 294916
  26.1 11.6 %copy-start.4 = (f32[192,128]{1,0:T(8,128)S(1)}, f32[192,128]{1,0:T(8,128)}, u32[]{:S(2)}) copy-start(f32[192,128]{1,0:T(8,128)} %constant.57.clone.refs_16_) | copy-start | bytes 294916
  26.1 11.6 %copy-start.5 = (f32[2,64,128]{2,1,0:T(8,128)S(1)}, f32[2,64,128]{2,1,0:T(8,128)}, u32[]{:S(2)}) copy-start(f32[2,64,128]{2,1,0:T(8,128)} %constant.59.clone.refs_18_) | copy-start | bytes 196612
  26.2 11.6 %copy-start.6 = (s32[64]{0:T(128)S(1)}, s32[64]{0:T(128)}, u32[]{:S(2)}) copy-start(s32[64]{0:T(128)} %span_ref.1) | copy-start | bytes 772
  34.9 1.5 collective-permute-start.9
  35.1 1.7 %collective-permute-start.11 = (bf16[2,2,32,768]{3,2,1,0:T(8,128)(2,1)S(1)}, bf16[2,2,32,768]{3,2,1,0:T(8,128)(2,1)S(1)}, u32[]{:S(2)}, u32[]{:S(2)}) collective-permute-start(bf16[2,2,32,768]{3,2,1,0:T(8,128)(2,1)S(1)} %collective-permute-done.10.refs_4_), channel_id=1, source_target_pairs={{0,1},{1,0},{2,3},{3,2},{4,5},{5,4},{6,7},{7,6},{8,9},{9,8},{10,11... | collective-permute-start | bytes 589832 | tf_op jit(solution)/shard_map/ppermute | solution.py:265
  35.5 1.5 collective-permute-start.13
  37.0 0.7 copy-start.13
  147.0 17.7 %copy-start.8 = (bf16[384,768]{1,0:T(8,128)(2,1)S(1)}, bf16[384,768]{1,0:T(8,128)(2,1)}, u32[]{:S(2)}) copy-start(bf16[384,768]{1,0:T(8,128)(2,1)} %get-tuple-element.24) | copy-start | bytes 1769476
  147.0 17.7 %copy-start.9 = (bf16[384,768]{1,0:T(8,128)(2,1)S(1)}, bf16[384,768]{1,0:T(8,128)(2,1)}, u32[]{:S(2)}) copy-start(bf16[384,768]{1,0:T(8,128)(2,1)} %get-tuple-element.30) | copy-start | bytes 1769476
  147.0 1.9 %collective-permute-start.15 = (bf16[192,768]{1,0:T(8,128)(2,1)}, bf16[192,768]{1,0:T(8,128)(2,1)S(1)}, u32[]{:S(2)}, u32[]{:S(2)}) collective-permute-start(bf16[192,768]{1,0:T(8,128)(2,1)} %get-tuple-element.27), channel_id=1, source_target_pairs={{0,1},{1,0},{2,3},{3,2},{4,5},{5,4},{6,7},{7,6},{8,9},{9,8},{10,11... | collective-permute-start | bytes 884744 | tf_op jit(solution)/shard_map/ppermute | solution.py:265
  147.3 2.8 %collective-permute-start.17 = (bf16[192,768]{1,0:T(8,128)(2,1)}, bf16[192,768]{1,0:T(8,128)(2,1)S(1)}, u32[]{:S(2)}, u32[]{:S(2)}) collective-permute-start(bf16[192,768]{1,0:T(8,128)(2,1)} %get-tuple-element.29), channel_id=1, source_target_pairs={{0,1},{1,0},{2,3},{3,2},{4,5},{5,4},{6,7},{7,6},{8,9},{9,8},{10,11... | collective-permute-start | bytes 884744 | tf_op jit(solution)/shard_map/ppermute | solution.py:265
  147.6 5.0 %collective-permute-start.14 = (bf16[384,768]{1,0:T(8,128)(2,1)}, bf16[384,768]{1,0:T(8,128)(2,1)S(1)}, u32[]{:S(2)}, u32[]{:S(2)}) collective-permute-start(bf16[384,768]{1,0:T(8,128)(2,1)} %get-tuple-element.25), channel_id=1, source_target_pairs={{0,1},{1,0},{2,3},{3,2},{4,5},{5,4},{6,7},{7,6},{8,9},{9,8},{10,11... | collective-permute-start | bytes 1769480 | tf_op jit(solution)/shard_map/ppermute | solution.py:265
  149.9 8.4 %collective-permute-start.16 = (bf16[192,768]{1,0:T(8,128)(2,1)S(1)}, bf16[192,768]{1,0:T(8,128)(2,1)S(1)}, u32[]{:S(2)}, u32[]{:S(2)}) collective-permute-start(bf16[192,768]{1,0:T(8,128)(2,1)S(1)} %add_convert_fusion.3), channel_id=1, source_target_pairs={{0,2},{1,3},{2,0},{3,1},{4,6},{5,7},{6,4},{7,5},{8,10},{9,11},{10,... | collective-permute-start | bytes 884744 | tf_op jit(solution)/shard_map/ppermute | solution.py:265
  151.2 13.4 %collective-permute-start.18 = (bf16[192,768]{1,0:T(8,128)(2,1)S(1)}, bf16[192,768]{1,0:T(8,128)(2,1)S(1)}, u32[]{:S(2)}, u32[]{:S(2)}) collective-permute-start(bf16[192,768]{1,0:T(8,128)(2,1)S(1)} %add_convert_fusion.2), channel_id=1, source_target_pairs={{0,2},{1,3},{2,0},{3,1},{4,6},{5,7},{6,4},{7,5},{8,10},{9,11},{10,... | collective-permute-start | bytes 884744 | tf_op jit(solution)/shard_map/ppermute | solution.py:265

commit v8 on v7

--- a/solution.py
+++ b/solution.py
@@ -371,7 +371,7 @@
     parts = [half] + [permute(half, "seq", functools.partial(to_z, k)) for k in (1, 2, 3)]
     block = join(seq % 4, parts)
     pair = jnp.stack([block, permute(block, "seq", to_y)])
-    return [pair] + [permute(pair, "seq", functools.partial(to_x, k)) for k in (1, 2, 3)]
+    return block, [pair] + [permute(pair, "seq", functools.partial(to_x, k)) for k in (1, 2, 3)]
 
 
 def swap(x, bit):
@@ -396,15 +396,16 @@
     seq = lax.axis_index("seq")
     head = lax.axis_index("head")
     half = lax.dynamic_slice_in_dim(latents, (head % 2) * 32, 32, 0)
-    halves = all_latents(half)
+    joined, halves = all_latents(half)
 
     b0 = patch_bias.astype(BF16)
     b1 = (patch_bias - b0.astype(F32)).astype(BF16)
     b2 = (patch_bias - b0.astype(F32) - b1.astype(F32)).astype(BF16)
     rest = jnp.zeros((ROWS - 131, patch_bias.shape[0]), BF16)
     wide = jnp.concatenate([patch_weight, b0[None], b1[None], b2[None], rest], axis=0)
-    far_part = swap(wide, 2)
-    parts = [wide, swap(wide, 1), far_part, swap(far_part, 1)]
+    ready = lax.optimization_barrier((wide, joined))[0]
+    far_part = swap(ready, 2)
+    parts = [wide, swap(ready, 1), far_part, swap(far_part, 1)]
     mg, mq, mv = through(parts, norm_gain, query_weight, key_weight, value_weight)
     others = [swap(halves[0], 1)] + [
         swap(lax.optimization_barrier((part, mq))[0], 1) for part in halves[1:]

time: 166 us -> 168 us (1.012)
  starting transfers between devices: 22.9 us -> 25.2 us
  waiting for transfers between devices: 18 us -> 16.2 us
    ppermute x19, starting transfers between devices: 22.9 us -> 25.2 us  [permute(): lax.ppermute(x, axis, [(i, to(i)) for i in range(lax.axis_size(axis))])]
    ppermute x19, waiting for transfers between devices: 18 us -> 16.2 us  [permute(): lax.ppermute(x, axis, [(i, to(i)) for i in range(lax.axis_size(axis))])]
  transfers between devices with their start and end apart: 19 -> 19, of which waited for: 8 -> 8; matrix products, arithmetic and copies ran while one was open for 1% -> 2% of each run, Pallas kernels for 5% -> 5%
where the time goes in v8:
time: 168 us; the launch traced here: 167 us
  Pallas kernels  118 us (70%)
  starting transfers between devices  25.2 us (15%)
  waiting for transfers between devices  16.2 us (10%)
  other arithmetic  3.96 us (2%)
  local copies, waits for them, and re-layouts  3.36 us (2%)
    pallas_call x1, Pallas kernels, attention(): pl.pallas_call(kernel, in_specs=[pl.BlockSpec(memory_space=pltpu.SMEM)] *...  109 us
    ppermute x19, starting transfers between devices, permute(): lax.ppermute(x, axis, [(i, to(i)) for i in range(lax.axis_size(axis))])  25.2 us
    ppermute x19, waiting for transfers between devices, permute(): lax.ppermute(x, axis, [(i, to(i)) for i in range(lax.axis_size(axis))])  16.2 us
    pallas_call x1, Pallas kernels, through(): pl.pallas_call(weights_kernel, grid_spec=pltpu.PrefetchScalarGridSpec(num...  8.76 us
  transfers between devices with their start and end apart: 19, of which 8 were waited for; matrix products, arithmetic and copies ran while one was open for 2% of the time, Pallas kernels for 5%

profile of v8, /device:TPU:1, one launch (start us, length us, event | category | flops | bytes accessed | tf_op | source)
XLA Modules:
  0.0 167.1 jit_solution(12073036121416564870)
XLA Ops:
  0.0 0.8 copy-done
  0.8 4.6 %collective-permute-start.2 = (bf16[32,384]{1,0:T(8,128)(2,1)S(1)}, bf16[32,384]{1,0:T(8,128)(2,1)S(1)}, u32[]{:S(2)}, u32[]{:S(2)}) collective-permute-start(bf16[32,384]{1,0:T(8,128)(2,1)S(1)} %constant_dynamic-slice_fusion.p0), channel_id=1, source_target_pairs={{0,12},{4,0},{8,4},{12,8},{16,28},{20,16},{24,20},{28,24},{32,44},... | collective-permute-start | bytes 73736 | tf_op jit(solution)/shard_map/ppermute | solution.py:265
  5.4 0.0 collective-permute-start.1
  5.4 0.7 collective-permute-start
  6.1 0.8 subtract_convert_fusion
  6.9 1.1 concatenate.6.p0.refs_11_
  8.1 0.0 collective-permute-done.2.p3
  8.1 1.5 collective-permute-done.1.p2
  9.6 0.0 collective-permute-done.p1
  9.6 0.2 shard_map.154
  9.7 1.4 collective-permute-start.7
  11.1 2.6 %collective-permute-start.3 = (bf16[2,32,768]{2,1,0:T(8,128)(2,1)S(1)}, bf16[2,32,768]{2,1,0:T(8,128)(2,1)S(1)}, u32[]{:S(2)}, u32[]{:S(2)}) collective-permute-start(bf16[2,32,768]{2,1,0:T(8,128)(2,1)S(1)} %shard_map.154), channel_id=1, source_target_pairs={{0,16},{4,20},{8,24},{12,28},{16,0},{20,4},{24,8},{28,12},{32,48},... | collective-permute-start | bytes 294920 | tf_op jit(solution)/shard_map/ppermute | solution.py:265
  13.7 2.7 %collective-permute-start.6 = (bf16[144,768]{1,0:T(8,128)(2,1)S(1)}, bf16[144,768]{1,0:T(8,128)(2,1)S(1)}, u32[]{:S(2)}, u32[]{:S(2)}) collective-permute-start(bf16[144,768]{1,0:T(8,128)(2,1)S(1)} %concatenate.6.p0.refs_11_), channel_id=1, source_target_pairs={{0,1},{1,0},{2,3},{3,2},{4,5},{5,4},{6,7},{7,6},{8,9},{9,8},{10,11... | collective-permute-start | bytes 663560 | tf_op jit(solution)/shard_map/ppermute | solution.py:265
  16.4 0.0 collective-permute-done.7.p2
  16.4 2.3 %collective-permute-start.8 = (bf16[144,768]{1,0:T(8,128)(2,1)S(1)}, bf16[144,768]{1,0:T(8,128)(2,1)S(1)}, u32[]{:S(2)}, u32[]{:S(2)}) collective-permute-start(bf16[144,768]{1,0:T(8,128)(2,1)S(1)} %collective-permute-done.7.p2), channel_id=1, source_target_pairs={{0,1},{1,0},{2,3},{3,2},{4,5},{5,4},{6,7},{7,6},{8,9},{9,8},{10,11... | collective-permute-start | bytes 663560 | tf_op jit(solution)/shard_map/ppermute | solution.py:265
  18.7 0.2 collective-permute-done.3
  18.9 2.5 %collective-permute-start.12 = (bf16[2,2,32,768]{3,2,1,0:T(8,128)(2,1)S(1)}, bf16[2,2,32,768]{3,2,1,0:T(8,128)(2,1)S(1)}, u32[]{:S(2)}, u32[]{:S(2)}) collective-permute-start(bf16[2,2,32,768]{3,2,1,0:T(8,128)(2,1)S(1)} %pad_maximum_fusion.refs_0_), channel_id=1, source_target_pairs={{0,96},{4,100},{8,104},{12,108},{16,112},{20,116},{24,120},{28,124... | collective-permute-start | bytes 589832 | tf_op jit(solution)/shard_map/ppermute | solution.py:265
  21.5 0.5 collective-permute-start.10
  22.0 0.6 collective-permute-start.5
  22.6 4.2 %collective-permute-start.4 = (bf16[2,2,32,768]{3,2,1,0:T(8,128)(2,1)S(1)}, bf16[2,2,32,768]{3,2,1,0:T(8,128)(2,1)S(1)}, u32[]{:S(2)}, u32[]{:S(2)}) collective-permute-start(bf16[2,2,32,768]{3,2,1,0:T(8,128)(2,1)S(1)} %pad_maximum_fusion.refs_0_), channel_id=1, source_target_pairs={{0,1},{1,0},{2,3},{3,2},{4,5},{5,4},{6,7},{7,6},{8,9},{9,8},{10,11... | collective-permute-start | bytes 589832 | tf_op jit(solution)/shard_map/ppermute | solution.py:265
  26.8 0.7 copy-done.12
  27.5 0.0 copy-start.5
  27.5 0.0 copy-start.6
  27.5 8.8 %shard_map.155 = (bf16[1056,144]{1,0:T(8,128)(2,1)}, bf16[144,768]{1,0:T(8,128)(2,1)}, bf16[144,768]{1,0:T(8,128)(2,1)}) custom-call(s32[1]{0:T(128)} %bitcast.1.me.head_ref, bf16[144,768]{1,0:T(8,128)(2,1)} %copy-done.7, bf16[144,768]{1,0:T(8,128)(2,1)} %copy-done.11, bf16[144,768]{1,0:T(8,128)(2,1)} %copy-done.10, bf16[144,768]{1,0:T(8,128)(2,1)} %copy-done.12, ...), custom_call_target="tpu_custom_call" | custom-call | flops 212336640 | bytes 7077888 | tf_op jit(solution)/shard_map/pallas_call | solution.py:303
  36.3 0.0 collective-permute-done.10.refs_4_
  36.3 0.1 collective-permute-start.9
  36.4 0.4 collective-permute-start.11
  36.9 0.1 collective-permute-start.13
  37.0 0.0 collective-permute-done.4.refs_1_
  37.0 0.8 collective-permute-done.9.refs_3_
  37.8 0.3 collective-permute-done.11.refs_5_
  38.1 0.3 collective-permute-done.13.refs_7_
  38.4 0.7 copy-done.13
  39.1 109.2 %shard_map.156 = (bf16[384,768]{1,0:T(8,128)(2,1)}, bf16[384,768]{1,0:T(8,128)(2,1)}, bf16[192,768]{1,0:T(8,128)(2,1)}, bf16[192,768]{1,0:T(8,128)(2,1)}, bf16[1...) custom-call(s32[1]{0:T(128)} %bitcast.seq_ref, s32[1]{0:T(128)} %bitcast.1.me.head_ref, ...), custom_call_target="tpu_custom_call" | custom-call | tf_op jit(solution)/shard_map/pallas_call | solution.py:239
  148.3 0.0 copy-start.8
  148.4 0.3 collective-permute-start.15
  148.7 0.3 collective-permute-start.17
  148.9 0.2 collective-permute-start.14
  149.2 1.0 collective-permute-done.15
  150.2 1.0 add_convert_fusion.3
  151.3 0.1 collective-permute-start.16
  151.4 0.0 collective-permute-done.17
  151.4 1.0 add_convert_fusion.2
  152.4 1.5 collective-permute-start.18
  153.9 5.8 %collective-permute-done.16 = bf16[192,768]{1,0:T(8,128)(2,1)S(1)} collective-permute-done((bf16[192,768]{1,0:T(8,128)(2,1)S(1)}, bf16[192,768]{1,0:T(8,128)(2,1)S(1)}, u32[]{:S(2)}, u32[]{:S(2)}) %collective-permute-start.16) | collective-permute-done | bytes 294944 | tf_op jit(solution)/shard_map/ppermute | solution.py:265
  159.7 6.3 %collective-permute-done.18 = bf16[192,768]{1,0:T(8,128)(2,1)S(1)} collective-permute-done((bf16[192,768]{1,0:T(8,128)(2,1)S(1)}, bf16[192,768]{1,0:T(8,128)(2,1)S(1)}, u32[]{:S(2)}, u32[]{:S(2)}) %collective-permute-start.18) | collective-permute-done | bytes 294944 | tf_op jit(solution)/shard_map/ppermute | solution.py:265
  166.0 0.0 collective-permute-done.14
  166.0 1.1 add_convert_fusion
  (32 shorter events, 0.1 us)
Async XLA Ops:
  0.0 0.8 copy-start
  0.8 7.3 %collective-permute-start.2 = (bf16[32,384]{1,0:T(8,128)(2,1)S(1)}, bf16[32,384]{1,0:T(8,128)(2,1)S(1)}, u32[]{:S(2)}, u32[]{:S(2)}) collective-permute-start(bf16[32,384]{1,0:T(8,128)(2,1)S(1)} %constant_dynamic-slice_fusion.p0), channel_id=1, source_target_pairs={{0,12},{4,0},{8,4},{12,8},{16,28},{20,16},{24,20},{28,24},{32,44},... | collective-permute-start | bytes 73736 | tf_op jit(solution)/shard_map/ppermute | solution.py:265
  5.4 4.2 %collective-permute-start.1 = (bf16[32,384]{1,0:T(8,128)(2,1)S(1)}, bf16[32,384]{1,0:T(8,128)(2,1)S(1)}, u32[]{:S(2)}, u32[]{:S(2)}) collective-permute-start(bf16[32,384]{1,0:T(8,128)(2,1)S(1)} %constant_dynamic-slice_fusion.p0), channel_id=1, source_target_pairs={{0,8},{4,12},{8,0},{12,4},{16,24},{20,28},{24,16},{28,20},{32,40},... | collective-permute-start | bytes 73736 | tf_op jit(solution)/shard_map/ppermute | solution.py:265
  5.4 4.2 %collective-permute-start = (bf16[32,384]{1,0:T(8,128)(2,1)S(1)}, bf16[32,384]{1,0:T(8,128)(2,1)S(1)}, u32[]{:S(2)}, u32[]{:S(2)}) collective-permute-start(bf16[32,384]{1,0:T(8,128)(2,1)S(1)} %constant_dynamic-slice_fusion.p0), channel_id=1, source_target_pairs={{0,4},{4,8},{8,12},{12,0},{16,20},{20,24},{24,28},{28,16},{32,36},... | collective-permute-start | bytes 73736 | tf_op jit(solution)/shard_map/ppermute | solution.py:265
  8.1 18.7 %copy-start.7 = (bf16[144,768]{1,0:T(8,128)(2,1)}, bf16[144,768]{1,0:T(8,128)(2,1)S(1)}, u32[]{:S(2)}) copy-start(bf16[144,768]{1,0:T(8,128)(2,1)S(1)} %concatenate.6.p0.refs_11_) | copy-start | bytes 663556
  9.7 6.7 %collective-permute-start.7 = (bf16[144,768]{1,0:T(8,128)(2,1)S(1)}, bf16[144,768]{1,0:T(8,128)(2,1)S(1)}, u32[]{:S(2)}, u32[]{:S(2)}) collective-permute-start(bf16[144,768]{1,0:T(8,128)(2,1)S(1)} %concatenate.6.p0.refs_11_), channel_id=1, source_target_pairs={{0,2},{1,3},{2,0},{3,1},{4,6},{5,7},{6,4},{7,5},{8,10},{9,11},{10,... | collective-permute-start | bytes 663560 | tf_op jit(solution)/shard_map/ppermute | solution.py:265
  11.1 7.8 %collective-permute-start.3 = (bf16[2,32,768]{2,1,0:T(8,128)(2,1)S(1)}, bf16[2,32,768]{2,1,0:T(8,128)(2,1)S(1)}, u32[]{:S(2)}, u32[]{:S(2)}) collective-permute-start(bf16[2,32,768]{2,1,0:T(8,128)(2,1)S(1)} %shard_map.154), channel_id=1, source_target_pairs={{0,16},{4,20},{8,24},{12,28},{16,0},{20,4},{24,8},{28,12},{32,48},... | collective-permute-start | bytes 294920 | tf_op jit(solution)/shard_map/ppermute | solution.py:265
  13.7 8.9 %collective-permute-start.6 = (bf16[144,768]{1,0:T(8,128)(2,1)S(1)}, bf16[144,768]{1,0:T(8,128)(2,1)S(1)}, u32[]{:S(2)}, u32[]{:S(2)}) collective-permute-start(bf16[144,768]{1,0:T(8,128)(2,1)S(1)} %concatenate.6.p0.refs_11_), channel_id=1, source_target_pairs={{0,1},{1,0},{2,3},{3,2},{4,5},{5,4},{6,7},{7,6},{8,9},{9,8},{10,11... | collective-permute-start | bytes 663560 | tf_op jit(solution)/shard_map/ppermute | solution.py:265
  16.4 10.4 %copy-start.10 = (bf16[144,768]{1,0:T(8,128)(2,1)}, bf16[144,768]{1,0:T(8,128)(2,1)S(1)}, u32[]{:S(2)}) copy-start(bf16[144,768]{1,0:T(8,128)(2,1)S(1)} %collective-permute-done.7.p2) | copy-start | bytes 663556
  16.4 10.4 %collective-permute-start.8 = (bf16[144,768]{1,0:T(8,128)(2,1)S(1)}, bf16[144,768]{1,0:T(8,128)(2,1)S(1)}, u32[]{:S(2)}, u32[]{:S(2)}) collective-permute-start(bf16[144,768]{1,0:T(8,128)(2,1)S(1)} %collective-permute-done.7.p2), channel_id=1, source_target_pairs={{0,1},{1,0},{2,3},{3,2},{4,5},{5,4},{6,7},{7,6},{8,9},{9,8},{10,11... | collective-permute-start | bytes 663560 | tf_op jit(solution)/shard_map/ppermute | solution.py:265
  18.9 17.3 %collective-permute-start.12 = (bf16[2,2,32,768]{3,2,1,0:T(8,128)(2,1)S(1)}, bf16[2,2,32,768]{3,2,1,0:T(8,128)(2,1)S(1)}, u32[]{:S(2)}, u32[]{:S(2)}) collective-permute-start(bf16[2,2,32,768]{3,2,1,0:T(8,128)(2,1)S(1)} %pad_maximum_fusion.refs_0_), channel_id=1, source_target_pairs={{0,96},{4,100},{8,104},{12,108},{16,112},{20,116},{24,120},{28,124... | collective-permute-start | bytes 589832 | tf_op jit(solution)/shard_map/ppermute | solution.py:265
  21.5 14.8 %collective-permute-start.10 = (bf16[2,2,32,768]{3,2,1,0:T(8,128)(2,1)S(1)}, bf16[2,2,32,768]{3,2,1,0:T(8,128)(2,1)S(1)}, u32[]{:S(2)}, u32[]{:S(2)}) collective-permute-start(bf16[2,2,32,768]{3,2,1,0:T(8,128)(2,1)S(1)} %pad_maximum_fusion.refs_0_), channel_id=1, source_target_pairs={{0,64},{4,68},{8,72},{12,76},{16,80},{20,84},{24,88},{28,92},{32,9... | collective-permute-start | bytes 589832 | tf_op jit(solution)/shard_map/ppermute | solution.py:265
  22.0 14.3 %collective-permute-start.5 = (bf16[2,2,32,768]{3,2,1,0:T(8,128)(2,1)S(1)}, bf16[2,2,32,768]{3,2,1,0:T(8,128)(2,1)S(1)}, u32[]{:S(2)}, u32[]{:S(2)}) collective-permute-start(bf16[2,2,32,768]{3,2,1,0:T(8,128)(2,1)S(1)} %pad_maximum_fusion.refs_0_), channel_id=1, source_target_pairs={{0,32},{4,36},{8,40},{12,44},{16,48},{20,52},{24,56},{28,60},{32,6... | collective-permute-start | bytes 589832 | tf_op jit(solution)/shard_map/ppermute | solution.py:265
  22.6 4.2 %copy-start.11 = (bf16[144,768]{1,0:T(8,128)(2,1)}, bf16[144,768]{1,0:T(8,128)(2,1)S(1)}, u32[]{:S(2)}) copy-start(bf16[144,768]{1,0:T(8,128)(2,1)S(1)} %collective-permute-done.6.p1) | copy-start | bytes 663556
  22.6 14.4 %collective-permute-start.4 = (bf16[2,2,32,768]{3,2,1,0:T(8,128)(2,1)S(1)}, bf16[2,2,32,768]{3,2,1,0:T(8,128)(2,1)S(1)}, u32[]{:S(2)}, u32[]{:S(2)}) collective-permute-start(bf16[2,2,32,768]{3,2,1,0:T(8,128)(2,1)S(1)} %pad_maximum_fusion.refs_0_), channel_id=1, source_target_pairs={{0,1},{1,0},{2,3},{3,2},{4,5},{5,4},{6,7},{7,6},{8,9},{9,8},{10,11... | collective-permute-start | bytes 589832 | tf_op jit(solution)/shard_map/ppermute | solution.py:265
  26.8 0.7 copy-start.12
  27.5 11.6 %copy-start.1 = (f32[48,768]{1,0:T(8,128)S(1)}, f32[48,768]{1,0:T(8,128)}, u32[]{:S(2)}) copy-start(f32[48,768]{1,0:T(8,128)} %constant.54.clone.refs_13_) | copy-start | bytes 442372
  27.5 11.6 %copy-start.2 = (f32[48,768]{1,0:T(8,128)S(1)}, f32[48,768]{1,0:T(8,128)}, u32[]{:S(2)}) copy-start(f32[48,768]{1,0:T(8,128)} %constant.53.clone.refs_12_) | copy-start | bytes 442372
  27.5 11.6 %copy-start.3 = (f32[192,128]{1,0:T(8,128)S(1)}, f32[192,128]{1,0:T(8,128)}, u32[]{:S(2)}) copy-start(f32[192,128]{1,0:T(8,128)} %constant.58.clone.refs_17_) | copy-start | bytes 294916
  27.5 11.6 %copy-start.4 = (f32[192,128]{1,0:T(8,128)S(1)}, f32[192,128]{1,0:T(8,128)}, u32[]{:S(2)}) copy-start(f32[192,128]{1,0:T(8,128)} %constant.57.clone.refs_16_) | copy-start | bytes 294916
  27.5 11.6 %copy-start.5 = (f32[2,64,128]{2,1,0:T(8,128)S(1)}, f32[2,64,128]{2,1,0:T(8,128)}, u32[]{:S(2)}) copy-start(f32[2,64,128]{2,1,0:T(8,128)} %constant.59.clone.refs_18_) | copy-start | bytes 196612
  27.5 11.6 %copy-start.6 = (s32[64]{0:T(128)S(1)}, s32[64]{0:T(128)}, u32[]{:S(2)}) copy-start(s32[64]{0:T(128)} %span_ref.1) | copy-start | bytes 772
  36.3 1.5 collective-permute-start.9
  36.4 1.7 collective-permute-start.11
  36.9 1.5 collective-permute-start.13
  38.4 0.7 copy-start.13
  148.3 17.7 %copy-start.8 = (bf16[384,768]{1,0:T(8,128)(2,1)S(1)}, bf16[384,768]{1,0:T(8,128)(2,1)}, u32[]{:S(2)}) copy-start(bf16[384,768]{1,0:T(8,128)(2,1)} %get-tuple-element.26) | copy-start | bytes 1769476
  148.3 17.7 %copy-start.9 = (bf16[384,768]{1,0:T(8,128)(2,1)S(1)}, bf16[384,768]{1,0:T(8,128)(2,1)}, u32[]{:S(2)}) copy-start(bf16[384,768]{1,0:T(8,128)(2,1)} %get-tuple-element.32) | copy-start | bytes 1769476
  148.4 1.9 %collective-permute-start.15 = (bf16[192,768]{1,0:T(8,128)(2,1)}, bf16[192,768]{1,0:T(8,128)(2,1)S(1)}, u32[]{:S(2)}, u32[]{:S(2)}) collective-permute-start(bf16[192,768]{1,0:T(8,128)(2,1)} %get-tuple-element.29), channel_id=1, source_target_pairs={{0,1},{1,0},{2,3},{3,2},{4,5},{5,4},{6,7},{7,6},{8,9},{9,8},{10,11... | collective-permute-start | bytes 884744 | tf_op jit(solution)/shard_map/ppermute | solution.py:265
  148.7 2.7 %collective-permute-start.17 = (bf16[192,768]{1,0:T(8,128)(2,1)}, bf16[192,768]{1,0:T(8,128)(2,1)S(1)}, u32[]{:S(2)}, u32[]{:S(2)}) collective-permute-start(bf16[192,768]{1,0:T(8,128)(2,1)} %get-tuple-element.31), channel_id=1, source_target_pairs={{0,1},{1,0},{2,3},{3,2},{4,5},{5,4},{6,7},{7,6},{8,9},{9,8},{10,11... | collective-permute-start | bytes 884744 | tf_op jit(solution)/shard_map/ppermute | solution.py:265
  148.9 17.1 %collective-permute-start.14 = (bf16[384,768]{1,0:T(8,128)(2,1)}, bf16[384,768]{1,0:T(8,128)(2,1)S(1)}, u32[]{:S(2)}, u32[]{:S(2)}) collective-permute-start(bf16[384,768]{1,0:T(8,128)(2,1)} %get-tuple-element.27), channel_id=1, source_target_pairs={{0,1},{1,0},{2,3},{3,2},{4,5},{5,4},{6,7},{7,6},{8,9},{9,8},{10,11... | collective-permute-start | bytes 1769480 | tf_op jit(solution)/shard_map/ppermute | solution.py:265
  151.3 8.4 %collective-permute-start.16 = (bf16[192,768]{1,0:T(8,128)(2,1)S(1)}, bf16[192,768]{1,0:T(8,128)(2,1)S(1)}, u32[]{:S(2)}, u32[]{:S(2)}) collective-permute-start(bf16[192,768]{1,0:T(8,128)(2,1)S(1)} %add_convert_fusion.3), channel_id=1, source_target_pairs={{0,2},{1,3},{2,0},{3,1},{4,6},{5,7},{6,4},{7,5},{8,10},{9,11},{10,... | collective-permute-start | bytes 884744 | tf_op jit(solution)/shard_map/ppermute | solution.py:265
  152.4 13.6 %collective-permute-start.18 = (bf16[192,768]{1,0:T(8,128)(2,1)S(1)}, bf16[192,768]{1,0:T(8,128)(2,1)S(1)}, u32[]{:S(2)}, u32[]{:S(2)}) collective-permute-start(bf16[192,768]{1,0:T(8,128)(2,1)S(1)} %add_convert_fusion.2), channel_id=1, source_target_pairs={{0,2},{1,3},{2,0},{3,1},{4,6},{5,7},{6,4},{7,5},{8,10},{9,11},{10,... | collective-permute-start | bytes 884744 | tf_op jit(solution)/shard_map/ppermute | solution.py:265

commit v9 on v7

--- a/solution.py
+++ b/solution.py
@@ -273,7 +273,10 @@
         for ref in (aq, ak, av, ag):
             ref[...] = jnp.zeros_like(ref)
 
-    part = jnp.where(k < 2, jnp.where(k == 0, p0[...], p1[...]), jnp.where(k == 2, p2[...], p3[...]))
+    n, half = k // 2, pl.ds(pl.multiple_of((k % 2) * wq.shape[0], 128), wq.shape[0])
+    part = jnp.where(
+        n < 2, jnp.where(n == 0, p0[:, half], p1[:, half]), jnp.where(n == 2, p2[:, half], p3[:, half])
+    )
     wide = part.astype(F32)
     bias = wide[128:129] + wide[129:130] + wide[130:131]
     row = lax.broadcasted_iota(jnp.int32, (ROWS - 128, part.shape[1]), 0)
@@ -284,12 +287,12 @@
     av[...] += dot(gained, wv[...])
     ag[...] += lax.dot_general(part, part, (((1,), (1,)), ((), ())), preferred_element_type=F32)
 
-    @pl.when(k == 3)
+    @pl.when(k == 7)
     def _():
         mq_ref[...] = aq[...].astype(BF16)
         mv_ref[...] = av[...].astype(BF16)
         mg_ref[: HEADS * HD, :] = ak[...].T.astype(BF16)
-        gram = ag[...] * (1.0 / (4 * part.shape[1]))
+        gram = ag[...] * (1.0 / (8 * part.shape[1]))
         high = gram.astype(BF16)
         mg_ref[HEADS * HD : HEADS * HD + ROWS, :] = high
         mg_ref[HEADS * HD + ROWS :, :] = (gram - high.astype(F32)).astype(BF16)
@@ -298,15 +301,15 @@
 def through(parts, gain, wq, wk, wv):
     columns = HEADS * HD
     whole = lambda *shape: pl.BlockSpec(shape, lambda k, me: (0,) * len(shape))
-    source = lambda k, me: me[0] ^ k
-    weight = pl.BlockSpec((columns, columns), lambda k, me: (source(k, me), 0))
+    source = lambda k, me: (me[0] ^ (k // 2)) * 2 + k % 2
+    weight = pl.BlockSpec((columns // 2, columns), lambda k, me: (source(k, me), 0))
     return pl.pallas_call(
         weights_kernel,
         grid_spec=pltpu.PrefetchScalarGridSpec(
             num_scalar_prefetch=1,
-            grid=(4,),
+            grid=(8,),
             in_specs=[whole(ROWS, columns)] * 4
-            + [pl.BlockSpec((1, 1, columns), lambda k, me: (source(k, me), 0, 0))]
+            + [pl.BlockSpec((1, 1, columns // 2), lambda k, me: (source(k, me), 0, 0))]
             + [weight] * 3,
             out_specs=[
                 whole(columns + 2 * ROWS, ROWS),
@@ -324,7 +327,7 @@
         cost_estimate=pl.CostEstimate(
             flops=2 * ROWS * 3072 * 240, bytes_accessed=3 * 3072 * 768, transcendentals=0
         ),
-    )(lax.axis_index("head").astype(jnp.int32).reshape(1), *parts, gain.reshape(4, 1, columns), wq, wk, wv)
+    )(lax.axis_index("head").astype(jnp.int32).reshape(1), *parts, gain.reshape(8, 1, columns // 2), wq, wk, wv)
 
 
 def join_kernel(z, p0, p1, p2, p3, out):

time: 166 us -> 168 us (1.012)
  Pallas kernels: 118 us -> 120 us
    pallas_call x1, Pallas kernels: 8.76 us -> 11 us  [through(): pl.pallas_call(weights_kernel, grid_spec=pltpu.PrefetchScalarGridSpec(num...]
  transfers between devices with their start and end apart: 19 -> 19, of which waited for: 8 -> 8; matrix products, arithmetic and copies ran while one was open for 1% -> 1% of each run, Pallas kernels for 5% -> 7%
where the time goes in v9:
time: 168 us
  Pallas kernels  120 us (71%)
  starting transfers between devices  22.9 us (14%)
  waiting for transfers between devices  18 us (11%)
  other arithmetic  3.96 us (2%)
  local copies, waits for them, and re-layouts  2.57 us (2%)
    pallas_call x1, Pallas kernels, attention(): pl.pallas_call(kernel, in_specs=[pl.BlockSpec(memory_space=pltpu.SMEM)] *...  109 us
    ppermute x19, starting transfers between devices, permute(): lax.ppermute(x, axis, [(i, to(i)) for i in range(lax.axis_size(axis))])  22.9 us
    ppermute x19, waiting for transfers between devices, permute(): lax.ppermute(x, axis, [(i, to(i)) for i in range(lax.axis_size(axis))])  18 us
    pallas_call x1, Pallas kernels, through(): pl.pallas_call(weights_kernel, grid_spec=pltpu.PrefetchScalarGridSpec(num...  11 us
  transfers between devices with their start and end apart: 19, of which 8 were waited for; matrix products, arithmetic and copies ran while one was open for 1% of the time, Pallas kernels for 7%

profile of v9, /device:TPU:1, one launch (start us, length us, event | category | flops | bytes accessed | tf_op | source)
XLA Modules:
  0.0 168.0 jit_solution(466669595219662315)
XLA Ops:
  0.0 0.8 subtract_convert_fusion
  0.8 1.1 concatenate.6.p0.refs_11_
  2.0 2.2 %collective-permute-start.7 = (bf16[144,768]{1,0:T(8,128)(2,1)S(1)}, bf16[144,768]{1,0:T(8,128)(2,1)S(1)}, u32[]{:S(2)}, u32[]{:S(2)}) collective-permute-start(bf16[144,768]{1,0:T(8,128)(2,1)S(1)} %concatenate.6.p0.refs_11_), channel_id=1, source_target_pairs={{0,2},{1,3},{2,0},{3,1},{4,6},{5,7},{6,4},{7,5},{8,10},{9,11},{10,... | collective-permute-start | bytes 663560 | tf_op jit(solution)/shard_map/ppermute | solution.py:265
  4.2 3.8 %collective-permute-start.2 = (bf16[32,384]{1,0:T(8,128)(2,1)S(1)}, bf16[32,384]{1,0:T(8,128)(2,1)S(1)}, u32[]{:S(2)}, u32[]{:S(2)}) collective-permute-start(bf16[32,384]{1,0:T(8,128)(2,1)S(1)} %constant_dynamic-slice_fusion.p0), channel_id=1, source_target_pairs={{0,12},{4,0},{8,4},{12,8},{16,28},{20,16},{24,20},{28,24},{32,44},... | collective-permute-start | bytes 73736 | tf_op jit(solution)/shard_map/ppermute | solution.py:265
  7.9 0.0 collective-permute-start.1
  7.9 0.7 collective-permute-start
  8.6 0.2 collective-permute-done.2.p3
  8.9 3.2 %collective-permute-done.1.p2 = bf16[32,384]{1,0:T(8,128)(2,1)S(1)} collective-permute-done((bf16[32,384]{1,0:T(8,128)(2,1)S(1)}, bf16[32,384]{1,0:T(8,128)(2,1)S(1)}, u32[]{:S(2)}, u32[]{:S(2)}) %collective-permute-start.1) | collective-permute-done | bytes 24608 | tf_op jit(solution)/shard_map/ppermute | solution.py:265
  12.1 0.0 collective-permute-done.p1
  12.1 0.2 shard_map.154
  12.3 2.7 %collective-permute-start.3 = (bf16[2,32,768]{2,1,0:T(8,128)(2,1)S(1)}, bf16[2,32,768]{2,1,0:T(8,128)(2,1)S(1)}, u32[]{:S(2)}, u32[]{:S(2)}) collective-permute-start(bf16[2,32,768]{2,1,0:T(8,128)(2,1)S(1)} %shard_map.154), channel_id=1, source_target_pairs={{0,16},{4,20},{8,24},{12,28},{16,0},{20,4},{24,8},{28,12},{32,48},... | collective-permute-start | bytes 294920 | tf_op jit(solution)/shard_map/ppermute | solution.py:265
  15.0 2.7 %collective-permute-start.6 = (bf16[144,768]{1,0:T(8,128)(2,1)S(1)}, bf16[144,768]{1,0:T(8,128)(2,1)S(1)}, u32[]{:S(2)}, u32[]{:S(2)}) collective-permute-start(bf16[144,768]{1,0:T(8,128)(2,1)S(1)} %concatenate.6.p0.refs_11_), channel_id=1, source_target_pairs={{0,1},{1,0},{2,3},{3,2},{4,5},{5,4},{6,7},{7,6},{8,9},{9,8},{10,11... | collective-permute-start | bytes 663560 | tf_op jit(solution)/shard_map/ppermute | solution.py:265
  17.7 0.0 collective-permute-done.7.p2
  17.7 0.1 collective-permute-start.8
  17.7 0.0 collective-permute-done.3
  17.8 2.5 %collective-permute-start.12 = (bf16[2,2,32,768]{3,2,1,0:T(8,128)(2,1)S(1)}, bf16[2,2,32,768]{3,2,1,0:T(8,128)(2,1)S(1)}, u32[]{:S(2)}, u32[]{:S(2)}) collective-permute-start(bf16[2,2,32,768]{3,2,1,0:T(8,128)(2,1)S(1)} %pad_maximum_fusion.refs_0_), channel_id=1, source_target_pairs={{0,96},{4,100},{8,104},{12,108},{16,112},{20,116},{24,120},{28,124... | collective-permute-start | bytes 589832 | tf_op jit(solution)/shard_map/ppermute | solution.py:265
  20.3 0.5 collective-permute-start.10
  20.8 0.6 collective-permute-start.5
  21.5 4.0 %collective-permute-start.4 = (bf16[2,2,32,768]{3,2,1,0:T(8,128)(2,1)S(1)}, bf16[2,2,32,768]{3,2,1,0:T(8,128)(2,1)S(1)}, u32[]{:S(2)}, u32[]{:S(2)}) collective-permute-start(bf16[2,2,32,768]{3,2,1,0:T(8,128)(2,1)S(1)} %pad_maximum_fusion.refs_0_), channel_id=1, source_target_pairs={{0,1},{1,0},{2,3},{3,2},{4,5},{5,4},{6,7},{7,6},{8,9},{9,8},{10,11... | collective-permute-start | bytes 589832 | tf_op jit(solution)/shard_map/ppermute | solution.py:265
  25.4 0.0 collective-permute-done.8.p3
  25.4 0.7 copy-done.12
  26.1 0.0 copy-start.5
  26.2 0.0 copy-start.6
  26.2 11.0 %shard_map.155 = (bf16[1056,144]{1,0:T(8,128)(2,1)}, bf16[144,768]{1,0:T(8,128)(2,1)}, bf16[144,768]{1,0:T(8,128)(2,1)}) custom-call(s32[1]{0:T(128)} %bitcast.1.me.head_ref, bf16[144,768]{1,0:T(8,128)(2,1)} %copy-done.7, bf16[144,768]{1,0:T(8,128)(2,1)} %copy-done.11, bf16[144,768]{1,0:T(8,128)(2,1)} %copy-done.10, bf16[144,768]{1,0:T(8,128)(2,1)} %copy-done.12, ...), custom_call_target="tpu_custom_call" | custom-call | flops 212336640 | bytes 7077888 | tf_op jit(solution)/shard_map/pallas_call | solution.py:306
  37.1 0.0 collective-permute-done.12.refs_6_
  37.1 0.0 collective-permute-done.10.refs_4_
  37.1 0.1 collective-permute-start.9
  37.3 0.4 collective-permute-start.11
  37.7 0.1 collective-permute-start.13
  37.8 0.0 collective-permute-done.4.refs_1_
  37.8 0.8 collective-permute-done.9.refs_3_
  38.7 0.3 collective-permute-done.11.refs_5_
  39.0 0.3 collective-permute-done.13.refs_7_
  39.2 0.7 copy-done.13
  39.9 109.2 %shard_map.156 = (bf16[384,768]{1,0:T(8,128)(2,1)}, bf16[384,768]{1,0:T(8,128)(2,1)}, bf16[192,768]{1,0:T(8,128)(2,1)}, bf16[192,768]{1,0:T(8,128)(2,1)}, bf16[1...) custom-call(s32[1]{0:T(128)} %bitcast.seq_ref, s32[1]{0:T(128)} %bitcast.1.me.head_ref, ...), custom_call_target="tpu_custom_call" | custom-call | tf_op jit(solution)/shard_map/pallas_call | solution.py:239
  149.2 0.0 copy-start.8
  149.2 0.3 collective-permute-start.15
  149.5 0.2 collective-permute-start.17
  149.8 0.3 collective-permute-start.14
  150.0 1.0 collective-permute-done.15
  151.1 1.0 add_convert_fusion.3
  152.1 0.2 collective-permute-start.16
  152.3 1.0 add_convert_fusion.2
  153.4 1.4 collective-permute-start.18
  154.8 0.0 collective-permute-done.14
  154.8 5.8 %collective-permute-done.16 = bf16[192,768]{1,0:T(8,128)(2,1)S(1)} collective-permute-done((bf16[192,768]{1,0:T(8,128)(2,1)S(1)}, bf16[192,768]{1,0:T(8,128)(2,1)S(1)}, u32[]{:S(2)}, u32[]{:S(2)}) %collective-permute-start.16) | collective-permute-done | bytes 294944 | tf_op jit(solution)/shard_map/ppermute | solution.py:265
  160.5 6.3 %collective-permute-done.18 = bf16[192,768]{1,0:T(8,128)(2,1)S(1)} collective-permute-done((bf16[192,768]{1,0:T(8,128)(2,1)S(1)}, bf16[192,768]{1,0:T(8,128)(2,1)S(1)}, u32[]{:S(2)}, u32[]{:S(2)}) %collective-permute-start.18) | collective-permute-done | bytes 294944 | tf_op jit(solution)/shard_map/ppermute | solution.py:265
  166.8 1.1 add_convert_fusion
  (32 shorter events, 0.1 us)
Async XLA Ops:
  0.0 4.2 %copy-start = (bf16[64,384]{1,0:T(8,128)(2,1)S(1)}, bf16[64,384]{1,0:T(8,128)(2,1)}, u32[]{:S(2)}) copy-start(bf16[64,384]{1,0:T(8,128)(2,1)} %param.16) | copy-start | bytes 147460
  2.0 23.5 %copy-start.7 = (bf16[144,768]{1,0:T(8,128)(2,1)}, bf16[144,768]{1,0:T(8,128)(2,1)S(1)}, u32[]{:S(2)}) copy-start(bf16[144,768]{1,0:T(8,128)(2,1)S(1)} %concatenate.6.p0.refs_11_) | copy-start | bytes 663556
  2.0 15.7 %collective-permute-start.7 = (bf16[144,768]{1,0:T(8,128)(2,1)S(1)}, bf16[144,768]{1,0:T(8,128)(2,1)S(1)}, u32[]{:S(2)}, u32[]{:S(2)}) collective-permute-start(bf16[144,768]{1,0:T(8,128)(2,1)S(1)} %concatenate.6.p0.refs_11_), channel_id=1, source_target_pairs={{0,2},{1,3},{2,0},{3,1},{4,6},{5,7},{6,4},{7,5},{8,10},{9,11},{10,... | collective-permute-start | bytes 663560 | tf_op jit(solution)/shard_map/ppermute | solution.py:265
  4.2 4.7 %collective-permute-start.2 = (bf16[32,384]{1,0:T(8,128)(2,1)S(1)}, bf16[32,384]{1,0:T(8,128)(2,1)S(1)}, u32[]{:S(2)}, u32[]{:S(2)}) collective-permute-start(bf16[32,384]{1,0:T(8,128)(2,1)S(1)} %constant_dynamic-slice_fusion.p0), channel_id=1, source_target_pairs={{0,12},{4,0},{8,4},{12,8},{16,28},{20,16},{24,20},{28,24},{32,44},... | collective-permute-start | bytes 73736 | tf_op jit(solution)/shard_map/ppermute | solution.py:265
  7.9 4.2 %collective-permute-start.1 = (bf16[32,384]{1,0:T(8,128)(2,1)S(1)}, bf16[32,384]{1,0:T(8,128)(2,1)S(1)}, u32[]{:S(2)}, u32[]{:S(2)}) collective-permute-start(bf16[32,384]{1,0:T(8,128)(2,1)S(1)} %constant_dynamic-slice_fusion.p0), channel_id=1, source_target_pairs={{0,8},{4,12},{8,0},{12,4},{16,24},{20,28},{24,16},{28,20},{32,40},... | collective-permute-start | bytes 73736 | tf_op jit(solution)/shard_map/ppermute | solution.py:265
  7.9 4.2 %collective-permute-start = (bf16[32,384]{1,0:T(8,128)(2,1)S(1)}, bf16[32,384]{1,0:T(8,128)(2,1)S(1)}, u32[]{:S(2)}, u32[]{:S(2)}) collective-permute-start(bf16[32,384]{1,0:T(8,128)(2,1)S(1)} %constant_dynamic-slice_fusion.p0), channel_id=1, source_target_pairs={{0,4},{4,8},{8,12},{12,0},{16,20},{20,24},{24,28},{28,16},{32,36},... | collective-permute-start | bytes 73736 | tf_op jit(solution)/shard_map/ppermute | solution.py:265
  12.3 5.5 %collective-permute-start.3 = (bf16[2,32,768]{2,1,0:T(8,128)(2,1)S(1)}, bf16[2,32,768]{2,1,0:T(8,128)(2,1)S(1)}, u32[]{:S(2)}, u32[]{:S(2)}) collective-permute-start(bf16[2,32,768]{2,1,0:T(8,128)(2,1)S(1)} %shard_map.154), channel_id=1, source_target_pairs={{0,16},{4,20},{8,24},{12,28},{16,0},{20,4},{24,8},{28,12},{32,48},... | collective-permute-start | bytes 294920 | tf_op jit(solution)/shard_map/ppermute | solution.py:265
  15.0 6.5 %collective-permute-start.6 = (bf16[144,768]{1,0:T(8,128)(2,1)S(1)}, bf16[144,768]{1,0:T(8,128)(2,1)S(1)}, u32[]{:S(2)}, u32[]{:S(2)}) collective-permute-start(bf16[144,768]{1,0:T(8,128)(2,1)S(1)} %concatenate.6.p0.refs_11_), channel_id=1, source_target_pairs={{0,1},{1,0},{2,3},{3,2},{4,5},{5,4},{6,7},{7,6},{8,9},{9,8},{10,11... | collective-permute-start | bytes 663560 | tf_op jit(solution)/shard_map/ppermute | solution.py:265
  17.7 7.8 %copy-start.10 = (bf16[144,768]{1,0:T(8,128)(2,1)}, bf16[144,768]{1,0:T(8,128)(2,1)S(1)}, u32[]{:S(2)}) copy-start(bf16[144,768]{1,0:T(8,128)(2,1)S(1)} %collective-permute-done.7.p2) | copy-start | bytes 663556
  17.7 7.8 %collective-permute-start.8 = (bf16[144,768]{1,0:T(8,128)(2,1)S(1)}, bf16[144,768]{1,0:T(8,128)(2,1)S(1)}, u32[]{:S(2)}, u32[]{:S(2)}) collective-permute-start(bf16[144,768]{1,0:T(8,128)(2,1)S(1)} %collective-permute-done.7.p2), channel_id=1, source_target_pairs={{0,1},{1,0},{2,3},{3,2},{4,5},{5,4},{6,7},{7,6},{8,9},{9,8},{10,11... | collective-permute-start | bytes 663560 | tf_op jit(solution)/shard_map/ppermute | solution.py:265
  17.8 19.3 %collective-permute-start.12 = (bf16[2,2,32,768]{3,2,1,0:T(8,128)(2,1)S(1)}, bf16[2,2,32,768]{3,2,1,0:T(8,128)(2,1)S(1)}, u32[]{:S(2)}, u32[]{:S(2)}) collective-permute-start(bf16[2,2,32,768]{3,2,1,0:T(8,128)(2,1)S(1)} %pad_maximum_fusion.refs_0_), channel_id=1, source_target_pairs={{0,96},{4,100},{8,104},{12,108},{16,112},{20,116},{24,120},{28,124... | collective-permute-start | bytes 589832 | tf_op jit(solution)/shard_map/ppermute | solution.py:265
  20.3 16.8 %collective-permute-start.10 = (bf16[2,2,32,768]{3,2,1,0:T(8,128)(2,1)S(1)}, bf16[2,2,32,768]{3,2,1,0:T(8,128)(2,1)S(1)}, u32[]{:S(2)}, u32[]{:S(2)}) collective-permute-start(bf16[2,2,32,768]{3,2,1,0:T(8,128)(2,1)S(1)} %pad_maximum_fusion.refs_0_), channel_id=1, source_target_pairs={{0,64},{4,68},{8,72},{12,76},{16,80},{20,84},{24,88},{28,92},{32,9... | collective-permute-start | bytes 589832 | tf_op jit(solution)/shard_map/ppermute | solution.py:265
  20.8 16.3 %collective-permute-start.5 = (bf16[2,2,32,768]{3,2,1,0:T(8,128)(2,1)S(1)}, bf16[2,2,32,768]{3,2,1,0:T(8,128)(2,1)S(1)}, u32[]{:S(2)}, u32[]{:S(2)}) collective-permute-start(bf16[2,2,32,768]{3,2,1,0:T(8,128)(2,1)S(1)} %pad_maximum_fusion.refs_0_), channel_id=1, source_target_pairs={{0,32},{4,36},{8,40},{12,44},{16,48},{20,52},{24,56},{28,60},{32,6... | collective-permute-start | bytes 589832 | tf_op jit(solution)/shard_map/ppermute | solution.py:265
  21.5 4.0 %copy-start.11 = (bf16[144,768]{1,0:T(8,128)(2,1)}, bf16[144,768]{1,0:T(8,128)(2,1)S(1)}, u32[]{:S(2)}) copy-start(bf16[144,768]{1,0:T(8,128)(2,1)S(1)} %collective-permute-done.6.p1) | copy-start | bytes 663556
  21.5 16.4 %collective-permute-start.4 = (bf16[2,2,32,768]{3,2,1,0:T(8,128)(2,1)S(1)}, bf16[2,2,32,768]{3,2,1,0:T(8,128)(2,1)S(1)}, u32[]{:S(2)}, u32[]{:S(2)}) collective-permute-start(bf16[2,2,32,768]{3,2,1,0:T(8,128)(2,1)S(1)} %pad_maximum_fusion.refs_0_), channel_id=1, source_target_pairs={{0,1},{1,0},{2,3},{3,2},{4,5},{5,4},{6,7},{7,6},{8,9},{9,8},{10,11... | collective-permute-start | bytes 589832 | tf_op jit(solution)/shard_map/ppermute | solution.py:265
  25.4 0.7 copy-start.12
  26.1 13.8 %copy-start.1 = (f32[48,768]{1,0:T(8,128)S(1)}, f32[48,768]{1,0:T(8,128)}, u32[]{:S(2)}) copy-start(f32[48,768]{1,0:T(8,128)} %constant.54.clone.refs_13_) | copy-start | bytes 442372
  26.1 13.8 %copy-start.2 = (f32[48,768]{1,0:T(8,128)S(1)}, f32[48,768]{1,0:T(8,128)}, u32[]{:S(2)}) copy-start(f32[48,768]{1,0:T(8,128)} %constant.53.clone.refs_12_) | copy-start | bytes 442372
  26.1 13.8 %copy-start.3 = (f32[192,128]{1,0:T(8,128)S(1)}, f32[192,128]{1,0:T(8,128)}, u32[]{:S(2)}) copy-start(f32[192,128]{1,0:T(8,128)} %constant.58.clone.refs_17_) | copy-start | bytes 294916
  26.1 13.8 %copy-start.4 = (f32[192,128]{1,0:T(8,128)S(1)}, f32[192,128]{1,0:T(8,128)}, u32[]{:S(2)}) copy-start(f32[192,128]{1,0:T(8,128)} %constant.57.clone.refs_16_) | copy-start | bytes 294916
  26.1 13.8 %copy-start.5 = (f32[2,64,128]{2,1,0:T(8,128)S(1)}, f32[2,64,128]{2,1,0:T(8,128)}, u32[]{:S(2)}) copy-start(f32[2,64,128]{2,1,0:T(8,128)} %constant.59.clone.refs_18_) | copy-start | bytes 196612
  26.2 13.8 %copy-start.6 = (s32[64]{0:T(128)S(1)}, s32[64]{0:T(128)}, u32[]{:S(2)}) copy-start(s32[64]{0:T(128)} %span_ref.1) | copy-start | bytes 772
  37.1 1.5 collective-permute-start.9
  37.3 1.7 collective-permute-start.11
  37.7 1.5 collective-permute-start.13
  39.2 0.7 copy-start.13
  149.2 17.7 %copy-start.8 = (bf16[384,768]{1,0:T(8,128)(2,1)S(1)}, bf16[384,768]{1,0:T(8,128)(2,1)}, u32[]{:S(2)}) copy-start(bf16[384,768]{1,0:T(8,128)(2,1)} %get-tuple-element.24) | copy-start | bytes 1769476
  149.2 17.7 %copy-start.9 = (bf16[384,768]{1,0:T(8,128)(2,1)S(1)}, bf16[384,768]{1,0:T(8,128)(2,1)}, u32[]{:S(2)}) copy-start(bf16[384,768]{1,0:T(8,128)(2,1)} %get-tuple-element.30) | copy-start | bytes 1769476
  149.2 1.9 %collective-permute-start.15 = (bf16[192,768]{1,0:T(8,128)(2,1)}, bf16[192,768]{1,0:T(8,128)(2,1)S(1)}, u32[]{:S(2)}, u32[]{:S(2)}) collective-permute-start(bf16[192,768]{1,0:T(8,128)(2,1)} %get-tuple-element.27), channel_id=1, source_target_pairs={{0,1},{1,0},{2,3},{3,2},{4,5},{5,4},{6,7},{7,6},{8,9},{9,8},{10,11... | collective-permute-start | bytes 884744 | tf_op jit(solution)/shard_map/ppermute | solution.py:265
  149.5 2.8 %collective-permute-start.17 = (bf16[192,768]{1,0:T(8,128)(2,1)}, bf16[192,768]{1,0:T(8,128)(2,1)S(1)}, u32[]{:S(2)}, u32[]{:S(2)}) collective-permute-start(bf16[192,768]{1,0:T(8,128)(2,1)} %get-tuple-element.29), channel_id=1, source_target_pairs={{0,1},{1,0},{2,3},{3,2},{4,5},{5,4},{6,7},{7,6},{8,9},{9,8},{10,11... | collective-permute-start | bytes 884744 | tf_op jit(solution)/shard_map/ppermute | solution.py:265
  149.8 5.0 %collective-permute-start.14 = (bf16[384,768]{1,0:T(8,128)(2,1)}, bf16[384,768]{1,0:T(8,128)(2,1)S(1)}, u32[]{:S(2)}, u32[]{:S(2)}) collective-permute-start(bf16[384,768]{1,0:T(8,128)(2,1)} %get-tuple-element.25), channel_id=1, source_target_pairs={{0,1},{1,0},{2,3},{3,2},{4,5},{5,4},{6,7},{7,6},{8,9},{9,8},{10,11... | collective-permute-start | bytes 1769480 | tf_op jit(solution)/shard_map/ppermute | solution.py:265
  152.1 8.4 %collective-permute-start.16 = (bf16[192,768]{1,0:T(8,128)(2,1)S(1)}, bf16[192,768]{1,0:T(8,128)(2,1)S(1)}, u32[]{:S(2)}, u32[]{:S(2)}) collective-permute-start(bf16[192,768]{1,0:T(8,128)(2,1)S(1)} %add_convert_fusion.3), channel_id=1, source_target_pairs={{0,2},{1,3},{2,0},{3,1},{4,6},{5,7},{6,4},{7,5},{8,10},{9,11},{10,... | collective-permute-start | bytes 884744 | tf_op jit(solution)/shard_map/ppermute | solution.py:265
  153.4 13.5 %collective-permute-start.18 = (bf16[192,768]{1,0:T(8,128)(2,1)S(1)}, bf16[192,768]{1,0:T(8,128)(2,1)S(1)}, u32[]{:S(2)}, u32[]{:S(2)}) collective-permute-start(bf16[192,768]{1,0:T(8,128)(2,1)S(1)} %add_convert_fusion.2), channel_id=1, source_target_pairs={{0,2},{1,3},{2,0},{3,1},{4,6},{5,7},{6,4},{7,5},{8,10},{9,11},{10,... | collective-permute-start | bytes 884744 | tf_op jit(solution)/shard_map/ppermute | solution.py:265
